TPU v7x, 32 devices: a whole 2x2x4 slice. The times are simulated.
32 devices in a mesh: clip: 8 (over z, x), row: 4 (over y, core).
Axes of the slice: x: 2, y: 2, z: 4, core: 2. Of those that a mesh axis runs over, the one named last changes fastest.
Arguments:
- latents: float32 [8, 8, 16, 256], P('clip', None, 'row'), may hold values from -6 to 6
- noise: float32 [8, 8, 16, 256], P('clip', None, 'row'), may hold values from -6 to 6
- levels: int32 [8, 8], P('clip'), may hold values from 0 to 999
- clip_ids: int32 [8, 8], P('clip'), may hold values from 0 to 1, as said below
- clip_lens: int32 [8, 2], P('clip'), may hold values from 0 to 8, as said below
- embed_w: float32 [16, 1024], P(None, ('clip', 'row')), may hold values from -1.5 to 1.5
- table_w: float32 [1000, 1024], P(None, ('clip', 'row')), may hold values from -6 to 6
- adaln_w: float32 [1024, 8192], P(('clip', 'row')), may hold values from -0.1875 to 0.1875
- qkv_w: float32 [1024, 3072], P(('clip', 'row')), may hold values from -0.1875 to 0.1875
- proj_w: float32 [1024, 1024], P(('clip', 'row')), may hold values from -0.75 to 0.75
- up_w: float32 [1024, 4096], P(('clip', 'row')), may hold values from -0.1875 to 0.1875
- down_w: float32 [4096, 1024], P(('clip', 'row')), may hold values from -0.09375 to 0.09375
- head_w: float32 [1024, 16], P(('clip', 'row')), may hold values from -0.1875 to 0.1875
- embed_avg: float32 [16, 1024], P(None, ('clip', 'row')), may hold values from -0.00012207031 to 0.00012207031
- table_avg: float32 [1000, 1024], P(None, ('clip', 'row')), may hold values from -0.00012207031 to 0.00012207031
- adaln_avg: float32 [1024, 8192], P(('clip', 'row')), may hold values from -0.00012207031 to 0.00012207031
- qkv_avg: float32 [1024, 3072], P(('clip', 'row')), may hold values from -0.00012207031 to 0.00012207031
- proj_avg: float32 [1024, 1024], P(('clip', 'row')), may hold values from -0.00012207031 to 0.00012207031
- up_avg: float32 [1024, 4096], P(('clip', 'row')), may hold values from -0.00012207031 to 0.00012207031
- down_avg: float32 [4096, 1024], P(('clip', 'row')), may hold values from -0.00012207031 to 0.00012207031
- head_avg: float32 [1024, 16], P(('clip', 'row')), may hold values from -0.0024414062 to 0.0024414062
- embed_sq: float32 [16, 1024], P(None, ('clip', 'row')), may hold values from 5.5234377e-06 to 2.2109374e-05
- table_sq: float32 [1000, 1024], P(None, ('clip', 'row')), may hold values from 1.75e-06 to 6.984375e-06
- adaln_sq: float32 [1024, 8192], P(('clip', 'row')), may hold values from 1.75e-06 to 6.984375e-06
- qkv_sq: float32 [1024, 3072], P(('clip', 'row')), may hold values from 1.75e-06 to 6.984375e-06
- proj_sq: float32 [1024, 1024], P(('clip', 'row')), may hold values from 1.75e-06 to 6.984375e-06
- up_sq: float32 [1024, 4096], P(('clip', 'row')), may hold values from 1.75e-06 to 6.984375e-06
- down_sq: float32 [4096, 1024], P(('clip', 'row')), may hold values from 1.75e-06 to 6.984375e-06
- head_sq: float32 [1024, 16], P(('clip', 'row')), may hold values from 3.4921875e-05 to 0.00013984375
Outputs:
- embed_new: float32 [16, 1024], P(None, ('clip', 'row'))
- table_new: float32 [1000, 1024], P(None, ('clip', 'row'))
- adaln_new: float32 [1024, 8192], P(('clip', 'row'))
- qkv_new: float32 [1024, 3072], P(('clip', 'row'))
- proj_new: float32 [1024, 1024], P(('clip', 'row'))
- up_new: float32 [1024, 4096], P(('clip', 'row'))
- down_new: float32 [4096, 1024], P(('clip', 'row'))
- head_new: float32 [1024, 16], P(('clip', 'row'))
- embed_mom: float32 [2, 16, 1024], P(None, None, ('clip', 'row'))
- table_mom: float32 [2, 1000, 1024], P(None, None, ('clip', 'row'))
- adaln_mom: float32 [2, 1024, 8192], P(None, ('clip', 'row'))
- qkv_mom: float32 [2, 1024, 3072], P(None, ('clip', 'row'))
- proj_mom: float32 [2, 1024, 1024], P(None, ('clip', 'row'))
- up_mom: float32 [2, 1024, 4096], P(None, ('clip', 'row'))
- down_mom: float32 [2, 4096, 1024], P(None, ('clip', 'row'))
- head_mom: float32 [2, 1024, 16], P(None, ('clip', 'row'))
- norms: float32 [8, 2], replicated
- loss: float32 [1], replicated
Inputs may be any that keep to these rules, and one draw needn't show every extreme that they name: In each group the frames of a clip slot are consecutive and clip_ids never falls: either every frame has id 0 (one clip of 8 frames) or frame f has id f // 4. Some group is of each kind in every draw. A group of one clip has clip_lens [8, 0, ...]; in the other groups every slot has 1 to 4 true frames, its first frames.
All inputs are finite; a program needn't handle non-finite values.
Results may differ from a plain program's by a relative error of at most 0.015.
The roundings to bfloat16 on the way count: a program that leaves them out, or rounds other values in their place, can miss the bound.
Values may be sent and summed in bfloat16 or wider, within the bound.
No kernel may reach another device: no remote copies, remote signals or barrier semaphores. Data moves between devices by JAX's collectives and lax.ppermute only.
A program may use at most 256 MiB of HBM per device.

v0:
```python
import math

import jax
import jax.numpy as jnp
from jax import lax
from jax.sharding import PartitionSpec as P

D = 1024
HEADS = 16
HD = 64
PD = 16
GRID = 16
LEVELS = 1000
STEP = 7
FRAMES = 8
CLIPS = 2


precise = lax.Precision.HIGHEST
beta_one = 0.9
beta_two = 0.999
adam_eps = 1e-08
weight_decay = 0.01
learn_rate = 1.0
norm_eps = 1e-06


def to_low(values):
    return values.astype(jnp.bfloat16)


def dot_low(formula, left, right):
    return jnp.einsum(formula, left, right, preferred_element_type=jnp.float32)


def layer_norm(values):
    center = values - jnp.mean(values, axis=-1, keepdims=True)
    spread = jnp.mean(center * center, axis=-1, keepdims=True)
    return center * lax.rsqrt(spread + norm_eps)


def norm_back(values, grad_out):
    normed, pullback = jax.vjp(layer_norm, values)
    return pullback(grad_out)[0]


def modulate(normed, shift, scale):
    return normed * (1.0 + scale[:, None, :]) + shift[:, None, :]


def gelu_tanh(values):
    return jax.nn.gelu(values, approximate=True)


def frame_layout(clip_row, length_row):
    frame_idx = jnp.arange(FRAMES, dtype=jnp.int32)
    same_clip = clip_row[:, None] == clip_row[None, :]
    starts = jnp.min(jnp.where(same_clip, frame_idx[None, :], FRAMES), axis=1)
    frame_pos = frame_idx - starts
    slot_idx = jnp.arange(CLIPS, dtype=jnp.int32)
    length = jnp.sum(
        jnp.where(clip_row[:, None] == slot_idx[None, :], length_row[None, :], 0), axis=1
    )
    is_true = frame_pos < length
    allowed = same_clip & (frame_idx[None, :] <= frame_idx[:, None]) & is_true[None, :]
    return (frame_pos, is_true, allowed)


def noise_mix(level_row):
    angle = (level_row.astype(jnp.float32) + 0.5) * (math.pi / (2 * LEVELS))
    return (jnp.cos(angle), jnp.sin(angle))


def rotary_angles(along_t, along_r, along_c):
    pieces = []
    for posit_val, width in ((along_t, HD // 4), (along_r, 3 * HD // 8), (along_c, 3 * HD // 8)):
        half_width = width // 2
        frequency = 10000.0 ** (-jnp.arange(half_width, dtype=jnp.float32) / half_width)
        pieces.append(posit_val.astype(jnp.float32)[:, None] * frequency[None, :])
    return jnp.concatenate(pieces, axis=1)


def token_angles(frame_pos, row_pos):
    grid_shape = (FRAMES, row_pos.shape[0], GRID)
    along_t = jnp.broadcast_to(frame_pos[:, None, None], grid_shape).reshape(-1)
    along_r = jnp.broadcast_to(row_pos[:, None][None, :, :], grid_shape).reshape(-1)
    along_c = jnp.broadcast_to(
        jnp.arange(GRID, dtype=jnp.int32)[None, None, :], grid_shape
    ).reshape(-1)
    return rotary_angles(along_t, along_r, along_c)


def rotate(values, angle):
    cosine = jnp.cos(angle)[:, None, :]
    sine_val = jnp.sin(angle)[:, None, :]
    pieces = []
    offset = 0
    for width in (HD // 4, 3 * HD // 8, 3 * HD // 8):
        half_width = width // 2
        lower_h = values[..., offset : offset + half_width]
        upper_h = values[..., offset + half_width : offset + width]
        angle_lo = offset // 2
        cos_part = cosine[..., angle_lo : angle_lo + half_width]
        sin_part = sine_val[..., angle_lo : angle_lo + half_width]
        pieces.append(lower_h * cos_part - upper_h * sin_part)
        pieces.append(upper_h * cos_part + lower_h * sin_part)
        offset += width
    return jnp.concatenate(pieces, axis=-1)


def to_heads(values):
    return values.reshape(-1, HEADS, HD).transpose(1, 0, 2)


def from_heads(values):
    return values.transpose(1, 0, 2).reshape(-1, D)


def head_forward(queries, keys_all, values_all, mask, scale):
    scores = jnp.where(mask, dot_low("qd,kd->qk", queries, keys_all) * scale, -1e30)
    top = jnp.max(scores, axis=1, keepdims=True)
    log_sum = top + jnp.log(jnp.sum(jnp.exp(scores - top), axis=1, keepdims=True))
    weights_p = to_low(jnp.exp(scores - log_sum))
    return (dot_low("qk,kd->qd", weights_p, values_all), log_sum[:, 0])


def head_backward(queries, keys_all, values_all, grad_out, log_sum, mask, scale):
    scores = jnp.where(mask, dot_low("qd,kd->qk", queries, keys_all) * scale, -1e30)
    weights_p = jnp.exp(scores - log_sum[:, None])
    grad_w = dot_low("qd,kd->qk", grad_out, values_all)
    inner = jnp.sum(weights_p * grad_w, axis=1, keepdims=True)
    grad_s = to_low(scale * weights_p * (grad_w - inner))
    return (
        dot_low("qk,kd->qd", grad_s, keys_all),
        dot_low("qk,qd->kd", grad_s, queries),
        dot_low("qk,qd->kd", to_low(weights_p), grad_out),
    )


def lamb_direction(weight, gradient, first_m, second_m, fix_one, fix_two):
    first_n = beta_one * first_m + (1.0 - beta_one) * gradient
    second_n = jnp.sqrt(beta_two * second_m * second_m + (1.0 - beta_two) * gradient * gradient)
    update = first_n / fix_one / (second_n / math.sqrt(fix_two) + adam_eps) + weight_decay * weight
    return (first_n, second_n, update)


def body(
    latents,
    noise,
    levels,
    clip_ids,
    clip_lens,
    embed_w,
    table_w,
    adaln_w,
    qkv_w,
    proj_w,
    up_w,
    down_w,
    head_w,
    embed_avg,
    table_avg,
    adaln_avg,
    qkv_avg,
    proj_avg,
    up_avg,
    down_avg,
    head_avg,
    embed_sq,
    table_sq,
    adaln_sq,
    qkv_sq,
    proj_sq,
    up_sq,
    down_sq,
    head_sq,
):
    masters = (embed_w, table_w, adaln_w, qkv_w, proj_w, up_w, down_w, head_w)
    firsts = (embed_avg, table_avg, adaln_avg, qkv_avg, proj_avg, up_avg, down_avg, head_avg)
    seconds = (embed_sq, table_sq, adaln_sq, qkv_sq, proj_sq, up_sq, down_sq, head_sq)
    gathered = (
        lax.all_gather(to_low(embed_w), ("clip", "row"), axis=1, tiled=True),
        lax.all_gather(to_low(table_w), ("clip", "row"), axis=1, tiled=True),
        lax.all_gather(to_low(adaln_w), ("clip", "row"), axis=0, tiled=True),
        lax.all_gather(to_low(qkv_w), ("clip", "row"), axis=0, tiled=True),
        lax.all_gather(to_low(proj_w), ("clip", "row"), axis=0, tiled=True),
        lax.all_gather(to_low(up_w), ("clip", "row"), axis=0, tiled=True),
        lax.all_gather(to_low(down_w), ("clip", "row"), axis=0, tiled=True),
        lax.all_gather(to_low(head_w), ("clip", "row"), axis=0, tiled=True),
    )
    embed_b, table_b, adaln_b, qkv_b, proj_b, up_b, down_b, head_b = gathered
    row_count = lax.axis_size("row")
    row_index = lax.axis_index("row")
    row_local = GRID // row_count
    per_frame = row_local * GRID
    count_tok = FRAMES * per_frame
    keys_frame = GRID * GRID
    level_row = levels[0]
    frame_pos, is_true, allowed = frame_layout(clip_ids[0], clip_lens[0])
    true_frames = lax.psum(jnp.sum(is_true.astype(jnp.float32)), "clip")
    count = true_frames * (GRID * GRID)
    alpha, sigma = noise_mix(level_row)
    clean = latents[0].reshape(FRAMES, per_frame, PD)
    fresh = noise[0].reshape(FRAMES, per_frame, PD)
    noisy = alpha[:, None, None] * clean + sigma[:, None, None] * fresh
    target = alpha[:, None, None] * fresh - sigma[:, None, None] * clean
    noisy_b = to_low(noisy.reshape(count_tok, PD))
    one_hot = (level_row[:, None] == jnp.arange(LEVELS, dtype=jnp.int32)[None, :]).astype(
        jnp.float32
    )
    cond = dot_low("fl,ld->fd", to_low(one_hot), table_b)
    cond_act = to_low(jax.nn.silu(cond))
    modul = dot_low("fd,dm->fm", cond_act, adaln_b)
    shift_a, scale_a, gate_a, shift_m, scale_m, gate_m, shift_f, scale_f = jnp.split(
        modul, 8, axis=1
    )
    row_pos = row_index * row_local + jnp.arange(row_local, dtype=jnp.int32)
    angle = token_angles(frame_pos, row_pos)
    mask = jnp.broadcast_to(
        allowed[:, None, :, None], (FRAMES, per_frame, FRAMES, keys_frame)
    ).reshape(count_tok, FRAMES * keys_frame)
    scale = HD ** (-0.5)
    hidden0 = dot_low("tc,cd->td", noisy_b, embed_b).reshape(FRAMES, per_frame, D)
    normed_a = layer_norm(hidden0)
    attn_in = to_low(modulate(normed_a, shift_a, scale_a)).reshape(count_tok, D)
    qkv = dot_low("td,de->te", attn_in, qkv_b)
    queries = to_low(rotate(qkv[:, :D].reshape(count_tok, HEADS, HD), angle))
    keys_loc = to_low(rotate(qkv[:, D : 2 * D].reshape(count_tok, HEADS, HD), angle))
    values_loc = to_low(qkv[:, 2 * D :])
    kv_shape = (FRAMES, row_local, GRID, D)
    keys_all, values_all = (
        lax.all_gather(keys_loc.reshape(kv_shape), "row", axis=1, tiled=True),
        lax.all_gather(values_loc.reshape(kv_shape), "row", axis=1, tiled=True),
    )

    def attend(items):
        return head_forward(items[0], items[1], items[2], mask, scale)

    heads_out, log_sum = lax.map(
        attend, (to_heads(queries), to_heads(keys_all), to_heads(values_all))
    )
    attn_b = to_low(from_heads(heads_out))
    proj_out = dot_low("td,de->te", attn_b, proj_b).reshape(FRAMES, per_frame, D)
    hidden1 = hidden0 + gate_a[:, None, :] * proj_out
    normed_m = layer_norm(hidden1)
    mlp_in = to_low(modulate(normed_m, shift_m, scale_m)).reshape(count_tok, D)
    up_out = dot_low("td,df->tf", mlp_in, up_b)
    act_b = to_low(gelu_tanh(up_out))
    down_out = dot_low("tf,fd->td", act_b, down_b).reshape(FRAMES, per_frame, D)
    hidden2 = hidden1 + gate_m[:, None, :] * down_out
    normed_f = layer_norm(hidden2)
    final_in = to_low(modulate(normed_f, shift_f, scale_f)).reshape(count_tok, D)
    pred = dot_low("td,dc->tc", final_in, head_b)
    token_true = (
        jnp.broadcast_to(is_true[:, None], (FRAMES, per_frame))
        .reshape(count_tok, 1)
        .astype(jnp.float32)
    )
    error = (pred - target.reshape(count_tok, PD)) * token_true
    loss_local = jnp.sum(error * error)
    grad_pred = to_low(2.0 * error / (PD * count))
    grad_head = dot_low("td,tc->dc", final_in, grad_pred)
    grad_fin = dot_low("tc,dc->td", grad_pred, head_b).reshape(FRAMES, per_frame, D)
    grad_shift_f = jnp.sum(grad_fin, axis=1)
    grad_scale_f = jnp.sum(grad_fin * normed_f, axis=1)
    grad_h2 = norm_back(hidden2, grad_fin * (1.0 + scale_f[:, None, :]))
    grad_gate_m = jnp.sum(grad_h2 * down_out, axis=1)
    grad_down_out = to_low(grad_h2 * gate_m[:, None, :]).reshape(count_tok, D)
    grad_down = dot_low("tf,td->fd", act_b, grad_down_out)
    grad_act = dot_low("td,fd->tf", grad_down_out, down_b)
    unused_act, gelu_pull = jax.vjp(gelu_tanh, up_out)
    grad_up_out = to_low(gelu_pull(grad_act)[0])
    grad_up = dot_low("td,tf->df", mlp_in, grad_up_out)
    grad_mlp = dot_low("tf,df->td", grad_up_out, up_b).reshape(FRAMES, per_frame, D)
    grad_shift_m = jnp.sum(grad_mlp, axis=1)
    grad_scale_m = jnp.sum(grad_mlp * normed_m, axis=1)
    grad_h1 = grad_h2 + norm_back(hidden1, grad_mlp * (1.0 + scale_m[:, None, :]))
    grad_gate_a = jnp.sum(grad_h1 * proj_out, axis=1)
    grad_proj_out = to_low(grad_h1 * gate_a[:, None, :]).reshape(count_tok, D)
    grad_proj = dot_low("td,te->de", attn_b, grad_proj_out)
    grad_attn = to_low(dot_low("te,de->td", grad_proj_out, proj_b))
    keys_use, values_use = (
        lax.all_gather(keys_loc.reshape(kv_shape), "row", axis=1, tiled=True),
        lax.all_gather(values_loc.reshape(kv_shape), "row", axis=1, tiled=True),
    )

    def attend_back(items):
        return head_backward(items[0], items[1], items[2], items[3], items[4], mask, scale)

    grad_q, grad_k, grad_v = lax.map(
        attend_back,
        (to_heads(queries), to_heads(keys_use), to_heads(values_use), to_heads(grad_attn), log_sum),
    )
    full_shape = (FRAMES, GRID, GRID, D)
    grad_k_loc, grad_v_loc = (
        lax.psum_scatter(
            from_heads(grad_k).reshape(full_shape).astype(jnp.bfloat16),
            "row",
            scatter_dimension=1,
            tiled=True,
        ).astype(jnp.float32),
        lax.psum_scatter(
            from_heads(grad_v).reshape(full_shape).astype(jnp.bfloat16),
            "row",
            scatter_dimension=1,
            tiled=True,
        ).astype(jnp.float32),
    )
    grad_q_pre = rotate(grad_q.transpose(1, 0, 2), -angle).reshape(count_tok, D)
    grad_k_pre = rotate(grad_k_loc.reshape(count_tok, HEADS, HD), -angle).reshape(count_tok, D)
    grad_qkv = to_low(
        jnp.concatenate([grad_q_pre, grad_k_pre, grad_v_loc.reshape(count_tok, D)], axis=1)
    )
    grad_qkv_w = dot_low("td,te->de", attn_in, grad_qkv)
    grad_in = dot_low("te,de->td", grad_qkv, qkv_b).reshape(FRAMES, per_frame, D)
    grad_shift_a = jnp.sum(grad_in, axis=1)
    grad_scale_a = jnp.sum(grad_in * normed_a, axis=1)
    grad_h0 = grad_h1 + norm_back(hidden0, grad_in * (1.0 + scale_a[:, None, :]))
    grad_embed = dot_low("tc,td->cd", noisy_b, to_low(grad_h0.reshape(count_tok, D)))
    grad_mod = lax.psum(
        jnp.concatenate(
            [
                grad_shift_a,
                grad_scale_a,
                grad_gate_a,
                grad_shift_m,
                grad_scale_m,
                grad_gate_m,
                grad_shift_f,
                grad_scale_f,
            ],
            axis=1,
        ).astype(jnp.bfloat16),
        "row",
    ).astype(jnp.float32)
    grad_mod_b = to_low(grad_mod)
    grad_cond_act = dot_low("fm,dm->fd", grad_mod_b, adaln_b)
    unused_silu, silu_pull = jax.vjp(jax.nn.silu, cond)
    grad_cond = silu_pull(grad_cond_act)[0]
    chosen = (jnp.arange(FRAMES, dtype=jnp.int32) % row_count == row_index).astype(jnp.float32)[
        :, None
    ]
    grad_table = jnp.einsum(
        "fl,fd->ld",
        one_hot,
        grad_cond * chosen,
        precision=precise,
        preferred_element_type=jnp.float32,
    )
    grad_adaln = dot_low("fd,fm->dm", cond_act * to_low(chosen), grad_mod_b)
    reduced = (
        lax.psum_scatter(grad_embed, ("clip", "row"), scatter_dimension=1, tiled=True),
        lax.psum_scatter(grad_table, ("clip", "row"), scatter_dimension=1, tiled=True),
        lax.psum_scatter(grad_adaln, ("clip", "row"), scatter_dimension=0, tiled=True),
        lax.psum_scatter(grad_qkv_w, ("clip", "row"), scatter_dimension=0, tiled=True),
        lax.psum_scatter(grad_proj, ("clip", "row"), scatter_dimension=0, tiled=True),
        lax.psum_scatter(grad_up, ("clip", "row"), scatter_dimension=0, tiled=True),
        lax.psum_scatter(grad_down, ("clip", "row"), scatter_dimension=0, tiled=True),
        lax.psum_scatter(grad_head, ("clip", "row"), scatter_dimension=0, tiled=True),
    )
    fix_one = 1.0 - beta_one**STEP
    fix_two = 1.0 - beta_two**STEP
    moms, updates, squares_w, squares_u = ([], [], [], [])
    for weight, gradient, first_m, second_m in zip(masters, reduced, firsts, seconds):
        first_n, second_n, update = lamb_direction(
            weight, gradient, first_m, second_m, fix_one, fix_two
        )
        moms.append(jnp.stack([first_n, second_n]))
        updates.append(update)
        squares_w.append(jnp.sum(weight * weight))
        squares_u.append(jnp.sum(update * update))
    sums_w, sums_u, loss_sum = lax.psum(
        (jnp.stack(squares_w), jnp.stack(squares_u), loss_local), ("clip", "row")
    )
    weight_norm = jnp.sqrt(sums_w)
    update_norm = jnp.sqrt(sums_u)
    trust = weight_norm / update_norm
    news = [
        weight - learn_rate * trust[number] * update
        for number, (weight, update) in enumerate(zip(masters, updates))
    ]
    return (
        news[0],
        news[1],
        news[2],
        news[3],
        news[4],
        news[5],
        news[6],
        news[7],
        moms[0],
        moms[1],
        moms[2],
        moms[3],
        moms[4],
        moms[5],
        moms[6],
        moms[7],
        jnp.stack([weight_norm, update_norm], axis=1),
        (loss_sum / (PD * count)).reshape(1),
    )


def solution(mesh):
    return jax.shard_map(
        body,
        mesh=mesh,
        in_specs=(
            P("clip", None, "row", None),
            P("clip", None, "row", None),
            P("clip", None),
            P("clip", None),
            P("clip", None),
            P(None, ("clip", "row")),
            P(None, ("clip", "row")),
            P(("clip", "row"), None),
            P(("clip", "row"), None),
            P(("clip", "row"), None),
            P(("clip", "row"), None),
            P(("clip", "row"), None),
            P(("clip", "row"), None),
            P(None, ("clip", "row")),
            P(None, ("clip", "row")),
            P(("clip", "row"), None),
            P(("clip", "row"), None),
            P(("clip", "row"), None),
            P(("clip", "row"), None),
            P(("clip", "row"), None),
            P(("clip", "row"), None),
            P(None, ("clip", "row")),
            P(None, ("clip", "row")),
            P(("clip", "row"), None),
            P(("clip", "row"), None),
            P(("clip", "row"), None),
            P(("clip", "row"), None),
            P(("clip", "row"), None),
            P(("clip", "row"), None),
        ),
        out_specs=(
            P(None, ("clip", "row")),
            P(None, ("clip", "row")),
            P(("clip", "row"), None),
            P(("clip", "row"), None),
            P(("clip", "row"), None),
            P(("clip", "row"), None),
            P(("clip", "row"), None),
            P(("clip", "row"), None),
            P(None, None, ("clip", "row")),
            P(None, None, ("clip", "row")),
            P(None, ("clip", "row"), None),
            P(None, ("clip", "row"), None),
            P(None, ("clip", "row"), None),
            P(None, ("clip", "row"), None),
            P(None, ("clip", "row"), None),
            P(None, ("clip", "row"), None),
            P(),
            P(),
        ),
        check_vma=False,
    )
```

profile of v0, /device:TPU:0, one launch (start us, length us, event | category | flops | bytes accessed | tf_op | source)
XLA Modules:
  0.0 2666.1 jit_solution(12742859223852767222)
XLA Ops:
  11.9 43.6 %all-gather = bf16[32,32,16]{1,2,0:T(8,128)(2,1)S(1)} all-gather(bf16[1,32,16]{1,2,0:T(8,128)(2,1)S(1)} %convert_bitcast_fusion.3), channel_id=1, replica_groups=mesh['clip'=8,'row'=4] {'clip','row'}, dimensions={0}, use_global_device_ids=true | all-gather | bytes 33792 | tf_op jit(solution)/shard_map/all_gather | solution.py:182
  73.0 115.0 %all-gather.13.cloned.1.call-done = bf16[1024,8192]{1,0:T(8,128)(2,1)} async-done(((bf16[32,8192]{1,0:T(8,128)(2,1)}), bf16[1024,8192]{1,0:T(8,128)(2,1)}) %all-gather.13.cloned.1.call-update) | async-done | bytes 16777232 | tf_op jit(solution)/shard_map/all_gather | solution.py:184
  197.7 61.5 %all-gather.15.cloned.1.call-done = bf16[1024,3072]{1,0:T(8,128)(2,1)} async-done(((bf16[32,3072]{1,0:T(8,128)(2,1)}), bf16[1024,3072]{1,0:T(8,128)(2,1)}) %all-gather.15.cloned.1.call-update) | async-done | bytes 6291472 | tf_op jit(solution)/shard_map/all_gather | solution.py:185
  306.6 40.0 %all-gather.1 = bf16[32,32,16]{1,2,0:T(8,128)(2,1)S(1)} all-gather(bf16[1,32,16]{1,2,0:T(8,128)(2,1)S(1)} %convert_bitcast_fusion.2), channel_id=1, replica_groups=mesh['clip'=8,'row'=4] {'clip','row'}, dimensions={0}, use_global_device_ids=true | all-gather | bytes 33792 | tf_op jit(solution)/shard_map/all_gather | solution.py:189
  351.3 17.7 psum.36
  372.6 14.0 concatenate.62
  430.3 113.3 %while.30 = (s32[]{:T(128)}, bf16[16,512,64]{1,2,0:T(8,128)(2,1)S(1)}, f32[16,512]{1,0:T(8,128)}, bf16[16,512,64]{2,1,0:T(8,128)(2,1)}, bf16[16,2048,64]{2,1,0:T...) while((s32[]{:T(128)}, ...), condition=%wide.region_16.17_spmd.clone.clone, body=%wide.region_13.16_spmd.clone.sunk.clone | while | flops 275774976 | bytes 18108560 | solution.py:239
  564.3 19.2 all-gather.25.cloned.1.call-done
  636.7 191.7 %while.31 = (s32[]{:T(128)}, f32[16,512,64]{1,2,0:T(8,128)S(1)}, bf16[16,2048,64]{1,2,0:T(8,128)(2,1)}, bf16[16,2048,64]{1,2,0:T(8,128)(2,1)}, bf16[16,512,64]{2...) while((s32[]{:T(128)}, f32[16,512,64]{1,2,0:T(8,128)S(1)}, ...), condition=%wide.region_29.30_spmd.clone.clone, body=%wide.region_27.29_spmd.clone.sunk.clone | while | flops 681573888 | bytes 38812840 | solution.py:290
  878.5 147.9 %all-reduce.9.cloned.1.call-done = (bf16[8,16,16,1024]{3,2,1,0:T(8,128)(2,1)}, bf16[8,16,16,1024]{3,2,1,0:T(8,128)(2,1)}) async-done(((bf16[8,16,16,1024]{3,2,1,0:T(8,128)(2,1)}, bf16[8,16,16,1024]{3,2,1,0:T(8,128)(2,1)}), (bf16[8,16,16,1024]{3,2,1,0:T(8,128)(2,1)}, bf16[8,16,16,1024]{3,2,1,0:T(8,128)(2,1)})) %all-reduce.9.cloned.1.call-update) | async-done | bytes 8388624
  1030.9 14.6 fusion.134
  1078.5 14.1 concatenate.64
  1123.1 22.0 all-reduce.7.cloned.1.call-done
  1170.0 15.0 fusion.127
  1197.5 13.3 fusion.93
  1211.0 71.1 %reduce-scatter.33.cloned.1.call-done = f32[32,16]{1,0:T(8,128)} async-done(((f32[1024,16]{1,0:T(8,128)}), f32[32,16]{1,0:T(8,128)}) %reduce-scatter.33.cloned.1.call-update) | async-done | bytes 2064
  1284.7 129.7 %reduce-scatter.31.cloned.1.call-done = f32[32,16]{1,0:T(8,128)} async-done(((f32[1024,16]{1,0:T(8,128)}), f32[32,16]{1,0:T(8,128)}) %reduce-scatter.31.cloned.1.call-update) | async-done | bytes 2064
  1417.1 136.9 %reduce-scatter.25.cloned.1.call-done = f32[32,1024]{1,0:T(8,128)} async-done(((f32[1024,1024]{1,0:T(8,128)}), f32[32,1024]{1,0:T(8,128)}) %reduce-scatter.25.cloned.1.call-update) | async-done | bytes 131088 | tf_op jit(solution)/shard_map/reduce_scatter | solution.py:356
  1557.0 136.1 %reduce-scatter.19.cloned.1.call-done = f32[1000,32]{0,1:T(8,128)} async-done(((f32[1000,1024]{0,1:T(8,128)}), f32[1000,32]{0,1:T(8,128)}) %reduce-scatter.19.cloned.1.call-update) | async-done | bytes 128016 | tf_op jit(solution)/shard_map/reduce_scatter | solution.py:353
  1696.1 155.5 %reduce-scatter.23.cloned.1.call-done = f32[32,3072]{1,0:T(8,128)} async-done(((f32[1024,3072]{1,0:T(8,128)}), f32[32,3072]{1,0:T(8,128)}) %reduce-scatter.23.cloned.1.call-update) | async-done | bytes 393232 | tf_op jit(solution)/shard_map/reduce_scatter | solution.py:355
  1855.3 180.6 %reduce-scatter.29.cloned.1.call-done = f32[128,1024]{1,0:T(8,128)} async-done(((f32[4096,1024]{1,0:T(8,128)}), f32[128,1024]{1,0:T(8,128)}) %reduce-scatter.29.cloned.1.call-update) | async-done | bytes 524304 | tf_op jit(solution)/shard_map/reduce_scatter | solution.py:358
  2039.9 182.7 %reduce-scatter.27.cloned.1.call-done = f32[32,4096]{1,0:T(8,128)} async-done(((f32[1024,4096]{1,0:T(8,128)}), f32[32,4096]{1,0:T(8,128)}) %reduce-scatter.27.cloned.1.call-update) | async-done | bytes 524304 | tf_op jit(solution)/shard_map/reduce_scatter | solution.py:357
  2226.9 353.6 %reduce-scatter.21.cloned.1.call-done = f32[32,8192]{1,0:T(8,128)} async-done(((f32[1024,8192]{1,0:T(8,128)}), f32[32,8192]{1,0:T(8,128)}) %reduce-scatter.21.cloned.1.call-update) | async-done | bytes 1048592 | tf_op jit(solution)/shard_map/reduce_scatter | solution.py:354
  2596.3 43.2 %all-reduce.2 = (f32[8]{0:T(128)}, f32[8]{0:T(128)}, f32[]{:T(128)}) all-reduce(f32[8]{0:T(128)} %stack.152, f32[8]{0:T(128)} %stack.143, f32[]{:T(128)} %get-tuple-element.408), channel_id=1, replica_groups=mesh['clip'=8,'row'=4] {'clip','row'}, use_global_device_ids=true, to_apply=%region_59.60 | all-reduce | flops 17 | bytes 136 | tf_op jit(solution)/shard_map/psum | solution.py:372
  (724 shorter events, 718.8 us)
Async XLA Ops:
  7.2 63.5 %all-gather.11.cloned.1.call-start = ((), (), s32[]{:S(2)}) async-start(), calls=%async_computation.8 | async-start | bytes 2162688 | tf_op jit(solution)/shard_map/all_gather | solution.py:183
  8.9 179.0 %all-gather.13.cloned.1.call-start = ((), (), s32[]{:S(2)}) async-start(), calls=%async_computation.9 | async-start | bytes 17301504 | tf_op jit(solution)/shard_map/all_gather | solution.py:184
  11.1 248.1 %all-gather.15.cloned.1.call-start = ((), (), s32[]{:S(2)}) async-start(), calls=%async_computation.10 | async-start | bytes 6488064 | tf_op jit(solution)/shard_map/all_gather | solution.py:185
  11.9 377.4 %all-gather.17.cloned.1.call-start = ((), (), s32[]{:S(2)}) async-start(), calls=%async_computation.11 | async-start | bytes 5242880 | tf_op jit(solution)/shard_map/all_gather | solution.py:232
  58.6 487.4 %copy-start.1 = (f32[8,64,1024]{2,1,0:T(8,128)}, f32[8,64,1024]{2,1,0:T(8,128)S(1)}, u32[]{:S(2)}) copy-start(f32[8,64,1024]{2,1,0:T(8,128)S(1)} %get-tuple-element.406) | copy-start | bytes 6291460
  294.0 115.7 %all-gather.19.cloned.1.call-start = ((), (), s32[]{:S(2)}) async-start(), calls=%async_computation.12 | async-start | bytes 5242880 | tf_op jit(solution)/shard_map/all_gather | solution.py:233
  296.9 249.1 %all-gather.21.cloned.1.call-start = ((), (), s32[]{:S(2)}) async-start(), calls=%async_computation.13 | async-start | bytes 2162688 | tf_op jit(solution)/shard_map/all_gather | solution.py:186
  297.6 255.2 %all-gather.23.cloned.1.call-start = ((), (), s32[]{:S(2)}) async-start(), calls=%async_computation.14 | async-start | bytes 8650752 | tf_op jit(solution)/shard_map/all_gather | solution.py:187
  298.4 285.1 %all-gather.25.cloned.1.call-start = ((), (), s32[]{:S(2)}) async-start(), calls=%async_computation.15 | async-start | bytes 8650752 | tf_op jit(solution)/shard_map/all_gather | solution.py:188
  299.3 727.1 %all-reduce.9.cloned.1.call-start = ((), (), s32[]{:S(2)}) async-start(), calls=%async_computation.25 | async-start | bytes 16777216
  874.4 270.6 %all-reduce.7.cloned.1.call-start = ((), (), s32[]{:S(2)}) async-start(), calls=%async_computation.16 | async-start | bytes 262144 | tf_op jit(solution)/shard_map/psum | solution.py:320
  1113.4 168.7 %reduce-scatter.33.cloned.1.call-start = ((), (), s32[]{:S(2)}) async-start(), calls=%async_computation.24 | async-start | bytes 540672
  1114.8 299.6 %reduce-scatter.31.cloned.1.call-start = ((), (), s32[]{:S(2)}) async-start(), calls=%async_computation.23 | async-start | bytes 540672
  1119.2 434.7 %reduce-scatter.25.cloned.1.call-start = ((), (), s32[]{:S(2)}) async-start(), calls=%async_computation.20 | async-start | bytes 4325376 | tf_op jit(solution)/shard_map/reduce_scatter | solution.py:356
  1122.8 570.3 %reduce-scatter.19.cloned.1.call-start = ((), (), s32[]{:S(2)}) async-start(), calls=%async_computation.17 | async-start | bytes 4325376 | tf_op jit(solution)/shard_map/reduce_scatter | solution.py:353
  1159.3 692.4 %reduce-scatter.23.cloned.1.call-start = ((), (), s32[]{:S(2)}) async-start(), calls=%async_computation.19 | async-start | bytes 12976128 | tf_op jit(solution)/shard_map/reduce_scatter | solution.py:355
  1168.8 867.1 %reduce-scatter.29.cloned.1.call-start = ((), (), s32[]{:S(2)}) async-start(), calls=%async_computation.22 | async-start | bytes 17301504 | tf_op jit(solution)/shard_map/reduce_scatter | solution.py:358
  1185.0 1037.6 %reduce-scatter.27.cloned.1.call-start = ((), (), s32[]{:S(2)}) async-start(), calls=%async_computation.21 | async-start | bytes 17301504 | tf_op jit(solution)/shard_map/reduce_scatter | solution.py:357
  1196.7 1383.8 %reduce-scatter.21.cloned.1.call-start = ((), (), s32[]{:S(2)}) async-start(), calls=%async_computation.18 | async-start | bytes 34603008 | tf_op jit(solution)/shard_map/reduce_scatter | solution.py:354
  1210.9 482.2 %copy-start.39 = (f32[1000,32]{0,1:T(8,128)S(1)}, f32[1000,32]{0,1:T(8,128)}, u32[]{:S(2)}) copy-start(f32[1000,32]{0,1:T(8,128)} %param.39) | copy-start | bytes 384004
  1210.9 640.7 %copy-start.28 = (f32[32,3072]{1,0:T(8,128)S(1)}, f32[32,3072]{1,0:T(8,128)}, u32[]{:S(2)}) copy-start(f32[32,3072]{1,0:T(8,128)} %param.41) | copy-start | bytes 1179652
  1211.0 640.7 %copy-start.61 = (f32[32,3072]{1,0:T(8,128)S(1)}, f32[32,3072]{1,0:T(8,128)}, u32[]{:S(2)}) copy-start(f32[32,3072]{1,0:T(8,128)} %param.57) | copy-start | bytes 1179652
  1211.0 640.7 %copy-start.62 = (f32[32,3072]{1,0:T(8,128)S(1)}, f32[32,3072]{1,0:T(8,128)}, u32[]{:S(2)}) copy-start(f32[32,3072]{1,0:T(8,128)} %param.49) | copy-start | bytes 1179652
  2039.9 540.6 %copy-start.14 = (f32[32,8192]{1,0:T(8,128)S(1)}, f32[32,8192]{1,0:T(8,128)}, u32[]{:S(2)}) copy-start(f32[32,8192]{1,0:T(8,128)} %param.40) | copy-start | bytes 3145732
  (116 other events, 5435.4 us)
Sparse Core Ops, SparseCore 0:
  11.5 59.1 all-gather.10
  74.2 113.7 all-gather.12
  191.4 67.7 all-gather.14
  294.1 33.6 all-gather.16
  329.8 34.7 all-gather.18
  367.9 56.2 all-gather.20
  427.7 76.4 all-gather.22
  507.7 75.8 all-gather.24
  874.5 151.8 all-reduce.8
  1113.5 31.4 all-reduce.6
  1147.9 134.0 reduce-scatter.32
  1284.8 129.6 reduce-scatter.30
  1416.8 137.1 reduce-scatter.24
  1556.2 136.8 reduce-scatter.18
  1700.0 151.5 reduce-scatter.22
  1853.8 182.0 reduce-scatter.28
  2038.0 184.5 reduce-scatter.26
  2224.8 355.6 reduce-scatter.20
where the time goes:
time: 2680 us; the launch traced here: 2670 us
  waiting for transfers between devices  1720 us (64%)
  matrix products  356 us (13%)
  local copies, waits for them, and re-layouts  312 us (12%)
  blocking collectives  145 us (5%)
  other arithmetic  109 us (4%)
    reduce_scatter x1, waiting for transfers between devices, body(): lax.psum_scatter(grad_adaln, ('clip', 'row'), scatter_dimension=0, tiled=...  354 us
    dot_general x131, matrix products, dot_low(): return jnp.einsum(formula, left, right, preferred_element_type=jnp.float32)  350 us
    unnamed x21, waiting for transfers between devices  349 us
    reduce_scatter x1, waiting for transfers between devices, body(): lax.psum_scatter(grad_up, ('clip', 'row'), scatter_dimension=0, tiled=True)  183 us
    reduce_scatter x1, waiting for transfers between devices, body(): lax.psum_scatter(grad_down, ('clip', 'row'), scatter_dimension=0, tiled=T...  181 us
    reduce_scatter x1, waiting for transfers between devices, body(): lax.psum_scatter(grad_qkv_w, ('clip', 'row'), scatter_dimension=0, tiled=...  156 us
    reduce_scatter x1, waiting for transfers between devices, body(): lax.psum_scatter(grad_proj, ('clip', 'row'), scatter_dimension=0, tiled=T...  137 us
    reduce_scatter x1, waiting for transfers between devices, body(): lax.psum_scatter(grad_table, ('clip', 'row'), scatter_dimension=1, tiled=...  136 us
  transfers between devices with their start and end apart: 18, of which 14 were waited for; matrix products, arithmetic and copies ran while one was open for 12% of the time, Pallas kernels for 0%

commit v1 on v0

v1 whole, which is shorter than its diff:
```python
import functools
import math

import jax
import jax.numpy as jnp
from jax import lax
from jax.experimental import pallas as pl
from jax.experimental.pallas import tpu as pltpu
from jax.sharding import PartitionSpec as P

D = 1024
HEADS = 16
HD = 64
FF = 4096
PD = 16
GRID = 16
LEVELS = 1000
STEP = 7
FRAMES = 8
CLIPS = 2
PER_FRAME = GRID * GRID
TOK = FRAMES * PER_FRAME
BOTH = ("clip", "row")
VMEM_BYTES = 56 * 1024 * 1024

precise = lax.Precision.HIGHEST
beta_one = 0.9
beta_two = 0.999
adam_eps = 1e-08
weight_decay = 0.01
learn_rate = 1.0
norm_eps = 1e-06
f32 = jnp.float32
bf16 = jnp.bfloat16


def to_low(values):
    return values.astype(bf16)


def dot_low(formula, left, right):
    return jnp.einsum(formula, left, right, preferred_element_type=f32)


def mm(left, right, left_dim, right_dim):
    return lax.dot_general(
        left, right, (((left_dim,), (right_dim,)), ((), ())), preferred_element_type=f32
    )


def layer_norm(values):
    center = values - jnp.mean(values, axis=-1, keepdims=True)
    spread = jnp.mean(center * center, axis=-1, keepdims=True)
    return center * lax.rsqrt(spread + norm_eps)


def norm_parts(values):
    center = values - jnp.mean(values, axis=-1, keepdims=True)
    spread = jnp.mean(center * center, axis=-1, keepdims=True)
    inverse = lax.rsqrt(spread + norm_eps)
    return center * inverse, inverse


def norm_back(normed, inverse, grad):
    mean_g = jnp.mean(grad, axis=-1, keepdims=True)
    mean_gn = jnp.mean(grad * normed, axis=-1, keepdims=True)
    return inverse * (grad - mean_g - normed * mean_gn)


def modulate(normed, shift, scale):
    return normed * (1.0 + scale[:, None, :]) + shift[:, None, :]


def gelu_tanh(values):
    return jax.nn.gelu(values, approximate=True)


def frame_layout(clip_row, length_row):
    frame_idx = jnp.arange(FRAMES, dtype=jnp.int32)
    same_clip = clip_row[:, None] == clip_row[None, :]
    starts = jnp.min(jnp.where(same_clip, frame_idx[None, :], FRAMES), axis=1)
    frame_pos = frame_idx - starts
    slot_idx = jnp.arange(CLIPS, dtype=jnp.int32)
    length = jnp.sum(
        jnp.where(clip_row[:, None] == slot_idx[None, :], length_row[None, :], 0), axis=1
    )
    is_true = frame_pos < length
    stops = jnp.minimum(frame_idx + 1, starts + length)
    return (frame_pos, is_true, starts, stops)


def noise_mix(level_row):
    angle = (level_row.astype(f32) + 0.5) * (math.pi / (2 * LEVELS))
    return (jnp.cos(angle), jnp.sin(angle))


def group_angles(frame_pos, lanes):
    place = jnp.arange(GRID, dtype=jnp.int32)
    j = jnp.arange(lanes, dtype=jnp.int32) % (HD // 2)
    edges = (0, HD // 8, HD // 8 + 3 * HD // 16, HD // 2)
    tables, masks = [], []
    for k, along in enumerate((frame_pos, place, place)):
        size = edges[k + 1] - edges[k]
        frequency = 10000.0 ** (-(j - edges[k]).astype(f32) / size)
        masks.append((j >= edges[k]) & (j < edges[k + 1]))
        frequency = jnp.where(masks[k], frequency, 0.0)
        tables.append(along.astype(f32)[:, None] * frequency[None, :])
    shape = (FRAMES, GRID, GRID, lanes)
    result = []
    for fn in (jnp.cos, jnp.sin):
        at_f = fn(tables[0])[:, None, None, :]
        at_r = fn(tables[1])[None, :, None, :]
        at_c = fn(tables[2])[None, None, :, :]
        value = jnp.where(masks[0], at_f, jnp.where(masks[1], at_r, at_c))
        result.append(jnp.broadcast_to(value, shape).reshape(TOK, lanes))
    return result


def rotary_order(width):
    order = []
    heads = width // HD
    for half in range(2):
        for head in range(heads):
            offset = 0
            for part in (HD // 4, 3 * HD // 8, 3 * HD // 8):
                start = head * HD + offset + half * (part // 2)
                order.extend(range(start, start + part // 2))
                offset += part
    return order


def rotary_permutation(width):
    order = jnp.array(rotary_order(width), dtype=jnp.int32)
    return (jnp.arange(width, dtype=jnp.int32)[:, None] == order[None, :]).astype(bf16)


def shape_of_mesh():
    clips, rows = lax.axis_size("clip"), lax.axis_size("row")
    ny, nz = rows // 2, 4
    nx = clips // nz
    bits = [count.bit_length() - 1 for count in (rows, rows * nx)]
    return (ny, nx, nz), (1, bits[0], bits[1])


def exchange(values, mask):
    count = lax.axis_size("clip") * lax.axis_size("row")
    return lax.ppermute(values, BOTH, [(i, i ^ mask) for i in range(count)])


def along(number):
    sizes, bits = shape_of_mesh()
    return {m: m << bits[number] for m in range(1, sizes[number])}


def chip_gather(shard, use_y=True, hold=None, hold_x=None):
    z_masks, x_masks = along(2), along(1)
    y_masks = along(0) if use_y else {}
    got = [exchange(shard, mask) for mask in z_masks.values()]
    own = jnp.stack([shard] + got)
    if hold is not None:
        own = tie(own, hold)
    pieces = [(own, 0, 0, 0)]
    at_y = {m: exchange(own, mask) for m, mask in y_masks.items()}
    sent = own if hold_x is None else tie(own, hold_x)
    at_x = {m: exchange(sent, mask) for m, mask in x_masks.items()}
    pieces += [(array, m, 0, 0) for m, array in at_y.items()]
    pieces += [(array, 0, m, 0) for m, array in at_x.items()]
    half = own.shape[0] // 2
    for my in at_y:
        for mx in at_x:
            pieces.append((exchange(at_y[my][:half], x_masks[mx]), my, mx, 0))
            pieces.append((exchange(at_x[mx][half:], y_masks[my]), my, mx, half))
    return pieces


def chip_scatter(groups, use_y=True, direct=False, hold=None):
    z_masks, x_masks = along(2), along(1)
    y_masks = along(0) if use_y else {}
    half = groups[0, 0].shape[0] // 2
    at_y = {m: [[], []] for m in y_masks}
    at_x = {m: [[], []] for m in x_masks}
    slant = []
    for my in y_masks:
        for mx in x_masks:
            piece = groups[my, mx]
            if direct:
                slant.append((piece, y_masks[my] ^ x_masks[mx]))
                continue
            at_y[my][0].append(exchange(piece[:half], x_masks[mx]))
            at_x[mx][1].append(exchange(piece[half:], y_masks[my]))

    def total(piece, terms):
        if not terms:
            return piece
        result = piece.astype(f32)
        for term in terms:
            result = result + term.astype(f32)
        return to_low(result)

    def joined(piece, terms):
        if not (terms[0] or terms[1]):
            return piece
        return jnp.concatenate([total(piece[:half], terms[0]), total(piece[half:], terms[1])])

    sent = [(joined(groups[m, 0], at_y[m]), mask) for m, mask in y_masks.items()]
    sent += [(joined(groups[0, m], at_x[m]), mask) for m, mask in x_masks.items()]
    own = total(groups[0, 0], [exchange(piece, mask) for piece, mask in sent + slant])
    if hold is not None:
        own = tie(own, hold)
    result = own[0].astype(f32)
    for m, mask in z_masks.items():
        result = result + exchange(own[m], mask).astype(f32)
    return result, tuple(piece for piece, mask in sent), own


def tie(values, *others):
    return lax.optimization_barrier((values,) + others)[0]


def row_masks():
    return [1 << bit for bit in range(lax.axis_size("row").bit_length() - 1)]


def row_sum(values):
    for mask in row_masks():
        values = values + exchange(values, mask)
    return values


def row_gather(values):
    place = lax.axis_index("row")
    values = values[None]
    for mask in row_masks():
        other = exchange(values, mask)
        first = place & mask == 0
        values = jnp.concatenate(
            [jnp.where(first, values, other), jnp.where(first, other, values)], axis=0
        )
    return values


def spread(values, axes):
    names = axes if isinstance(axes, tuple) else (axes,)
    count = 1
    for name in names:
        count *= lax.axis_size(name)
    copies = jnp.broadcast_to(values[None], (count,) + values.shape)
    return lax.all_to_all(copies, axes, 0, 0, tiled=True)


def run_kernel(
    kernel, grid, inputs, outputs, scratch=(), scalars=None, after=(), flops=0, moved=2**22, exps=0
):
    count = 0 if scalars is None else 1

    def spec(block, index):
        if index is None:
            zeros = (0,) * len(block)
            return pl.BlockSpec(block, lambda *ids: zeros)
        return pl.BlockSpec(block, lambda *ids: index(*ids[: len(grid)]))

    arrays, in_specs = [], []
    for entry in inputs:
        arrays.append(entry[0])
        if len(entry) == 1:
            in_specs.append(spec(entry[0].shape, None))
        elif len(entry) == 2:
            in_specs.append(pl.BlockSpec(memory_space=entry[1]))
        else:
            in_specs.append(spec(entry[1], entry[2]))
    many, extra = len(arrays), len(after)
    arrays.extend(after)
    in_specs.extend([pl.BlockSpec(memory_space=pl.ANY)] * extra)
    out_specs, out_shape = [], []
    for shape, dtype, *rest in outputs:
        out_shape.append(jax.ShapeDtypeStruct(shape, dtype))
        if not rest:
            out_specs.append(spec(shape, None))
        elif len(rest) == 1:
            out_specs.append(pl.BlockSpec(memory_space=rest[0]))
        else:
            out_specs.append(spec(*rest))

    def wrapped(*refs):
        kernel(*refs[: count + many], *refs[count + many + extra :])

    call = pl.pallas_call(
        wrapped,
        grid_spec=pltpu.PrefetchScalarGridSpec(
            num_scalar_prefetch=count,
            grid=grid,
            in_specs=in_specs,
            out_specs=out_specs,
            scratch_shapes=list(scratch),
        ),
        out_shape=out_shape,
        compiler_params=pltpu.CompilerParams(vmem_limit_bytes=VMEM_BYTES),
        cost_estimate=pl.CostEstimate(flops=flops, bytes_accessed=moved, transcendentals=exps),
    )
    return call(*([] if scalars is None else [scalars]), *arrays)


def frame_rows(columns):
    return (PER_FRAME, columns), lambda f: (f, 0)


def head_mask(width, head, rotary):
    lane = lax.broadcasted_iota(jnp.int32, (1, width), 1)
    if rotary:
        return (lane % (width // 2)) // (HD // 2) == head
    return lane // HD == head


def chip_number(coords, my, mx, mz):
    return ((coords[2] ^ mz) * coords[5] + (coords[1] ^ mx)) * coords[4] + (coords[0] ^ my)


def run_place(coords, pieces, columns, after=()):
    rows = pieces[0][0].shape[1]
    chips = sum(piece[0].shape[0] for piece in pieces)
    edges = [sum(columns[:k]) for k in range(len(columns) + 1)]

    def kernel(coords_ref, *refs):
        sources = refs[: len(pieces)]
        targets = refs[len(pieces) : len(pieces) + len(columns)]
        sems = refs[-1]
        copies = []
        for source, (array, my, mx, first) in zip(sources, pieces):
            for k in range(array.shape[0]):
                chip = chip_number(coords_ref, my, mx, first + k)
                spot = pl.ds(pl.multiple_of(chip * rows, rows), rows)
                for number, target in enumerate(targets):
                    lanes = pl.ds(edges[number], columns[number])
                    copies.append(
                        pltpu.make_async_copy(
                            source.at[k, :, lanes], target.at[spot, :], sems.at[len(copies)]
                        )
                    )
        for copy in copies:
            copy.start()
        for copy in copies:
            copy.wait()

    return run_kernel(
        kernel,
        (1,),
        [(piece[0], pl.ANY) for piece in pieces],
        [((chips * rows, wide), bf16) for wide in columns],
        [pltpu.SemaphoreType.DMA((chips * len(columns),))],
        coords,
        after,
        moved=4 * chips * rows * sum(columns),
    )


def run_qkv(coords, noisy, embed, shift, scale, cosine, sine, pieces, after=()):
    rows, columns = pieces[0][0].shape[1:]
    width = columns // 3
    half = width // 2

    def kernel(coords_ref, noisy_ref, embed_ref, shift_ref, scale_ref, cos_ref, sin_ref, *refs):
        sources = refs[: len(pieces)]
        q_ref, k_ref, v_ref, in_ref, w_ref, sems = refs[len(pieces) :]
        frame = pl.program_id(0)

        def copies():
            made = []
            for source, (array, my, mx, first) in zip(sources, pieces):
                for k in range(array.shape[0]):
                    place = (coords_ref[2] ^ (first + k)) * coords_ref[5] + (coords_ref[1] ^ mx)
                    spot = pl.ds(pl.multiple_of(place * rows, rows), rows)
                    made.append(
                        pltpu.make_async_copy(source.at[k], w_ref.at[spot, :], sems.at[len(made)])
                    )
            return made

        @pl.when(frame == 0)
        def start():
            for copy in copies():
                copy.start()

        hidden = mm(noisy_ref[...], embed_ref[...], 1, 0)
        normed, unused = norm_parts(hidden)
        spot = pl.ds(frame, 1)
        attn_in = to_low(normed * (1.0 + scale_ref[spot, :]) + shift_ref[spot, :])
        in_ref[...] = attn_in

        @pl.when(frame == 0)
        def finish():
            for copy in copies():
                copy.wait()

        out = mm(attn_in, w_ref[...], 1, 0)
        cos, sin = cos_ref[...], sin_ref[...]
        for ref, base, factor in ((q_ref, 0, HD**-0.5), (k_ref, width, 1.0)):
            lower = out[:, base : base + half]
            upper = out[:, base + half : base + width]
            ref[:, :half] = to_low(lower * cos - upper * sin) * factor
            ref[:, half:] = to_low(upper * cos + lower * sin) * factor
        v_ref[...] = to_low(out[:, 2 * width :])

    chips = sum(piece[0].shape[0] for piece in pieces)
    return run_kernel(
        kernel,
        (FRAMES,),
        [
            (noisy, *frame_rows(PD)),
            (embed,),
            (shift,),
            (scale,),
            (cosine, *frame_rows(half)),
            (sine, *frame_rows(half)),
        ]
        + [(piece[0], pl.ANY) for piece in pieces],
        [((TOK, width), bf16, *frame_rows(width))] * 3
        + [((TOK, D), bf16, *frame_rows(D)), ((D, columns), bf16)],
        [pltpu.SemaphoreType.DMA((chips,))],
        coords,
        after,
        flops=2 * TOK * D * columns,
        moved=12 * 2**20,
    )


def attend_kernel(span_ref, q_ref, k_ref, v_ref, o_ref, lse_ref, q_scr, s_scr, m_scr, l_scr, acc_scr):
    frame = pl.program_id(0)
    width = q_ref.shape[1]
    heads = width // HD
    block = PER_FRAME
    start, stop = span_ref[0, frame], span_ref[1, frame]
    query = q_ref[...]
    for head in range(heads):
        q_scr[head * block : (head + 1) * block, :] = jnp.where(
            head_mask(width, head, True), query, jnp.zeros_like(query)
        )
    m_scr[...] = jnp.full_like(m_scr, -1e30)
    l_scr[...] = jnp.zeros_like(l_scr)
    acc_scr[...] = jnp.zeros_like(acc_scr)

    def scores(e, carry):
        keys = k_ref[pl.ds(e * block, block), :]
        for head in range(heads):
            rows = slice(head * block, (head + 1) * block)
            score = mm(q_scr[rows, :], keys, 1, 1)
            s_scr[e, rows, :] = score
            top = jnp.maximum(score[:, :128], score[:, 128:])
            m_scr[rows, :] = jnp.maximum(m_scr[rows, :], top)
        return carry

    lax.fori_loop(start, stop, scores, 0)
    for head in range(heads):
        rows = slice(head * block, (head + 1) * block)
        m_scr[rows, :] = jnp.broadcast_to(
            jnp.max(m_scr[rows, :], axis=1, keepdims=True), (block, 128)
        )

    def combine(e, carry):
        values = v_ref[pl.ds(e * block, block), :]
        for head in range(heads):
            rows = slice(head * block, (head + 1) * block)
            top = m_scr[rows, :]
            left = jnp.exp(s_scr[e, rows, :128] - top)
            right = jnp.exp(s_scr[e, rows, 128:] - top)
            l_scr[rows, :] = l_scr[rows, :] + (left + right)
            weight = jnp.concatenate([to_low(left), to_low(right)], axis=1)
            acc_scr[rows, :] = acc_scr[rows, :] + mm(weight, values, 1, 0)
        return carry

    lax.fori_loop(start, stop, combine, 0)
    result = jnp.zeros((block, width), f32)
    for head in range(heads):
        rows = slice(head * block, (head + 1) * block)
        total = jnp.sum(l_scr[rows, :], axis=1, keepdims=True)
        lse_ref[rows, :] = m_scr[rows, :] + jnp.log(total)
        result = jnp.where(head_mask(width, head, False), acc_scr[rows, :] / total, result)
    o_ref[...] = to_low(result).reshape(o_ref.shape)


def run_attend(span, query, keys, values, rows, after=()):
    width = query.shape[1]
    heads = width // HD
    block = PER_FRAME
    per_frame = block // rows
    return run_kernel(
        attend_kernel,
        (FRAMES,),
        [(query, *frame_rows(width)), (keys,), (values,)],
        [
            ((rows, FRAMES, per_frame, width), bf16, (rows, 1, per_frame, width), lambda f: (0, f, 0, 0)),
            ((FRAMES * heads * block, 128), f32, (heads * block, 128), lambda f: (f, 0)),
        ],
        [
            pltpu.VMEM((heads * block, width), bf16),
            pltpu.VMEM((FRAMES, heads * block, block), f32),
            pltpu.VMEM((heads * block, 128), f32),
            pltpu.VMEM((heads * block, 128), f32),
            pltpu.VMEM((heads * block, width), f32),
        ],
        span,
        after,
        flops=2 * 2 * 36 * block * block * 256 * heads,
        moved=10 * 2**20,
        exps=36 * block * block * heads,
    )


def attend_back_kernel(
    span_ref, q_ref, k_ref, v_ref, o_ref, g_ref, lse_ref, cos_ref, sin_ref, out_ref,
    q_scr, g_scr, d_scr, dq_scr, dk_scr, dv_scr, p_scr, s_scr,
):
    frame = pl.program_id(0)
    width = q_ref.shape[1]
    half = width // 2
    heads = width // HD
    block = PER_FRAME
    start, stop = span_ref[0, frame], span_ref[1, frame]

    @pl.when(frame == 0)
    def clear():
        dk_scr[...] = jnp.zeros_like(dk_scr)
        dv_scr[...] = jnp.zeros_like(dv_scr)

    query = q_ref[...]
    grad = g_ref[...].reshape(block, width)
    product = grad.astype(f32) * o_ref[...].reshape(block, width).astype(f32)
    for head in range(heads):
        rows = slice(head * block, (head + 1) * block)
        q_scr[rows, :] = jnp.where(head_mask(width, head, True), query, jnp.zeros_like(query))
        own = head_mask(width, head, False)
        g_scr[rows, :] = jnp.where(own, grad, jnp.zeros_like(grad))
        inner = jnp.sum(jnp.where(own, product, 0.0), axis=1, keepdims=True)
        d_scr[rows, :] = jnp.broadcast_to(inner, (block, 128))
    dq_scr[...] = jnp.zeros_like(dq_scr)

    def step(e, carry):
        spot = pl.ds(e * block, block)
        keys, values = k_ref[spot, :], v_ref[spot, :]
        for head in range(heads):
            rows = slice(head * block, (head + 1) * block)
            score = mm(q_scr[rows, :], keys, 1, 1)
            grad_w = mm(g_scr[rows, :], values, 1, 1)
            lse, inner = lse_ref[rows, :], d_scr[rows, :]
            for part in range(2):
                lanes = slice(part * 128, (part + 1) * 128)
                weight = jnp.exp(score[:, lanes] - lse)
                p_scr[rows, lanes] = to_low(weight)
                s_scr[rows, lanes] = to_low(weight * (grad_w[:, lanes] - inner))
            dq_scr[rows, :] = dq_scr[rows, :] + mm(s_scr[rows, :], keys, 1, 0)
        dk_scr[spot, :] = dk_scr[spot, :] + mm(s_scr[...], q_scr[...], 0, 0)
        dv_scr[spot, :] = dv_scr[spot, :] + mm(p_scr[...], g_scr[...], 0, 0)
        return carry

    lax.fori_loop(start, stop, step, 0)

    def unrotate(grads, cosine, sine, where, base):
        lower, upper = grads[:, :half], grads[:, half:]
        out_ref[where, base : base + half] = to_low(lower * cosine + upper * sine)
        out_ref[where, base + half : base + width] = to_low(upper * cosine - lower * sine)

    total = jnp.zeros((block, width), f32)
    for head in range(heads):
        rows = slice(head * block, (head + 1) * block)
        total = jnp.where(head_mask(width, head, True), dq_scr[rows, :], total)
    spot = pl.ds(frame * block, block)
    unrotate(total * HD**-0.5, cos_ref[spot, :], sin_ref[spot, :], spot, 0)

    @pl.when(frame == FRAMES - 1)
    def finish():
        def one(e, carry):
            spot = pl.ds(e * block, block)
            unrotate(dk_scr[spot, :], cos_ref[spot, :], sin_ref[spot, :], spot, width)
            out_ref[spot, 2 * width :] = to_low(dv_scr[spot, :])
            return carry

        lax.fori_loop(0, FRAMES, one, 0)


def run_attend_back(span, query, keys, values, out, grad, lse, cosine, sine, after=()):
    block = PER_FRAME
    rows, unused, per_frame, width = out.shape
    heads = width // HD
    parts = (rows, 1, per_frame, width), lambda f: (0, f, 0, 0)
    return run_kernel(
        attend_back_kernel,
        (FRAMES,),
        [
            (query, *frame_rows(width)),
            (keys,),
            (values,),
            (out, *parts),
            (grad, *parts),
            (lse, (heads * block, 128), lambda f: (f, 0)),
            (cosine,),
            (sine,),
        ],
        [((TOK, 3 * width), bf16)],
        [
            pltpu.VMEM((heads * block, width), bf16),
            pltpu.VMEM((heads * block, width), bf16),
            pltpu.VMEM((heads * block, 128), f32),
            pltpu.VMEM((heads * block, width), f32),
            pltpu.VMEM((TOK, width), f32),
            pltpu.VMEM((TOK, width), f32),
            pltpu.VMEM((heads * block, block), bf16),
            pltpu.VMEM((heads * block, block), bf16),
        ],
        span,
        after,
        flops=5 * 2 * 36 * block * block * 256 * heads,
        moved=12 * 2**20,
        exps=36 * block * block * heads,
    )[0]


def run_qkv_back(coords, noisy, embed, scale, attn_in, grad, weight, nx, nz, after=()):
    columns = weight.shape[1]
    rows = D // (nx * nz)

    def kernel(coords_ref, noisy_ref, embed_ref, scale_ref, in_ref, g_ref, w_ref, sum_ref, ge_ref, *refs):
        outs, acc = refs[:nx], refs[nx]
        frame = pl.program_id(0)
        noisy, grad = noisy_ref[...], g_ref[...]
        accumulate(acc, frame, mm(in_ref[...], grad, 0, 0))
        normed, inverse = norm_parts(mm(noisy, embed_ref[...], 1, 0))
        grad_in = mm(grad, w_ref[...], 1, 1)
        spot = pl.ds(frame, 1)
        sum_ref[spot, :D] = jnp.sum(grad_in, axis=0, keepdims=True)
        sum_ref[spot, D:] = jnp.sum(grad_in * normed, axis=0, keepdims=True)
        grad_h = norm_back(normed, inverse, grad_in * (1.0 + scale_ref[spot, :]))
        accumulate(ge_ref, frame, mm(noisy, to_low(grad_h), 0, 0))

        @pl.when(frame == FRAMES - 1)
        def finish():
            for mx in range(nx):
                for mz in range(nz):
                    place = (coords_ref[2] ^ mz) * coords_ref[5] + (coords_ref[1] ^ mx)
                    where = pl.ds(pl.multiple_of(place * rows, rows), rows)
                    outs[mx][mz] = to_low(acc[where, :])

    outs = run_kernel(
        kernel,
        (FRAMES,),
        [
            (noisy, *frame_rows(PD)),
            (embed,),
            (scale,),
            (attn_in, *frame_rows(D)),
            (grad, *frame_rows(columns)),
            (weight,),
        ],
        [((FRAMES, 2 * D), f32), ((PD, D), f32)] + [((nz, rows, columns), bf16)] * nx,
        [pltpu.VMEM((D, columns), f32)],
        coords,
        after,
        flops=4 * TOK * D * columns,
        moved=12 * 2**20,
    )
    return outs[0], outs[1], {(0, mx): out for mx, out in enumerate(outs[2:])}


REST = {
    name: slice(k * D, (k + 1) * D)
    for k, name in enumerate(("gate_a", "shift_m", "scale_m", "gate_m", "shift_f", "scale_f"))
}


def by_frame(ref, name, first, count, per_frame):
    rows = [
        jnp.broadcast_to(ref[pl.ds(first + k, 1), REST[name]], (per_frame, D))
        for k in range(count)
    ]
    return jnp.concatenate(rows, axis=0)


def store_sums(ref, first, number, values, per_frame):
    for k in range(values.shape[0] // per_frame):
        rows = values[k * per_frame : (k + 1) * per_frame]
        lanes = slice(number * D, (number + 1) * D)
        ref[pl.ds(first + k, 1), lanes] = jnp.sum(rows, axis=0, keepdims=True)


def run_proj(coords, attn, noisy, embed, rest, own, other, after=()):
    rows, tokens, width = attn.shape
    per_frame, steps = tokens // FRAMES, 2
    block, count = tokens // steps, FRAMES // steps

    def kernel(coords_ref, a_ref, n_ref, e_ref, rest_ref, own_ref, other_ref, h_ref, p_ref, in_ref):
        first = pl.program_id(0) * count
        mine = coords_ref[3] == 0
        attn_b = jnp.concatenate([a_ref[r] for r in range(rows)], axis=1)
        one, two = mm(attn_b, own_ref[...], 1, 0), mm(attn_b, other_ref[...], 1, 0)
        out = jnp.concatenate([jnp.where(mine, one, two), jnp.where(mine, two, one)], axis=1)
        p_ref[...] = out
        hidden = mm(n_ref[...], e_ref[...], 1, 0)
        hidden = hidden + by_frame(rest_ref, "gate_a", first, count, per_frame) * out
        h_ref[...] = hidden
        normed, unused = norm_parts(hidden)
        scale = by_frame(rest_ref, "scale_m", first, count, per_frame)
        shift = by_frame(rest_ref, "shift_m", first, count, per_frame)
        in_ref[...] = to_low(normed * (1.0 + scale) + shift)

    part = (block, D), lambda i: (i, 0)
    return run_kernel(
        kernel,
        (steps,),
        [
            (attn, (rows, block, width), lambda i: (0, i, 0)),
            (noisy, (block, PD), lambda i: (i, 0)),
            (embed,),
            (rest,),
            (own,),
            (other,),
        ],
        [((tokens, D), f32, *part), ((tokens, D), f32, *part), ((tokens, D), bf16, *part)],
        scalars=coords,
        after=after,
        flops=2 * tokens * D * D,
        moved=10 * 2**20,
    )


GELU_C = math.sqrt(2.0 / math.pi)
GELU_A = 0.044715


def gelu_value(x):
    return 0.5 * x * (1.0 + jnp.tanh(GELU_C * (x + GELU_A * (x * x * x))))


def gelu_slope(x):
    square = x * x
    t = jnp.tanh(GELU_C * x * (1.0 + GELU_A * square))
    return 0.5 * (1.0 + t) + (0.5 * GELU_C) * x * (1.0 - t * t) * (1.0 + 3.0 * GELU_A * square)


CHUNK = 512


def down_rows(weight):
    return weight, (CHUNK, D), lambda j: (j, 0)


def up_columns(weight):
    return weight, (D, CHUNK), lambda j: (0, j)


def run_up(mlp_in, up, after=()):
    tokens, hidden = mlp_in.shape[0], up.shape[1]

    def kernel(in_ref, up_ref, out_ref, act_ref):
        out = mm(in_ref[...], up_ref[...], 1, 0)
        out_ref[...] = out
        act_ref[...] = to_low(gelu_value(out))

    part = (tokens, CHUNK), lambda j: (0, j)
    return run_kernel(
        kernel,
        (hidden // CHUNK,),
        [(mlp_in,), up_columns(up)],
        [((tokens, hidden), f32, *part), ((tokens, hidden), bf16, *part)],
        after=after,
        flops=2 * tokens * D * hidden,
        moved=10 * 2**20,
    )


def run_up_down(mlp_in, up, down, after=()):
    tokens, hidden = mlp_in.shape[0], up.shape[1]
    steps = hidden // CHUNK

    def kernel(in_ref, up_ref, down_ref, out_ref, act_ref, part_ref, acc):
        j = pl.program_id(0)
        out = mm(in_ref[...], up_ref[...], 1, 0)
        out_ref[...] = out
        act = to_low(gelu_value(out))
        act_ref[...] = act
        accumulate(acc, j, mm(act, down_ref[...], 1, 0))

        @pl.when(j == steps - 1)
        def finish():
            part_ref[...] = to_low(acc[...])

    part = (tokens, CHUNK), lambda j: (0, j)
    return run_kernel(
        kernel,
        (steps,),
        [(mlp_in,), up_columns(up), down_rows(down)],
        [
            ((tokens, hidden), f32, *part),
            ((tokens, hidden), bf16, *part),
            ((tokens, D), bf16),
        ],
        [pltpu.VMEM((tokens, D), f32)],
        after=after,
        flops=4 * tokens * D * hidden,
        moved=16 * 2**20,
    )


def accumulate(acc, step, term):
    @pl.when(step == 0)
    def first():
        acc[...] = term

    @pl.when(step > 0)
    def more():
        acc[...] = acc[...] + term


def run_down(act, down, after=()):
    tokens, hidden = act.shape

    def kernel(act_ref, down_ref, out_ref):
        accumulate(out_ref, pl.program_id(0), mm(act_ref[...], down_ref[...], 1, 0))

    return run_kernel(
        kernel,
        (hidden // CHUNK,),
        [(act, (tokens, CHUNK), lambda j: (0, j)), down_rows(down)],
        [((tokens, D), f32)],
        after=after,
        flops=2 * tokens * D * hidden,
        moved=8 * 2**20,
    )[0]


def run_head(flags, hidden1, part, got, rest, head, target, after=()):
    tokens = hidden1.shape[0]
    per_frame = tokens // FRAMES

    def kernel(
        flag_ref, h_ref, p_ref, got_ref, rest_ref, head_ref, t_ref,
        gd_ref, gh_ref, sum_ref, ghead_ref, loss_ref,
    ):
        frame = pl.program_id(0)

        @pl.when(frame == 0)
        def clear():
            ghead_ref[...] = jnp.zeros_like(ghead_ref)

        mod = lambda name: rest_ref[pl.ds(frame, 1), REST[name]]
        down_out = p_ref[...] + got_ref[...].astype(f32)
        hidden = h_ref[...] + mod("gate_m") * down_out
        normed, inverse = norm_parts(hidden)
        scale = 1.0 + mod("scale_f")
        final_in = to_low(normed * scale + mod("shift_f"))
        pred = mm(final_in, head_ref[...], 1, 0)
        error = (pred - t_ref[...]) * flag_ref[frame]
        loss_ref[pl.ds(frame, 1), :] = jnp.broadcast_to(
            jnp.sum(jnp.sum(error * error, axis=1, keepdims=True), axis=0, keepdims=True), (1, 128)
        )
        grad_pred = to_low(2.0 * error / flag_ref[FRAMES])
        ghead_ref[...] = ghead_ref[...] + mm(final_in, grad_pred, 0, 0)
        grad_fin = mm(grad_pred, head_ref[...], 1, 1)
        store_sums(sum_ref, frame, 1, grad_fin, per_frame)
        store_sums(sum_ref, frame, 2, grad_fin * normed, per_frame)
        grad = norm_back(normed, inverse, grad_fin * scale)
        gh_ref[...] = grad
        store_sums(sum_ref, frame, 0, grad * down_out, per_frame)
        gd_ref[...] = to_low(grad * mod("gate_m"))

    part_spec = (per_frame, D), lambda f: (f, 0)
    return run_kernel(
        kernel,
        (FRAMES,),
        [
            (flags, pltpu.SMEM),
            (hidden1, *part_spec),
            (part, *part_spec),
            (got, *part_spec),
            (rest,),
            (head,),
            (target, (per_frame, PD), lambda f: (f, 0)),
        ],
        [
            ((tokens, D), bf16, *part_spec),
            ((tokens, D), f32, *part_spec),
            ((FRAMES, 3 * D), f32),
            ((D, PD), f32),
            ((FRAMES, 128), f32),
        ],
        after=after,
        flops=8 * tokens * D * PD,
        moved=10 * 2**20,
    )


def run_act_back(grad, down, up_out, after=()):
    tokens, hidden = up_out.shape

    def kernel(g_ref, down_ref, up_ref, out_ref):
        grad_act = mm(g_ref[...], down_ref[...], 1, 1)
        out_ref[...] = to_low(grad_act * gelu_slope(up_ref[...]))

    part = (tokens, CHUNK), lambda j: (0, j)
    return run_kernel(
        kernel,
        (hidden // CHUNK,),
        [(grad,), down_rows(down), (up_out, *part)],
        [((tokens, hidden), bf16, *part)],
        after=after,
        flops=2 * tokens * D * hidden,
        moved=10 * 2**20,
    )[0]


def run_act_up_back(grad, down, up_out, up, after=()):
    tokens, hidden = up_out.shape
    steps = hidden // CHUNK

    def kernel(g_ref, down_ref, o_ref, up_ref, out_ref, part_ref, acc):
        j = pl.program_id(0)
        grad_act = mm(g_ref[...], down_ref[...], 1, 1)
        grad_out = to_low(grad_act * gelu_slope(o_ref[...]))
        out_ref[...] = grad_out
        accumulate(acc, j, mm(grad_out, up_ref[...], 1, 1))

        @pl.when(j == steps - 1)
        def finish():
            part_ref[...] = to_low(acc[...])

    part = (tokens, CHUNK), lambda j: (0, j)
    return run_kernel(
        kernel,
        (steps,),
        [(grad,), down_rows(down), (up_out, *part), up_columns(up)],
        [((tokens, hidden), bf16, *part), ((tokens, D), bf16)],
        [pltpu.VMEM((tokens, D), f32)],
        after=after,
        flops=4 * tokens * D * hidden,
        moved=16 * 2**20,
    )


def run_up_back(grad, up, after=()):
    tokens, hidden = grad.shape

    def kernel(g_ref, up_ref, out_ref):
        accumulate(out_ref, pl.program_id(0), mm(g_ref[...], up_ref[...], 1, 1))

    return run_kernel(
        kernel,
        (hidden // CHUNK,),
        [(grad, (tokens, CHUNK), lambda j: (0, j)), up_columns(up)],
        [((tokens, D), f32)],
        after=after,
        flops=2 * tokens * D * hidden,
        moved=8 * 2**20,
    )[0]


def group_list(sizes):
    ny, nx, nz = sizes
    return [(my, mx) for my in range(ny) for mx in range(nx)]


def run_down_dw(coords, sizes, acts, grads, after=()):
    groups, nz = group_list(sizes), sizes[2]
    hidden = acts[0].shape[1]
    rows = hidden // (len(groups) * nz)
    steps = hidden // CHUNK

    def kernel(coords_ref, a_ref, b_ref, ga_ref, gb_ref, *refs):
        outs, acc = refs[: len(groups)], refs[len(groups)]
        j = pl.program_id(0)
        acc[j] = mm(a_ref[...], ga_ref[...], 0, 0) + mm(b_ref[...], gb_ref[...], 0, 0)

        @pl.when(j == steps - 1)
        def finish():
            for out, (my, mx) in zip(outs, groups):
                for mz in range(nz):
                    first = chip_number(coords_ref, my, mx, mz) * rows
                    spot = pl.ds(pl.multiple_of(first % CHUNK, rows), rows)
                    out[mz] = to_low(acc[first // CHUNK, spot, :])

    part = (acts[0].shape[0], CHUNK), lambda j: (0, j)
    outs = run_kernel(
        kernel,
        (steps,),
        [(acts[0], *part), (acts[1], *part), (grads[0],), (grads[1],)],
        [((nz, rows, D), bf16)] * len(groups),
        [pltpu.VMEM((steps, CHUNK, D), f32)],
        coords,
        after,
        flops=4 * acts[0].shape[0] * D * hidden,
        moved=10 * 2**20,
    )
    return dict(zip(groups, outs))


def run_up_dw(coords, sizes, ins, grads, proj, after=()):
    groups, nz = group_list(sizes), sizes[2]
    hidden = grads[0].shape[1]
    rows = D // (len(groups) * nz)
    steps = hidden // CHUNK

    def kernel(coords_ref, a_ref, b_ref, ga_ref, gb_ref, proj_ref, *refs):
        outs, acc = refs[: len(groups)], refs[len(groups)]
        j = pl.program_id(0)

        @pl.when(j < steps)
        def up_part():
            acc[...] = mm(a_ref[...], ga_ref[...], 0, 0) + mm(b_ref[...], gb_ref[...], 0, 0)

        @pl.when(j == steps)
        def proj_part():
            acc[...] = proj_ref[...].astype(f32)

        for out, (my, mx) in zip(outs, groups):
            for mz in range(nz):
                first = chip_number(coords_ref, my, mx, mz) * rows
                out[mz] = to_low(acc[pl.ds(pl.multiple_of(first, rows), rows), :])

    part = (grads[0].shape[0], CHUNK), lambda j: (0, jnp.minimum(j, steps - 1))
    outs = run_kernel(
        kernel,
        (steps + 1,),
        [(ins[0],), (ins[1],), (grads[0], *part), (grads[1], *part), (proj,)],
        [((nz, rows, hidden + CHUNK), bf16, (nz, rows, CHUNK), lambda j: (0, 0, j))] * len(groups),
        [pltpu.VMEM((D, CHUNK), f32)],
        coords,
        after,
        flops=4 * ins[0].shape[0] * D * hidden,
        moved=14 * 2**20,
    )
    return dict(zip(groups, outs))


def run_proj_back(coords, grad_h2, part, got, hidden1, proj_out, rest, own, other, attn, noisy, after=()):
    rows, tokens, width = attn.shape
    per_frame, steps = tokens // FRAMES, 2
    block, count = tokens // steps, FRAMES // steps

    def kernel(
        coords_ref, g_ref, p_ref, got_ref, h_ref, po_ref, rest_ref, own_ref, other_ref, a_ref, n_ref,
        ga_ref, mine_ref, theirs_ref, sum_ref, ge_ref, acc,
    ):
        step = pl.program_id(0)
        first = step * count
        mine = coords_ref[3] == 0
        grad_mlp = p_ref[...] + got_ref[...].astype(f32)
        normed, inverse = norm_parts(h_ref[...])
        store_sums(sum_ref, first, 1, grad_mlp, per_frame)
        store_sums(sum_ref, first, 2, grad_mlp * normed, per_frame)
        scale = by_frame(rest_ref, "scale_m", first, count, per_frame)
        grad = g_ref[...] + norm_back(normed, inverse, grad_mlp * (1.0 + scale))
        store_sums(sum_ref, first, 0, grad * po_ref[...], per_frame)
        low = to_low(grad * by_frame(rest_ref, "gate_a", first, count, per_frame))
        lower, upper = low[:, : D // 2], low[:, D // 2 :]
        grad_attn = mm(jnp.where(mine, lower, upper), own_ref[...], 1, 1)
        grad_attn = grad_attn + mm(jnp.where(mine, upper, lower), other_ref[...], 1, 1)
        grad_attn = to_low(grad_attn)
        attn_b = jnp.concatenate([a_ref[r] for r in range(rows)], axis=1)
        for r in range(rows):
            ga_ref[r] = grad_attn[:, r * width : (r + 1) * width]
        accumulate(acc, step, mm(attn_b, low, 0, 0))
        accumulate(ge_ref, step, mm(n_ref[...], to_low(grad), 0, 0))

        @pl.when(step == steps - 1)
        def finish():
            lower, upper = to_low(acc[:, : D // 2]), to_low(acc[:, D // 2 :])
            mine_ref[...] = jnp.where(mine, lower, upper)
            theirs_ref[...] = jnp.where(mine, upper, lower)

    piece = (block, D), lambda i: (i, 0)
    wide = (rows, block, width), lambda i: (0, i, 0)
    return run_kernel(
        kernel,
        (steps,),
        [
            (grad_h2, *piece),
            (part, *piece),
            (got, *piece),
            (hidden1, *piece),
            (proj_out, *piece),
            (rest,),
            (own,),
            (other,),
            (attn, *wide),
            (noisy, (block, PD), lambda i: (i, 0)),
        ],
        [
            ((rows, tokens, width), bf16, *wide),
            ((D, D // 2), bf16),
            ((D, D // 2), bf16),
            ((FRAMES, 3 * D), f32),
            ((PD, D), f32),
        ],
        [pltpu.VMEM((D, D), f32)],
        coords,
        after,
        flops=4 * tokens * D * D,
        moved=18 * 2**20,
    )


def run_lamb(entries, slots, fixes, after=()):
    def kernel(*refs):
        many = len(entries)
        ins, outs = refs[: 4 * many], refs[4 * many : 6 * many]
        sums = refs[6 * many]
        lane = lax.broadcasted_iota(jnp.int32, (1, 128), 1)
        row = jnp.zeros((1, 128), f32)
        for k, slot in enumerate(slots):
            weight, grad, first, second = (ref[...] for ref in ins[4 * k : 4 * k + 4])
            mom_ref, update_ref = outs[2 * k : 2 * k + 2]
            first_n, second_n, update = lamb_direction(weight, grad, first, second, *fixes)
            mom_ref[0] = first_n
            mom_ref[1] = second_n
            update_ref[...] = update
            for value, place in ((weight, 2 * slot), (update, 2 * slot + 1)):
                total = jnp.sum(value * value, axis=0, keepdims=True)
                total = jnp.sum(total, axis=1, keepdims=True)
                row = row + jnp.where(lane == place, total, 0.0)
        sums[...] = row

    outputs = []
    for weight, *unused in entries:
        outputs += [((2,) + weight.shape, f32), (weight.shape, f32)]
    moved = 28 * sum(entry[0].size for entry in entries)
    flat = [(array,) for entry in entries for array in entry]
    outs = run_kernel(kernel, (1,), flat, outputs + [((1, 128), f32)], after=after, moved=moved)
    return outs[0:-1:2], outs[1:-1:2], outs[-1]


def run_update(weights, updates, totals):
    def kernel(totals_ref, *refs):
        many = len(weights)
        lane = lax.broadcasted_iota(jnp.int32, (1, 128), 1)
        norms = jnp.sqrt(jnp.sum(totals_ref[...], axis=0, keepdims=True))
        for k in range(many):
            weight_ref, update_ref, out_ref = refs[k], refs[many + k], refs[2 * many + k]
            pick = lambda at: jnp.sum(jnp.where(lane == at, norms, 0.0), axis=1, keepdims=True)
            trust = learn_rate * (pick(2 * k) / pick(2 * k + 1))
            out_ref[...] = weight_ref[...] - trust * update_ref[...]

    return run_kernel(
        kernel,
        (1,),
        [(totals,)] + [(array,) for array in list(weights) + list(updates)],
        [(weight.shape, f32) for weight in weights],
        moved=12 * sum(weight.size for weight in weights),
    )


def lamb_direction(weight, gradient, first_m, second_m, fix_one, fix_two):
    first_n = beta_one * first_m + (1.0 - beta_one) * gradient
    second_n = jnp.sqrt(beta_two * second_m * second_m + (1.0 - beta_two) * gradient * gradient)
    update = first_n / fix_one / (second_n / math.sqrt(fix_two) + adam_eps) + weight_decay * weight
    return (first_n, second_n, update)


def body(
    latents, noise, levels, clip_ids, clip_lens,
    embed_w, table_w, adaln_w, qkv_w, proj_w, up_w, down_w, head_w,
    embed_avg, table_avg, adaln_avg, qkv_avg, proj_avg, up_avg, down_avg, head_avg,
    embed_sq, table_sq, adaln_sq, qkv_sq, proj_sq, up_sq, down_sq, head_sq,
):
    masters = (embed_w, table_w, adaln_w, qkv_w, proj_w, up_w, down_w, head_w)
    firsts = (embed_avg, table_avg, adaln_avg, qkv_avg, proj_avg, up_avg, down_avg, head_avg)
    seconds = (embed_sq, table_sq, adaln_sq, qkv_sq, proj_sq, up_sq, down_sq, head_sq)
    clips, rows = lax.axis_size("clip"), lax.axis_size("row")
    count_dev = clips * rows
    sizes, unused_bits = shape_of_mesh()
    ny, nx, nz = sizes
    clip_index, row_index = lax.axis_index("clip"), lax.axis_index("row")
    core = row_index % 2
    coords = jnp.stack(
        [
            row_index // 2,
            clip_index % nx,
            clip_index // nx,
            core,
            jnp.full_like(core, ny),
            jnp.full_like(core, nx),
        ]
    ).astype(jnp.int32)
    part = D // count_dev
    width = D // rows
    row_local = GRID // rows
    per_frame = row_local * GRID
    count_tok = FRAMES * per_frame
    hidden = FF // 2
    unit = FF // count_dev
    level_row = levels[0]
    frame_pos, is_true, starts, stops = frame_layout(clip_ids[0], clip_lens[0])
    span = jnp.stack([starts, stops]).astype(jnp.int32)

    own_count = jnp.sum(is_true.astype(f32))
    packed = jnp.concatenate(
        [
            level_row.astype(f32),
            jnp.broadcast_to(own_count, (8,)),
            embed_w.reshape(-1),
            head_w.reshape(-1),
        ]
    )
    everyone = spread(packed.reshape(1, -1), BOTH).reshape(count_dev, -1)
    all_levels = everyone[::rows, :FRAMES].astype(jnp.int32).reshape(-1)
    count = jnp.sum(everyone[::rows, FRAMES]) * PER_FRAME
    embed_b = to_low(everyone[:, 16 : 16 + PD * part].reshape(count_dev, PD, part))
    embed_b = embed_b.transpose(1, 0, 2).reshape(PD, D)
    head_b = to_low(everyone[:, 16 + PD * part :]).reshape(D, PD)

    one_hot = (all_levels[:, None] == jnp.arange(LEVELS, dtype=jnp.int32)[None, :]).astype(f32)
    cond = dot_low("fl,ld->fd", to_low(one_hot), to_low(table_w))
    cond_act = to_low(jax.nn.silu(cond))
    adaln_low = to_low(adaln_w)

    def mod_terms(lower, upper):
        wide = (upper - lower) * D // rows
        terms = to_low(dot_low("fd,dm->fm", cond_act, adaln_low[:, lower * D : upper * D]))
        terms = terms.reshape(clips, FRAMES, rows, wide).transpose(0, 2, 1, 3)
        return terms.reshape(count_dev, FRAMES, wide)

    def modulation(terms):
        total = row_gather(jnp.sum(terms.astype(f32), axis=0))
        return total.transpose(1, 0, 2).reshape(FRAMES, -1)

    first_terms = lax.all_to_all(mod_terms(0, 2), BOTH, 0, 0, tiled=True)
    first = modulation(first_terms)
    shift_a, scale_a = first[:, :D], first[:, D:]

    alpha, sigma = noise_mix(level_row)
    clean = latents[0].reshape(FRAMES, per_frame, PD)
    fresh = noise[0].reshape(FRAMES, per_frame, PD)
    noisy = alpha[:, None, None] * clean + sigma[:, None, None] * fresh
    target = (alpha[:, None, None] * fresh - sigma[:, None, None] * clean).reshape(count_tok, PD)
    noisy_own = to_low(noisy).reshape(count_tok, PD)
    perm = rotary_permutation(width)
    qkv_low = to_low(qkv_w).reshape(part, 3, rows, width)
    turned = to_low(dot_low("dgrw,wv->rdgv", qkv_low[:, :2], perm))
    mine = jnp.concatenate([turned, qkv_low[:, 2:].transpose(2, 0, 1, 3)], axis=2)
    mine = mine.reshape(rows, part, 3 * width)
    token_cols = count_tok * PD // part
    tokens = jnp.broadcast_to(noisy_own.reshape(1, part, token_cols), (rows, part, token_cols))
    mine = tie(jnp.concatenate([mine, tokens], axis=2), everyone)
    mine = lax.all_to_all(mine, "row", 0, 0, tiled=True)
    noisy_all = mine[:, :, 3 * width :].reshape(rows, FRAMES, per_frame, PD)
    noisy_all = noisy_all.transpose(1, 0, 2, 3).reshape(TOK, PD)
    qkv_pieces = chip_gather(
        mine[:, :, : 3 * width].reshape(rows * part, 3 * width), False, hold=first_terms
    )

    def halves(weight, blocks):
        parts = weight.reshape(weight.shape[0], -1, 2, weight.shape[1] // (2 * blocks))
        mine = lax.dynamic_index_in_dim(parts, core, 2, keepdims=False)
        theirs = lax.dynamic_index_in_dim(parts, 1 - core, 2, keepdims=False)
        return mine.reshape(weight.shape[0], -1), theirs.reshape(weight.shape[0], -1)

    up_mine, up_theirs = halves(to_low(up_w), count_dev // 2)
    proj_mine, proj_theirs = halves(to_low(proj_w), 1)
    tall_mine = jnp.concatenate([up_mine, proj_mine], axis=1)
    tall_got = exchange(jnp.concatenate([up_theirs, proj_theirs], axis=1), 1)
    is_zero = core == 0
    tall = jnp.concatenate(
        [jnp.where(is_zero, tall_mine, tall_got), jnp.where(is_zero, tall_got, tall_mine)]
    )
    tall_pieces = chip_gather(tall, hold=qkv_pieces[0][0], hold_x=qkv_pieces[1][0])
    down_pieces = chip_gather(tie(to_low(down_w), tall_pieces[0][0]))

    cosine, sine = group_angles(frame_pos, width // 2)
    query, keys, values, attn_in, qkv_b = run_qkv(
        coords, noisy_all, embed_b, shift_a, scale_a, cosine, sine, qkv_pieces,
        after=(tall_pieces[0][0],),
    )
    attn_heads, lse = run_attend(span, query, keys, values, rows)
    rest_terms = lax.all_to_all(tie(mod_terms(2, 8), query), BOTH, 0, 0, tiled=True)
    rest = modulation(rest_terms)

    def swap_row(wide):
        return lax.all_to_all(wide, "row", 0, 0, tiled=True)

    attn = tie(attn_heads, rest_terms, down_pieces[0][0]).reshape(rows, count_tok, width)
    attn = swap_row(attn)
    up_b, proj_own = run_place(coords, tall_pieces, (hidden, D // 2), after=(attn_heads,))
    proj_other = exchange(proj_own, 1)
    hidden1, proj_out, mlp_in = run_proj(
        coords, attn, noisy_own, embed_b, rest, proj_own, proj_other
    )
    mlp_in_other = exchange(mlp_in, 1)
    up_out, act = run_up(mlp_in, up_b)
    down_b = run_place(coords, down_pieces, (D,), after=(act,))[0]
    up_out_other, act_other, part_other = run_up_down(mlp_in_other, up_b, down_b)
    part_got = exchange(part_other, 1)
    part_own = run_down(act, down_b, after=(part_other,))
    flags = jnp.concatenate([is_true.astype(f32), (PD * count).reshape(1)])
    grad_down_out, grad_h2, sums_f, grad_head, losses = run_head(
        flags, hidden1, part_own, part_got, rest, head_b, target
    )
    loss_local = jnp.sum(losses[:, 0])

    grad_down_other = exchange(grad_down_out, 1)
    grad_up = run_act_back(grad_down_out, down_b, up_out)
    down_groups = run_down_dw(
        coords, sizes, (act, act_other), (grad_down_out, grad_down_other), after=(grad_up,)
    )
    scatter_down = lambda hold: chip_scatter(down_groups, hold=hold)
    grad_up_other, mlp_other = run_act_up_back(
        grad_down_other, down_b, up_out_other, up_b, after=(down_groups[0, 0],)
    )
    mlp_got = exchange(mlp_other, 1)
    mlp_own = run_up_back(grad_up, up_b, after=(mlp_other,))
    grad_attn, proj_mine, proj_theirs, sums_m, embed_h1 = run_proj_back(
        coords, grad_h2, mlp_own, mlp_got, hidden1, proj_out, rest,
        proj_own, proj_other, attn, noisy_own,
    )
    grad_attn = swap_row(grad_attn).reshape(rows, FRAMES, per_frame, width)
    proj_term = to_low(proj_mine.astype(f32) + exchange(proj_theirs, 1).astype(f32))
    tall_groups = run_up_dw(
        coords, sizes, (mlp_in, mlp_in_other), (grad_up, grad_up_other), proj_term
    )
    down_sum, down_xy, down_z = scatter_down(tall_groups[0, 0])
    tall_sum, tall_xy, tall_z = chip_scatter(tall_groups, direct=True)
    grad_qkv = run_attend_back(
        span, query, keys, values, attn_heads, grad_attn, lse, cosine, sine,
        after=(tall_groups[0, 0], down_z),
    )
    sums_a, grad_embed, qkv_groups = run_qkv_back(
        coords, noisy_all, embed_b, scale_a, attn_in, grad_qkv, qkv_b, nx, nz,
        after=(tall_z, down_sum),
    )
    qkv_sum, unused_xy, qkv_z = chip_scatter(qkv_groups, False)
    grad_embed = grad_embed + embed_h1

    keep = lax.dynamic_slice_in_dim(tall_sum, core * part, part)
    got = exchange(to_low(lax.dynamic_slice_in_dim(tall_sum, (1 - core) * part, part)), 1)
    got = got.astype(f32)
    pair_sum = jnp.stack([jnp.where(is_zero, keep, got), jnp.where(is_zero, got, keep)], axis=1)
    up_sum = pair_sum[:, :, :hidden].reshape(part, 2, count_dev // 2, unit)
    up_sum = up_sum.transpose(0, 2, 1, 3).reshape(part, FF)
    proj_sum = pair_sum[:, :, hidden:].reshape(part, D)
    qkv_sum = tie(to_low(qkv_sum), tall_sum).reshape(rows, part, 3 * width)
    qkv_sum = swap_row(qkv_sum).reshape(rows, part, 3, width)
    turned = dot_low("rdgv,wv->dgrw", qkv_sum[:, :, :2], perm)
    straight = qkv_sum[:, :, 2:].transpose(1, 2, 0, 3).astype(f32)
    qkv_sum = jnp.concatenate([turned, straight], axis=1).reshape(part, 3 * D)

    def mod_row(values_mod):
        wide = values_mod.shape[1] // rows
        total = to_low(row_sum(values_mod))
        return lax.dynamic_slice_in_dim(total, row_index * wide, wide, axis=1)

    def mod_all(total):
        wide = total.shape[-1]
        total = total.reshape(clips, rows, FRAMES, wide)
        return total.transpose(0, 2, 1, 3).reshape(clips * FRAMES, rows * wide)

    mod_rest = mod_row(jnp.concatenate([sums_m, sums_f], axis=1))
    mod_rest = mod_all(spread(tie(mod_rest, grad_qkv), BOTH))

    small = jnp.concatenate(
        [
            grad_embed.reshape(PD, count_dev, part).transpose(1, 0, 2).reshape(count_dev, -1),
            grad_head.reshape(count_dev, -1),
        ],
        axis=1,
    )
    small = to_low(small).reshape(count_dev, 1, -1)
    mod_first = mod_row(sums_a)
    wide = mod_first.shape[-1]
    lines = small.shape[-1] // wide
    last = jnp.concatenate(
        [
            jnp.broadcast_to(mod_first[None], (count_dev, FRAMES, wide)),
            small.reshape(count_dev, lines, wide),
        ],
        axis=1,
    )
    last = lax.all_to_all(tie(last, qkv_z), BOTH, 0, 0, tiled=True)
    mod_first = mod_all(last[:, :FRAMES])
    small = jnp.sum(last[:, FRAMES:].astype(f32), axis=0).reshape(-1)
    embed_sum = small[: PD * part].reshape(PD, part)
    head_sum = small[PD * part :].reshape(part, PD)
    grad_mod_b = jnp.concatenate([mod_first, mod_rest], axis=1)
    grad_adaln = dot_low("fd,fm->dm", cond_act, grad_mod_b)
    grad_cond_act = dot_low("fm,dm->fd", grad_mod_b, adaln_low)
    unused_silu, silu_pull = jax.vjp(jax.nn.silu, cond)
    grad_cond = silu_pull(grad_cond_act)[0]
    grad_table = jnp.einsum(
        "fl,fd->dl", one_hot, grad_cond, precision=precise, preferred_element_type=f32
    )

    fixes = (1.0 - beta_one**STEP, 1.0 - beta_two**STEP)
    reduced = (
        embed_sum, grad_table, grad_adaln, qkv_sum, proj_sum, up_sum, down_sum, head_sum.T,
    )
    turned = (1, 7)
    flip = lambda k, array: jnp.swapaxes(array, -1, -2) if k in turned else array
    weights = [flip(k, array) for k, array in enumerate(masters)]
    entries = [
        (weights[k], reduced[k], flip(k, firsts[k]), flip(k, seconds[k])) for k in range(8)
    ]
    moms, updates, rows_of_sums = [None] * 8, [None] * 8, []
    for group in ((6,), (4, 5), (3,), (0, 1, 2, 7)):
        got_moms, got_updates, sums = run_lamb([entries[k] for k in group], group, fixes)
        rows_of_sums.append(sums)
        for k, mom, update in zip(group, got_moms, got_updates):
            moms[k], updates[k] = flip(k, mom), update
    lane = jnp.arange(128, dtype=jnp.int32)[None, :]
    sums = sum(rows_of_sums) + jnp.where(lane == 16, loss_local, 0.0)
    totals = spread(sums, BOTH).reshape(count_dev, 128)
    news = run_update(weights, updates, totals)
    news = [flip(k, array) for k, array in enumerate(news)]
    totals = jnp.sum(totals, axis=0)
    norms = jnp.sqrt(totals[:16].reshape(8, 2))
    return (*news, *moms, norms, totals[16:17] / (PD * count))


def solution(mesh):
    wide, tall = P(None, BOTH), P(BOTH, None)
    weights = (wide, wide, tall, tall, tall, tall, tall, tall)
    moments = (P(None, None, BOTH),) * 2 + (P(None, BOTH, None),) * 6
    return jax.shard_map(
        body,
        mesh=mesh,
        in_specs=(
            P("clip", None, "row", None),
            P("clip", None, "row", None),
            P("clip", None),
            P("clip", None),
            P("clip", None),
        )
        + weights * 3,
        out_specs=weights + moments + (P(), P()),
        check_vma=False,
    )
```

time: 2680 us -> 622 us (0.23)
  waiting for transfers between devices: 1720 us -> 164 us
  matrix products: 356 us -> 5.54 us
  local copies, waits for them, and re-layouts: 312 us -> 35.8 us
  Pallas kernels: 0 us -> 256 us
  blocking collectives: 145 us -> 10.6 us
  starting transfers between devices: 1.51 us -> 107 us
  other arithmetic: 109 us -> 30.6 us
    reduce_scatter x6 -> x0, waiting for transfers between devices: 1150 us -> none  [the longest x1 354 us: body(): lax.psum_scatter(grad_adaln, ('clip', 'row'), scatter_dimension=0, tiled=...]
    unnamed x21 -> x0, waiting for transfers between devices: 349 us -> none
    dot_general x132 -> x8, matrix products: 353 us -> 5.54 us  [the longest x7 4.6 us: dot_low(): return jnp.einsum(formula, left, right, preferred_element_type=f32)]
    pallas_call x0 -> x22, Pallas kernels: none -> 256 us  [run_kernel(): return call(*([] if scalars is None else [scalars]), *arrays)]
    all_gather x8 -> x0, waiting for transfers between devices: 206 us -> none  [the longest x1 115 us: body(): lax.all_gather(to_low(adaln_w), ('clip', 'row'), axis=0, tiled=True)]
    ppermute x0 -> x51, waiting for transfers between devices: none -> 142 us  [exchange(): return lax.ppermute(values, BOTH, [(i, i ^ mask) for i in range(count)])]
    all_gather x2 -> x0, blocking collectives: 83.6 us -> none  [the longest x1 43.6 us: body(): lax.all_gather(to_low(embed_w), ('clip', 'row'), axis=1, tiled=True)]
    psum x2 -> x0, blocking collectives: 60.9 us -> none  [the longest x1 43.2 us: body(): lax.psum((jnp.stack(squares_w), jnp.stack(squares_u), loss_local), ('clip...]
  transfers between devices with their start and end apart: 18 -> 60, of which waited for: 14 -> 21; matrix products, arithmetic and copies ran while one was open for 12% -> 9% of each run, Pallas kernels for 0% -> 33%
where the time goes in v1:
time: 622 us; the launch traced here: 615 us
  Pallas kernels  256 us (41%)
  waiting for transfers between devices  164 us (26%)
  starting transfers between devices  107 us (17%)
  local copies, waits for them, and re-layouts  35.8 us (6%)
  other arithmetic  30.6 us (5%)
  blocking collectives  10.6 us (2%)
    pallas_call x22, Pallas kernels, run_kernel(): return call(*([] if scalars is None else [scalars]), *arrays)  256 us
    ppermute x51, waiting for transfers between devices, exchange(): return lax.ppermute(values, BOTH, [(i, i ^ mask) for i in range(count)])  142 us
    ppermute x51, starting transfers between devices, exchange(): return lax.ppermute(values, BOTH, [(i, i ^ mask) for i in range(count)])  57.7 us
    all_to_all x3, starting transfers between devices, swap_row(): return lax.all_to_all(wide, 'row', 0, 0, tiled=True)  20 us
    all_to_all x2, waiting for transfers between devices, spread(): return lax.all_to_all(copies, axes, 0, 0, tiled=True)  13.7 us
  transfers between devices with their start and end apart: 60, of which 21 were waited for; matrix products, arithmetic and copies ran while one was open for 9% of the time, Pallas kernels for 33%

profile of v1, /device:TPU:0, one launch (start us, length us, event | category | flops | bytes accessed | tf_op | source)
XLA Modules:
  0.0 615.0 jit_solution(13792969390263003398)
XLA Ops:
  47.5 16.6 %collective-permute-done.2 = bf16[128,768]{1,0:T(8,128)(2,1)S(1)} collective-permute-done((bf16[128,768]{1,0:T(8,128)(2,1)S(1)}, bf16[128,768]{1,0:T(8,128)(2,1)S(1)}, u32[]{:S(2)}, u32[]{:S(2)}) %collective-permute-start.2) | collective-permute-done | bytes 196640 | tf_op jit(solution)/shard_map/ppermute | solution.py:147
  65.4 13.3 %collective-permute-done.3 = bf16[128,768]{1,0:T(8,128)(2,1)S(1)} collective-permute-done((bf16[128,768]{1,0:T(8,128)(2,1)S(1)}, bf16[128,768]{1,0:T(8,128)(2,1)S(1)}, u32[]{:S(2)}, u32[]{:S(2)}) %collective-permute-start.3) | collective-permute-done | bytes 196640 | tf_op jit(solution)/shard_map/ppermute | solution.py:147
  85.0 13.8 %collective-permute-done.5.refs_8_ = bf16[4,128,768]{2,1,0:T(8,128)(2,1)S(1)} collective-permute-done((bf16[4,128,768]{2,1,0:T(8,128)(2,1)S(1)}, bf16[4,128,768]{2,1,0:T(8,128)(2,1)S(1)}, u32[]{:S(2)}, u32[]{:S(2)}) %collective-permute-start.5) | collective-permute-done | bytes 786464 | tf_op jit(solution)/shard_map/ppermute | solution.py:147
  99.7 14.9 %shard_map.421 = (bf16[2048,256]{1,0:T(8,128)(2,1)}, bf16[2048,256]{1,0:T(8,128)(2,1)}, bf16[2048,256]{1,0:T(8,128)(2,1)}, bf16[2048,1024]{1,0:T(8,128)(2,1)}, bf16[1024,768]{1,0:T(8,128)(2,1)}) custom-call(s32[6]{0:T(128)} %stack.77.refs_0_, bf16[2048,16]{1,0:T(8,128)(2,1)} %bitcast.204, bf16[16,1024]{1,0:T(8,128)(2,1)} %reshape.510.refs_2_.refs_3_, ...), custom_call_target="tpu_custom_call" | custom-call | flops 3221225472 | bytes 12582912 | tf_op jit(solution)/shard_map/pallas_call | solution.py:300
  130.1 13.9 %collective-permute-done.10 = bf16[128,1024]{1,0:T(8,128)(2,1)S(1)} collective-permute-done((bf16[128,1024]{1,0:T(8,128)(2,1)S(1)}, bf16[128,1024]{1,0:T(8,128)(2,1)S(1)}, u32[]{:S(2)}, u32[]{:S(2)}) %collective-permute-start.10) | collective-permute-done | bytes 262176 | tf_op jit(solution)/shard_map/ppermute | solution.py:147
  144.1 14.4 %collective-permute-done.11 = bf16[128,1024]{1,0:T(8,128)(2,1)S(1)} collective-permute-done((bf16[128,1024]{1,0:T(8,128)(2,1)S(1)}, bf16[128,1024]{1,0:T(8,128)(2,1)S(1)}, u32[]{:S(2)}, u32[]{:S(2)}) %collective-permute-start.11) | collective-permute-done | bytes 262176 | tf_op jit(solution)/shard_map/ppermute | solution.py:147
  167.1 32.2 %shard_map.422 = (bf16[4,8,64,256]{3,2,1,0:T(8,128)(2,1)}, f32[8192,128]{1,0:T(8,128)}) custom-call(s32[2,8]{1,0:T(2,128)} %pad_add_fusion.refs_0_, bf16[2048,256]{1,0:T(8,128)(2,1)} %get-tuple-element.101.refs_1_, bf16[2048,256]{1,0:T(8,128)(2,1)} %get-tuple-element.102.refs_2_, bf16[2048,256]{1,0:T(8,128)(2,1)} %get-tuple-element.103.refs_3_), custom_call_target="tpu_custom_call" | custom-call | flops 9663676416 | bytes 10485760 | tf_op jit(solution)/shard_map/pallas_call | solution.py:300
  212.6 7.5 %collective-permute-done.14 = f32[2,8,1536]{2,1,0:T(8,128)S(1)} collective-permute-done((f32[2,8,1536]{2,1,0:T(8,128)S(1)}, f32[2,8,1536]{2,1,0:T(8,128)S(1)}, u32[]{:S(2)}, u32[]{:S(2)}) %collective-permute-start.14) | collective-permute-done | bytes 98336 | tf_op jit(solution)/shard_map/ppermute | solution.py:147
  227.9 14.1 %collective-permute-done.21.refs_2_ = bf16[4,128,1024]{2,1,0:T(8,128)(2,1)S(1)} collective-permute-done((bf16[4,128,1024]{2,1,0:T(8,128)(2,1)S(1)}, bf16[4,128,1024]{2,1,0:T(8,128)(2,1)S(1)}, u32[]{:S(2)}, u32[]{:S(2)}) %collective-permute-start.21) | collective-permute-done | bytes 1048608 | tf_op jit(solution)/shard_map/ppermute | solution.py:147
  263.8 10.3 %shard_map.427 = (f32[512,2048]{1,0:T(8,128)}, bf16[512,2048]{1,0:T(8,128)(2,1)}, bf16[512,1024]{1,0:T(8,128)(2,1)}) custom-call(bf16[512,1024]{1,0:T(8,128)(2,1)} %copy-done.54, bf16[1024,2048]{1,0:T(8,128)(2,1)} %get-tuple-element.111.refs_1_.refs_3_, bf16[2048,1024]{1,0:T(8,128)(2,1)} %shard_map.426.refs_2_.refs_1_), custom_call_target="tpu_custom_call" | custom-call | flops 4294967296 | bytes 16777216 | tf_op jit(solution)/shard_map/pallas_call | solution.py:300
  285.7 9.9 %shard_map.429 = (bf16[512,1024]{1,0:T(8,128)(2,1)}, f32[512,1024]{1,0:T(8,128)}, f32[8,3072]{1,0:T(8,128)}, f32[1024,16]{1,0:T(8,128)}, f32[8,128]{1,0:T(8,128)}) custom-call(f32[9]{0:T(128)} %pad_maximum_fusion.19.refs_0_, f32[512,1024]{1,0:T(8,128)} %get-tuple-element.114.refs_1_.refs_4_, f32[512,1024]{1,0:T(8,128)} %shard_map.428.refs_2_, ...), custom_call_target="tpu_custom_call" | custom-call | flops 67108864 | bytes 10485760 | tf_op jit(solution)/shard_map/pallas_call | solution.py:300
  296.1 8.0 %shard_map.430.refs_5_.refs_0_.refs_3_ = bf16[512,2048]{1,0:T(8,128)(2,1)} custom-call(bf16[512,1024]{1,0:T(8,128)(2,1)} %get-tuple-element.116.refs_0_.refs_3_, bf16[2048,1024]{1,0:T(8,128)(2,1)} %shard_map.426.refs_2_.refs_1_, f32[512,2048]{1,0:T(8,128)} %get-tuple-element.117.refs_2_), custom_call_target="tpu_custom_call" | custom-call | flops 2147483648 | bytes 10485760 | tf_op jit(solution)/shard_map/pallas_call | solution.py:300
  305.2 10.1 %shard_map.431 = (bf16[4,128,1024]{2,1,0:T(8,128)(2,1)}, bf16[4,128,1024]{2,1,0:T(8,128)(2,1)}, bf16[4,128,1024]{2,1,0:T(8,128)(2,1)}, bf16[4,128,1024]{2,1,0:T(8,128)(2,1)}) custom-call(s32[6]{0:T(128)} %stack.77.refs_0_, bf16[512,2048]{1,0:T(8,128)(2,1)} %get-tuple-element.112.refs_6_.refs_0_.refs_1_, bf16[512,2048]{1,0:T(8,128)(2,1)} %get-tuple-element.113.refs_2_, ...), custom_call_target="tpu_custom_call" | custom-call | flops 4294967296 | bytes 10485760 | tf_op jit(solution)/shard_map/pallas_call | solution.py:300
  318.8 11.7 %shard_map.432 = (bf16[512,2048]{1,0:T(8,128)(2,1)}, bf16[512,1024]{1,0:T(8,128)(2,1)}) custom-call(bf16[512,1024]{1,0:T(8,128)(2,1)} %copy-done.55, bf16[2048,1024]{1,0:T(8,128)(2,1)} %shard_map.426.refs_2_.refs_1_, f32[512,2048]{1,0:T(8,128)} %get-tuple-element.122.refs_2_, bf16[1024,2048]{1,0:T(8,128)(2,1)} %get-tuple-element.111.refs_1_.refs_3_, ...), custom_call_target="tpu_custom_call" | custom-call | flops 4294967296 | bytes 16777216 | tf_op jit(solution)/shard_map/pallas_call | solution.py:300
  341.3 11.2 %shard_map.434 = (bf16[4,512,256]{2,1,0:T(8,128)(2,1)}, bf16[1024,512]{1,0:T(8,128)(2,1)}, bf16[1024,512]{1,0:T(8,128)(2,1)}, f32[8,3072]{1,0:T(8,128)}, f32[16,1024]{1,0:T(8,128)}) custom-call(s32[6]{0:T(128)} %stack.77.refs_0_, f32[512,1024]{1,0:T(8,128)} %get-tuple-element.124.refs_1_, f32[512,1024]{1,0:T(8,128)} %shard_map.433.refs_2_, ...), custom_call_target="tpu_custom_call" | custom-call | flops 2147483648 | bytes 18874368 | tf_op jit(solution)/shard_map/pallas_call | solution.py:300
  354.5 12.9 %all-to-all-start.5 = ((bf16[4,512,256]{2,1,0:T(8,128)(2,1)}), bf16[4,512,256]{2,1,0:T(8,128)(2,1)}, u32[]{:S(2)}, u32[]{:S(2)}) async-start(bf16[4,512,256]{2,1,0:T(8,128)(2,1)} %get-tuple-element.137), calls=%async_computation.5 | async-start | bytes 2097152 | tf_op jit(solution)/shard_map/all_to_all | solution.py:1272
  371.3 10.2 %shard_map.435 = (bf16[4,64,2560]{2,1,0:T(8,128)(2,1)}, bf16[4,64,2560]{2,1,0:T(8,128)(2,1)}, bf16[4,64,2560]{2,1,0:T(8,128)(2,1)}, bf16[4,64,2560]{2,1,0:T(8,128)(2,1)}) custom-call(s32[6]{0:T(128)} %stack.77.refs_0_, bf16[512,1024]{1,0:T(8,128)(2,1)} %get-tuple-element.110.refs_0_.refs_1_, bf16[512,1024]{1,0:T(8,128)(2,1)} %copy-done.54, ...), custom_call_target="tpu_custom_call" | custom-call | flops 4294967296 | bytes 14680064 | tf_op jit(solution)/shard_map/pallas_call | solution.py:300
  396.4 57.5 %shard_map.438.refs_5_ = bf16[2048,768]{1,0:T(8,128)(2,1)} custom-call(s32[2,8]{1,0:T(2,128)} %pad_add_fusion.refs_0_, bf16[2048,256]{1,0:T(8,128)(2,1)} %get-tuple-element.101.refs_1_, bf16[2048,256]{1,0:T(8,128)(2,1)} %get-tuple-element.102.refs_2_, bf16[2048,256]{1,0:T(8,128)(2,1)} %get-tuple-element.103.refs_3_, ...), custom_call_target="tpu_custom_call" | custom-call | flops 24159191040 | bytes 12582912 | tf_op jit(solution)/shard_map/pallas_call | solution.py:300
  459.2 22.3 %shard_map.439 = (f32[8,2048]{1,0:T(8,128)}, f32[16,1024]{1,0:T(8,128)}, bf16[4,128,768]{2,1,0:T(8,128)(2,1)}, bf16[4,128,768]{2,1,0:T(8,128)(2,1)}) custom-call(s32[6]{0:T(128)} %stack.77.refs_0_, bf16[2048,16]{1,0:T(8,128)(2,1)} %bitcast.205, bf16[16,1024]{1,0:T(8,128)(2,1)} %reshape.510.refs_2_.refs_3_, f32[8,1024]{1,0:T(8,128)} %get-tuple-element.355.refs_4_.refs_3_, ...), custom_call_target="tpu_custom_call" | custom-call | flops 6442450944 | bytes 12582912 | tf_op jit(solution)/shard_map/pallas_call | solution.py:300
  489.5 12.2 %collective-permute-done.43 = bf16[4,128,768]{2,1,0:T(8,128)(2,1)S(1)} collective-permute-done((bf16[4,128,768]{2,1,0:T(8,128)(2,1)}, bf16[4,128,768]{2,1,0:T(8,128)(2,1)S(1)}, u32[]{:S(2)}, u32[]{:S(2)}) %collective-permute-start.43) | collective-permute-done | bytes 786464 | tf_op jit(solution)/shard_map/ppermute | solution.py:147
  513.3 14.8 %collective-permute-done.45 = bf16[128,768]{1,0:T(8,128)(2,1)S(1)} collective-permute-done((bf16[128,768]{1,0:T(8,128)(2,1)S(1)}, bf16[128,768]{1,0:T(8,128)(2,1)S(1)}, u32[]{:S(2)}, u32[]{:S(2)}) %collective-permute-start.45) | collective-permute-done | bytes 196640 | tf_op jit(solution)/shard_map/ppermute | solution.py:147
  547.3 8.8 %collective-permute-done.50 = f32[8,6144]{1,0:T(8,128)S(1)} collective-permute-done((f32[8,6144]{1,0:T(8,128)S(1)}, f32[8,6144]{1,0:T(8,128)S(1)}, u32[]{:S(2)}, u32[]{:S(2)}) %collective-permute-start.50) | collective-permute-done | bytes 196640 | tf_op jit(solution)/shard_map/ppermute | solution.py:147
  575.5 10.0 %all-to-all-done.8 = bf16[32,8,1536]{2,1,0:T(8,128)(2,1)S(1)} async-done(((bf16[32,8,1536]{2,1,0:T(8,128)(2,1)}), bf16[32,8,1536]{2,1,0:T(8,128)(2,1)S(1)}, u32[]{:S(2)}, u32[]{:S(2)}) %all-to-all-start.8) | async-done | bytes 786464 | tf_op jit(solution)/shard_map/all_to_all | solution.py:248
  596.8 10.6 %all_to_all.50 = f32[32,1,128]{2,1,0:T(1,128)S(1)} all-to-all(f32[32,1,128]{2,1,0:T(1,128)S(1)} %broadcast_in_dim.205), channel_id=1, replica_groups=mesh['clip'=8,'row'=4] {'clip','row'}, dimensions={0} | all-to-all | bytes 32768 | tf_op jit(solution)/shard_map/all_to_all | solution.py:248
  (406 shorter events, 248.8 us)
Async XLA Ops:
  35.2 46.8 %collective-permute-start.7 = (bf16[64,2560]{1,0:T(8,128)(2,1)S(1)}, bf16[64,2560]{1,0:T(8,128)(2,1)S(1)}, u32[]{:S(2)}, u32[]{:S(2)}) collective-permute-start(bf16[64,2560]{1,0:T(8,128)(2,1)S(1)} %get-tuple-element.344), channel_id=1, source_target_pairs={{0,8},{1,9},{2,10},{3,11},{4,12},{5,13},{6,14},{7,15},{8,0},{9,1},... | collective-permute-start | bytes 983048 | tf_op jit(solution)/shard_map/ppermute | solution.py:147
  36.9 45.0 %collective-permute-start.8 = (bf16[64,2560]{1,0:T(8,128)(2,1)S(1)}, bf16[64,2560]{1,0:T(8,128)(2,1)S(1)}, u32[]{:S(2)}, u32[]{:S(2)}) collective-permute-start(bf16[64,2560]{1,0:T(8,128)(2,1)S(1)} %get-tuple-element.344), channel_id=1, source_target_pairs={{0,16},{1,17},{2,18},{3,19},{4,20},{5,21},{6,22},{7,23},{8,24},{9,... | collective-permute-start | bytes 983048 | tf_op jit(solution)/shard_map/ppermute | solution.py:147
  41.3 37.4 %collective-permute-start.3 = (bf16[128,768]{1,0:T(8,128)(2,1)S(1)}, bf16[128,768]{1,0:T(8,128)(2,1)S(1)}, u32[]{:S(2)}, u32[]{:S(2)}) collective-permute-start(bf16[128,768]{1,0:T(8,128)(2,1)S(1)} %bitcast.198), channel_id=1, source_target_pairs={{0,16},{1,17},{2,18},{3,19},{4,20},{5,21},{6,22},{7,23},{8,24},{9,... | collective-permute-start | bytes 589832 | tf_op jit(solution)/shard_map/ppermute | solution.py:147
  41.6 37.1 %collective-permute-start.4 = (bf16[128,768]{1,0:T(8,128)(2,1)S(1)}, bf16[128,768]{1,0:T(8,128)(2,1)S(1)}, u32[]{:S(2)}, u32[]{:S(2)}) collective-permute-start(bf16[128,768]{1,0:T(8,128)(2,1)S(1)} %bitcast.199), channel_id=1, source_target_pairs={{0,24},{1,25},{2,26},{3,27},{4,28},{5,29},{6,30},{7,31},{8,16},{9,... | collective-permute-start | bytes 589832 | tf_op jit(solution)/shard_map/ppermute | solution.py:147
  114.7 52.2 %all-to-all-start.3 = ((bf16[32,8,1536]{2,1,0:T(8,128)(2,1)}), bf16[32,8,1536]{2,1,0:T(8,128)(2,1)S(1)}, u32[]{:S(2)}, u32[]{:S(2)}) async-start(bf16[32,8,1536]{2,1,0:T(8,128)(2,1)} %bitcast.40), calls=%async_computation.3 | async-start | bytes 1572864 | tf_op jit(solution)/shard_map/all_to_all | solution.py:1268
  120.5 39.5 %collective-permute-start.15 = (bf16[4,64,2560]{2,1,0:T(8,128)(2,1)S(1)}, bf16[4,64,2560]{2,1,0:T(8,128)(2,1)}, u32[]{:S(2)}, u32[]{:S(2)}) collective-permute-start(bf16[4,64,2560]{2,1,0:T(8,128)(2,1)S(1)} %copy-done.1), channel_id=1, source_target_pairs={{0,2},{1,3},{2,0},{3,1},{4,6},{5,7},{6,4},{7,5},{8,10},{9,11},{10,... | collective-permute-start | bytes 3932168 | tf_op jit(solution)/shard_map/ppermute | solution.py:147
  122.3 41.1 %collective-permute-start.16 = (bf16[4,64,2560]{2,1,0:T(8,128)(2,1)S(1)}, bf16[4,64,2560]{2,1,0:T(8,128)(2,1)}, u32[]{:S(2)}, u32[]{:S(2)}) collective-permute-start(bf16[4,64,2560]{2,1,0:T(8,128)(2,1)S(1)} %copy-done.1), channel_id=1, source_target_pairs={{0,4},{1,5},{2,6},{3,7},{4,0},{5,1},{6,2},{7,3},{8,12},{9,13},{10,... | collective-permute-start | bytes 3932168 | tf_op jit(solution)/shard_map/ppermute | solution.py:147
  126.6 31.8 %collective-permute-start.11 = (bf16[128,1024]{1,0:T(8,128)(2,1)S(1)}, bf16[128,1024]{1,0:T(8,128)(2,1)S(1)}, u32[]{:S(2)}, u32[]{:S(2)}) collective-permute-start(bf16[128,1024]{1,0:T(8,128)(2,1)S(1)} %convert_element_type.282), channel_id=1, source_target_pairs={{0,16},{1,17},{2,18},{3,19},{4,20},{5,21},{6,22},{7,23},{8,24},{9,... | collective-permute-start | bytes 786440 | tf_op jit(solution)/shard_map/ppermute | solution.py:147
  161.9 41.1 %collective-permute-start.17 = (bf16[2,64,2560]{2,1,0:T(8,128)(2,1)}, bf16[2,64,2560]{2,1,0:T(8,128)(2,1)}, u32[]{:S(2)}, u32[]{:S(2)}) collective-permute-start(bf16[2,64,2560]{2,1,0:T(8,128)(2,1)} %slice.201), channel_id=1, source_target_pairs={{0,4},{1,5},{2,6},{3,7},{4,0},{5,1},{6,2},{7,3},{8,12},{9,13},{10,... | collective-permute-start | bytes 1966088 | tf_op jit(solution)/shard_map/ppermute | solution.py:147
  165.4 37.7 %collective-permute-start.18 = (bf16[2,64,2560]{2,1,0:T(8,128)(2,1)}, bf16[2,64,2560]{2,1,0:T(8,128)(2,1)}, u32[]{:S(2)}, u32[]{:S(2)}) collective-permute-start(bf16[2,64,2560]{2,1,0:T(8,128)(2,1)} %slice.202), channel_id=1, source_target_pairs={{0,2},{1,3},{2,0},{3,1},{4,6},{5,7},{6,4},{7,5},{8,10},{9,11},{10,... | collective-permute-start | bytes 1966088 | tf_op jit(solution)/shard_map/ppermute | solution.py:147
  167.0 36.1 %collective-permute-start.13 = (f32[1,8,1536]{2,1,0:T(8,128)S(1)}, f32[1,8,1536]{2,1,0:T(8,128)S(1)}, u32[]{:S(2)}, u32[]{:S(2)}) collective-permute-start(f32[1,8,1536]{2,1,0:T(8,128)S(1)} %bitcast.223), channel_id=1, source_target_pairs={{0,1},{1,0},{2,3},{3,2},{4,5},{5,4},{6,7},{7,6},{8,9},{9,8},{10,11... | collective-permute-start | bytes 147464 | tf_op jit(solution)/shard_map/ppermute | solution.py:147
  212.2 29.8 %collective-permute-start.21 = (bf16[4,128,1024]{2,1,0:T(8,128)(2,1)S(1)}, bf16[4,128,1024]{2,1,0:T(8,128)(2,1)S(1)}, u32[]{:S(2)}, u32[]{:S(2)}) collective-permute-start(bf16[4,128,1024]{2,1,0:T(8,128)(2,1)S(1)} %pad_maximum_fusion.1.refs_1_), channel_id=1, source_target_pairs={{0,2},{1,3},{2,0},{3,1},{4,6},{5,7},{6,4},{7,5},{8,10},{9,11},{10,... | collective-permute-start | bytes 3145736 | tf_op jit(solution)/shard_map/ppermute | solution.py:147
  212.6 29.6 %collective-permute-start.22 = (bf16[4,128,1024]{2,1,0:T(8,128)(2,1)S(1)}, bf16[4,128,1024]{2,1,0:T(8,128)(2,1)}, u32[]{:S(2)}, u32[]{:S(2)}) collective-permute-start(bf16[4,128,1024]{2,1,0:T(8,128)(2,1)S(1)} %pad_maximum_fusion.1.refs_1_), channel_id=1, source_target_pairs={{0,4},{1,5},{2,6},{3,7},{4,0},{5,1},{6,2},{7,3},{8,12},{9,13},{10,... | collective-permute-start | bytes 3145736 | tf_op jit(solution)/shard_map/ppermute | solution.py:147
  227.9 34.9 %collective-permute-start.20 = (bf16[512,1024]{1,0:T(8,128)(2,1)}, bf16[512,1024]{1,0:T(8,128)(2,1)S(1)}, u32[]{:S(2)}, u32[]{:S(2)}) collective-permute-start(bf16[512,1024]{1,0:T(8,128)(2,1)} %get-tuple-element.110.refs_0_.refs_1_), channel_id=1, source_target_pairs={{0,1},{1,0},{2,3},{3,2},{4,5},{5,4},{6,7},{7,6},{8,9},{9,8},{10,11... | collective-permute-start | bytes 3145736 | tf_op jit(solution)/shard_map/ppermute | solution.py:147
  330.9 36.5 %collective-permute-start.28 = (bf16[4,128,1024]{2,1,0:T(8,128)(2,1)S(1)}, bf16[4,128,1024]{2,1,0:T(8,128)(2,1)}, u32[]{:S(2)}, u32[]{:S(2)}) collective-permute-start(bf16[4,128,1024]{2,1,0:T(8,128)(2,1)S(1)} %pad_maximum_fusion.2), channel_id=1, source_target_pairs={{0,2},{1,3},{2,0},{3,1},{4,6},{5,7},{6,4},{7,5},{8,10},{9,11},{10,... | collective-permute-start | bytes 3145736 | tf_op jit(solution)/shard_map/ppermute | solution.py:147
  332.6 34.7 %collective-permute-start.30 = (bf16[4,128,1024]{2,1,0:T(8,128)(2,1)S(1)}, bf16[4,128,1024]{2,1,0:T(8,128)(2,1)}, u32[]{:S(2)}, u32[]{:S(2)}) collective-permute-start(bf16[4,128,1024]{2,1,0:T(8,128)(2,1)S(1)} %pad_maximum_fusion.3), channel_id=1, source_target_pairs={{0,4},{1,5},{2,6},{3,7},{4,0},{5,1},{6,2},{7,3},{8,12},{9,13},{10,... | collective-permute-start | bytes 3145736 | tf_op jit(solution)/shard_map/ppermute | solution.py:147
  354.5 42.0 %all-to-all-start.5 = ((bf16[4,512,256]{2,1,0:T(8,128)(2,1)}), bf16[4,512,256]{2,1,0:T(8,128)(2,1)}, u32[]{:S(2)}, u32[]{:S(2)}) async-start(bf16[4,512,256]{2,1,0:T(8,128)(2,1)} %get-tuple-element.137), calls=%async_computation.5 | async-start | bytes 2097152 | tf_op jit(solution)/shard_map/all_to_all | solution.py:1272
  382.3 73.9 %collective-permute-start.36 = (bf16[4,64,2560]{2,1,0:T(8,128)(2,1)}, bf16[4,64,2560]{2,1,0:T(8,128)(2,1)S(1)}, u32[]{:S(2)}, u32[]{:S(2)}) collective-permute-start(bf16[4,64,2560]{2,1,0:T(8,128)(2,1)} %get-tuple-element.132), channel_id=1, source_target_pairs={{0,2},{1,3},{2,0},{3,1},{4,6},{5,7},{6,4},{7,5},{8,10},{9,11},{10,... | collective-permute-start | bytes 3932168 | tf_op jit(solution)/shard_map/ppermute | solution.py:147
  384.1 72.1 %collective-permute-start.37 = (bf16[4,64,2560]{2,1,0:T(8,128)(2,1)}, bf16[4,64,2560]{2,1,0:T(8,128)(2,1)S(1)}, u32[]{:S(2)}, u32[]{:S(2)}) collective-permute-start(bf16[4,64,2560]{2,1,0:T(8,128)(2,1)} %get-tuple-element.133), channel_id=1, source_target_pairs={{0,4},{1,5},{2,6},{3,7},{4,0},{5,1},{6,2},{7,3},{8,12},{9,13},{10,... | collective-permute-start | bytes 3932168 | tf_op jit(solution)/shard_map/ppermute | solution.py:147
  385.5 70.7 %collective-permute-start.38 = (bf16[4,64,2560]{2,1,0:T(8,128)(2,1)}, bf16[4,64,2560]{2,1,0:T(8,128)(2,1)}, u32[]{:S(2)}, u32[]{:S(2)}) collective-permute-start(bf16[4,64,2560]{2,1,0:T(8,128)(2,1)} %get-tuple-element.134), channel_id=1, source_target_pairs={{0,6},{1,7},{2,4},{3,5},{4,2},{5,3},{6,0},{7,1},{8,14},{9,15},{10,... | collective-permute-start | bytes 3932168 | tf_op jit(solution)/shard_map/ppermute | solution.py:147
  385.9 68.1 %collective-permute-start.34 = (bf16[128,1024]{1,0:T(8,128)(2,1)}, bf16[128,1024]{1,0:T(8,128)(2,1)}, u32[]{:S(2)}, u32[]{:S(2)}) collective-permute-start(bf16[128,1024]{1,0:T(8,128)(2,1)} %get-tuple-element.333), channel_id=1, source_target_pairs={{0,16},{1,17},{2,18},{3,19},{4,20},{5,21},{6,22},{7,23},{8,24},{9,... | collective-permute-start | bytes 786440 | tf_op jit(solution)/shard_map/ppermute | solution.py:147
  391.6 62.4 %collective-permute-start.35 = (bf16[128,1024]{1,0:T(8,128)(2,1)S(1)}, bf16[128,1024]{1,0:T(8,128)(2,1)}, u32[]{:S(2)}, u32[]{:S(2)}) collective-permute-start(bf16[128,1024]{1,0:T(8,128)(2,1)S(1)} %get-tuple-element.332), channel_id=1, source_target_pairs={{0,24},{1,25},{2,26},{3,27},{4,28},{5,29},{6,30},{7,31},{8,16},{9,... | collective-permute-start | bytes 786440 | tf_op jit(solution)/shard_map/ppermute | solution.py:147
  454.0 90.5 %collective-permute-start.49 = (f32[8,6144]{1,0:T(8,128)S(1)}, f32[8,6144]{1,0:T(8,128)}, u32[]{:S(2)}, u32[]{:S(2)}) collective-permute-start(f32[8,6144]{1,0:T(8,128)S(1)} %constant_dynamic-update-slice_fusion), channel_id=1, source_target_pairs={{0,1},{1,0},{2,3},{3,2},{4,5},{5,4},{6,7},{7,6},{8,9},{9,8},{10,11... | collective-permute-start | bytes 589832 | tf_op jit(solution)/shard_map/ppermute | solution.py:147
  501.7 30.5 %collective-permute-start.48 = (f32[8,2048]{1,0:T(8,128)}, f32[8,2048]{1,0:T(8,128)}, u32[]{:S(2)}, u32[]{:S(2)}) collective-permute-start(f32[8,2048]{1,0:T(8,128)} %add.226), channel_id=1, source_target_pairs={{0,2},{1,3},{2,0},{3,1},{4,6},{5,7},{6,4},{7,5},{8,10},{9,11},{10,... | collective-permute-start | bytes 196616 | tf_op jit(solution)/shard_map/ppermute | solution.py:147
  (96 other events, 1188.8 us)

commit v2 on v1

--- a/solution.py
+++ b/solution.py
@@ -152,65 +152,120 @@
     return {m: m << bits[number] for m in range(1, sizes[number])}
 
 
-def chip_gather(shard, use_y=True, hold=None, hold_x=None):
-    z_masks, x_masks = along(2), along(1)
-    y_masks = along(0) if use_y else {}
-    got = [exchange(shard, mask) for mask in z_masks.values()]
-    own = jnp.stack([shard] + got)
-    if hold is not None:
-        own = tie(own, hold)
-    pieces = [(own, 0, 0, 0)]
-    at_y = {m: exchange(own, mask) for m, mask in y_masks.items()}
-    sent = own if hold_x is None else tie(own, hold_x)
-    at_x = {m: exchange(sent, mask) for m, mask in x_masks.items()}
-    pieces += [(array, m, 0, 0) for m, array in at_y.items()]
-    pieces += [(array, 0, m, 0) for m, array in at_x.items()]
-    half = own.shape[0] // 2
-    for my in at_y:
-        for mx in at_x:
-            pieces.append((exchange(at_y[my][:half], x_masks[mx]), my, mx, 0))
-            pieces.append((exchange(at_x[mx][half:], y_masks[my]), my, mx, half))
-    return pieces
-
-
-def chip_scatter(groups, use_y=True, direct=False, hold=None):
-    z_masks, x_masks = along(2), along(1)
-    y_masks = along(0) if use_y else {}
-    half = groups[0, 0].shape[0] // 2
-    at_y = {m: [[], []] for m in y_masks}
-    at_x = {m: [[], []] for m in x_masks}
-    slant = []
-    for my in y_masks:
-        for mx in x_masks:
-            piece = groups[my, mx]
-            if direct:
-                slant.append((piece, y_masks[my] ^ x_masks[mx]))
-                continue
-            at_y[my][0].append(exchange(piece[:half], x_masks[mx]))
-            at_x[mx][1].append(exchange(piece[half:], y_masks[my]))
-
-    def total(piece, terms):
-        if not terms:
-            return piece
-        result = piece.astype(f32)
-        for term in terms:
-            result = result + term.astype(f32)
-        return to_low(result)
-
-    def joined(piece, terms):
-        if not (terms[0] or terms[1]):
-            return piece
-        return jnp.concatenate([total(piece[:half], terms[0]), total(piece[half:], terms[1])])
-
-    sent = [(joined(groups[m, 0], at_y[m]), mask) for m, mask in y_masks.items()]
-    sent += [(joined(groups[0, m], at_x[m]), mask) for m, mask in x_masks.items()]
-    own = total(groups[0, 0], [exchange(piece, mask) for piece, mask in sent + slant])
-    if hold is not None:
-        own = tie(own, hold)
-    result = own[0].astype(f32)
-    for m, mask in z_masks.items():
-        result = result + exchange(own[m], mask).astype(f32)
-    return result, tuple(piece for piece, mask in sent), own
+class Gather:
+    def __init__(self, shard, use_y=True):
+        self.shard = shard
+        self.z_masks, self.x_masks = along(2), along(1)
+        self.y_masks = along(0) if use_y else {}
+
+    def go_z(self, *hold):
+        came = [exchange(self.shard, mask) for mask in self.z_masks.values()]
+        self.own = jnp.stack([self.shard] + came)
+        if hold:
+            self.own = tie(self.own, *hold)
+
+    def go_direct(self):
+        self.go_xy()
+        self.slant = [
+            (exchange(self.own, y_mask ^ x_mask), my, mx, 0)
+            for my, y_mask in self.y_masks.items()
+            for mx, x_mask in self.x_masks.items()
+        ]
+
+    def go_xy(self, hold_x=()):
+        self.at_y = {m: exchange(self.own, mask) for m, mask in self.y_masks.items()}
+        sent = tie(self.own, *hold_x) if hold_x else self.own
+        self.at_x = {m: exchange(sent, mask) for m, mask in self.x_masks.items()}
+
+    def came_xy(self):
+        return tuple(self.at_y.values()) + tuple(self.at_x.values())
+
+    def go_slant(self, *hold):
+        at_y, at_x = self.at_y, self.at_x
+        if hold:
+            at_y = {m: tie(array, *hold) for m, array in at_y.items()}
+            at_x = {m: tie(array, *hold) for m, array in at_x.items()}
+        half = self.own.shape[0] // 2
+        self.slant = []
+        for my in at_y:
+            for mx in at_x:
+                self.slant.append((exchange(at_y[my][:half], self.x_masks[mx]), my, mx, 0))
+                self.slant.append((exchange(at_x[mx][half:], self.y_masks[my]), my, mx, half))
+
+    def pieces(self):
+        pieces = [(self.own, 0, 0, 0)]
+        pieces += [(array, m, 0, 0) for m, array in self.at_y.items()]
+        pieces += [(array, 0, m, 0) for m, array in self.at_x.items()]
+        return pieces + self.slant
+
+
+class Scatter:
+    def __init__(self, groups, *hold):
+        self.groups = groups
+        self.z_masks, self.x_masks, self.y_masks = along(2), along(1), along(0)
+        half = groups[0, 0].shape[0] // 2
+        at_y = {m: [[], []] for m in self.y_masks}
+        at_x = {m: [[], []] for m in self.x_masks}
+        for my in self.y_masks:
+            for mx in self.x_masks:
+                piece = groups[my, mx]
+                one = exchange(piece[:half], self.x_masks[mx])
+                two = exchange(piece[half:], self.y_masks[my])
+                if hold:
+                    one, two = tie(one, *hold), tie(two, *hold)
+                at_y[my][0].append(one)
+                at_x[mx][1].append(two)
+
+        def joined(piece, terms):
+            if not (terms[0] or terms[1]):
+                return piece
+            parts = total(piece[:half], terms[0]), total(piece[half:], terms[1])
+            return jnp.concatenate(parts)
+
+        self.sent = {(m, 0): joined(groups[m, 0], at_y[m]) for m in self.y_masks}
+        self.sent.update({(0, m): joined(groups[0, m], at_x[m]) for m in self.x_masks})
+
+    def go_xy(self, extra=None, *hold):
+        masks = {(m, 0): mask for m, mask in self.y_masks.items()}
+        masks.update({(0, m): mask for m, mask in self.x_masks.items()})
+        sent, self.extra, slant = dict(self.sent), extra, []
+        if extra is not None:
+            sent = {g: jnp.concatenate([piece, extra[g]], axis=2) for g, piece in sent.items()}
+            slant = [(extra[my, mx], self.y_masks[my] ^ self.x_masks[mx])
+                     for my in self.y_masks for mx in self.x_masks]
+        if hold:
+            sent = {g: tie(piece, *hold) for g, piece in sent.items()}
+        self.came = [exchange(piece, masks[g]) for g, piece in sent.items()]
+        self.came_slant = [exchange(piece, mask) for piece, mask in slant]
+
+    def go_z(self, *hold):
+        came = list(self.came)
+        if hold:
+            came = [tie(array, *hold) for array in came]
+        width = self.groups[0, 0].shape[2]
+        self.own = total(self.groups[0, 0], [array[:, :, :width] for array in came])
+        if self.extra is not None:
+            terms = [array[:, :, width:] for array in came] + self.came_slant
+            self.own = jnp.concatenate([self.own, total(self.extra[0, 0], terms)], axis=2)
+        self.came_z = [exchange(self.own[m], mask) for m, mask in self.z_masks.items()]
+
+    def result(self, *hold):
+        came = list(self.came_z)
+        if hold:
+            came = [tie(array, *hold) for array in came]
+        value = self.own[0].astype(f32)
+        for array in came:
+            value = value + array.astype(f32)
+        return value
+
+
+def total(piece, terms):
+    if not terms:
+        return piece
+    value = piece.astype(f32)
+    for term in terms:
+        value = value + term.astype(f32)
+    return to_low(value)
 
 
 def tie(values, *others):
@@ -221,10 +276,10 @@
     return [1 << bit for bit in range(lax.axis_size("row").bit_length() - 1)]
 
 
-def row_sum(values):
+def row_sum(values, *hold):
     for mask in row_masks():
-        values = values + exchange(values, mask)
-    return values
+        values = values + exchange(to_low(values), mask).astype(f32)
+    return tie(values, *hold) if hold else values
 
 
 def row_gather(values):
@@ -237,6 +292,20 @@
             [jnp.where(first, values, other), jnp.where(first, other, values)], axis=0
         )
     return values
+
+
+def row_swap(values):
+    place = lax.axis_index("row")
+    steps = len(row_masks())
+    values = values.reshape((2,) * steps + values.shape[1:])
+    for step, mask in enumerate(row_masks()):
+        axis = steps - 1 - step
+        mine = (place >> step) & 1
+        keep = lax.dynamic_index_in_dim(values, mine, axis, keepdims=False)
+        got = exchange(lax.dynamic_index_in_dim(values, 1 - mine, axis, keepdims=False), mask)
+        low, high = jnp.where(mine == 0, keep, got), jnp.where(mine == 0, got, keep)
+        values = jnp.stack([low, high], axis=axis)
+    return values.reshape((-1,) + values.shape[steps:])
 
 
 def spread(values, axes):
@@ -304,6 +373,14 @@
     return (PER_FRAME, columns), lambda f: (f, 0)
 
 
+def frame_lines(ref, first, count, per_frame):
+    lines = [
+        jnp.broadcast_to(ref[pl.ds(first + k, 1), :], (per_frame, ref.shape[1]))
+        for k in range(count)
+    ]
+    return jnp.concatenate(lines, axis=0)
+
+
 def head_mask(width, head, rotary):
     lane = lax.broadcasted_iota(jnp.int32, (1, width), 1)
     if rotary:
@@ -353,82 +430,113 @@
     )
 
 
-def run_qkv(coords, noisy, embed, shift, scale, cosine, sine, pieces, after=()):
+def run_qkv_attend(coords, span, noisy, embed, shift, scale, cosine, sine, pieces, ranks, after=()):
     rows, columns = pieces[0][0].shape[1:]
     width = columns // 3
-    half = width // 2
-
-    def kernel(coords_ref, noisy_ref, embed_ref, shift_ref, scale_ref, cos_ref, sin_ref, *refs):
+    half, heads, per_frame = width // 2, width // HD, PER_FRAME // ranks
+    count = 2
+    block, steps = count * PER_FRAME, FRAMES // count
+    stack = heads * PER_FRAME
+    base = coords.shape[0]
+
+    def kernel(number_ref, noisy_ref, embed_ref, shift_ref, scale_ref, cos_ref, sin_ref, *refs):
         sources = refs[: len(pieces)]
-        q_ref, k_ref, v_ref, in_ref, w_ref, sems = refs[len(pieces) :]
-        frame = pl.program_id(0)
+        q_ref, k_ref, v_ref, in_ref, w_ref, o_ref, lse_ref, sems, *scratch = refs[len(pieces) :]
+        step = pl.program_id(0)
 
         def copies():
             made = []
             for source, (array, my, mx, first) in zip(sources, pieces):
                 for k in range(array.shape[0]):
-                    place = (coords_ref[2] ^ (first + k)) * coords_ref[5] + (coords_ref[1] ^ mx)
+                    place = (number_ref[2] ^ (first + k)) * number_ref[5] + (number_ref[1] ^ mx)
                     spot = pl.ds(pl.multiple_of(place * rows, rows), rows)
                     made.append(
                         pltpu.make_async_copy(source.at[k], w_ref.at[spot, :], sems.at[len(made)])
                     )
             return made
 
-        @pl.when(frame == 0)
+        @pl.when(step == 0)
         def start():
             for copy in copies():
                 copy.start()
 
-        hidden = mm(noisy_ref[...], embed_ref[...], 1, 0)
-        normed, unused = norm_parts(hidden)
-        spot = pl.ds(frame, 1)
-        attn_in = to_low(normed * (1.0 + scale_ref[spot, :]) + shift_ref[spot, :])
-        in_ref[...] = attn_in
-
-        @pl.when(frame == 0)
-        def finish():
-            for copy in copies():
-                copy.wait()
-
-        out = mm(attn_in, w_ref[...], 1, 0)
-        cos, sin = cos_ref[...], sin_ref[...]
-        for ref, base, factor in ((q_ref, 0, HD**-0.5), (k_ref, width, 1.0)):
-            lower = out[:, base : base + half]
-            upper = out[:, base + half : base + width]
-            ref[:, :half] = to_low(lower * cos - upper * sin) * factor
-            ref[:, half:] = to_low(upper * cos + lower * sin) * factor
-        v_ref[...] = to_low(out[:, 2 * width :])
-
+        @pl.when(step < steps)
+        def project():
+            normed, unused = norm_parts(mm(noisy_ref[...], embed_ref[...], 1, 0))
+            scale = frame_lines(scale_ref, step * count, count, PER_FRAME)
+            shift = frame_lines(shift_ref, step * count, count, PER_FRAME)
+            attn_in = to_low(normed * (1.0 + scale) + shift)
+            in_ref[...] = attn_in
+
+            @pl.when(step == 0)
+            def finish():
+                for copy in copies():
+                    copy.wait()
+
+            out = mm(attn_in, w_ref[...], 1, 0)
+            cos, sin = cos_ref[...], sin_ref[...]
+            spot = pl.ds(step * block, block)
+            for ref, first, factor in ((q_ref, 0, HD**-0.5), (k_ref, width, 1.0)):
+                lower = out[:, first : first + half]
+                upper = out[:, first + half : first + width]
+                ref[spot, :half] = to_low(lower * cos - upper * sin) * factor
+                ref[spot, half:] = to_low(upper * cos + lower * sin) * factor
+            v_ref[spot, :] = to_low(out[:, 2 * width :])
+
+        @pl.when(step >= steps)
+        def attend():
+            frame = step - steps
+            first, last = number_ref[base + frame], number_ref[base + FRAMES + frame]
+            attend_frame(frame, first, last, q_ref, k_ref, v_ref, o_ref, lse_ref, *scratch)
+
+    lines = lambda wide: ((block, wide), lambda i: (jnp.minimum(i, steps - 1), 0))
+    at_frame = lambda i: jnp.maximum(i - steps, 0)
     chips = sum(piece[0].shape[0] for piece in pieces)
     return run_kernel(
         kernel,
-        (FRAMES,),
-        [
-            (noisy, *frame_rows(PD)),
+        (steps + FRAMES,),
+        [
+            (noisy, *lines(PD)),
             (embed,),
             (shift,),
             (scale,),
-            (cosine, *frame_rows(half)),
-            (sine, *frame_rows(half)),
+            (cosine, *lines(half)),
+            (sine, *lines(half)),
         ]
         + [(piece[0], pl.ANY) for piece in pieces],
-        [((TOK, width), bf16, *frame_rows(width))] * 3
-        + [((TOK, D), bf16, *frame_rows(D)), ((D, columns), bf16)],
-        [pltpu.SemaphoreType.DMA((chips,))],
-        coords,
+        [((TOK, width), bf16)] * 3
+        + [
+            ((TOK, D), bf16, *lines(D)),
+            ((D, columns), bf16),
+            (
+                (ranks, FRAMES, per_frame, width),
+                bf16,
+                (ranks, 1, per_frame, width),
+                lambda i: (0, at_frame(i), 0, 0),
+            ),
+            ((FRAMES * stack, 128), f32, (stack, 128), lambda i: (at_frame(i), 0)),
+        ],
+        [
+            pltpu.SemaphoreType.DMA((chips,)),
+            pltpu.VMEM((stack, width), bf16),
+            pltpu.VMEM((FRAMES, stack, PER_FRAME), f32),
+            pltpu.VMEM((stack, 128), f32),
+            pltpu.VMEM((stack, 128), f32),
+            pltpu.VMEM((stack, width), f32),
+        ],
+        jnp.concatenate([coords, span.reshape(-1)]),
         after,
-        flops=2 * TOK * D * columns,
-        moved=12 * 2**20,
-    )
-
-
-def attend_kernel(span_ref, q_ref, k_ref, v_ref, o_ref, lse_ref, q_scr, s_scr, m_scr, l_scr, acc_scr):
-    frame = pl.program_id(0)
+        flops=2 * TOK * D * columns + 4 * 36 * PER_FRAME * PER_FRAME * 256 * heads,
+        moved=20 * 2**20,
+        exps=36 * PER_FRAME * PER_FRAME * heads,
+    )
+
+
+def attend_frame(frame, start, stop, q_ref, k_ref, v_ref, o_ref, lse_ref, q_scr, s_scr, m_scr, l_scr, acc_scr):
     width = q_ref.shape[1]
     heads = width // HD
     block = PER_FRAME
-    start, stop = span_ref[0, frame], span_ref[1, frame]
-    query = q_ref[...]
+    query = q_ref[pl.ds(frame * block, block), :]
     for head in range(heads):
         q_scr[head * block : (head + 1) * block, :] = jnp.where(
             head_mask(width, head, True), query, jnp.zeros_like(query)
@@ -474,34 +582,6 @@
         lse_ref[rows, :] = m_scr[rows, :] + jnp.log(total)
         result = jnp.where(head_mask(width, head, False), acc_scr[rows, :] / total, result)
     o_ref[...] = to_low(result).reshape(o_ref.shape)
-
-
-def run_attend(span, query, keys, values, rows, after=()):
-    width = query.shape[1]
-    heads = width // HD
-    block = PER_FRAME
-    per_frame = block // rows
-    return run_kernel(
-        attend_kernel,
-        (FRAMES,),
-        [(query, *frame_rows(width)), (keys,), (values,)],
-        [
-            ((rows, FRAMES, per_frame, width), bf16, (rows, 1, per_frame, width), lambda f: (0, f, 0, 0)),
-            ((FRAMES * heads * block, 128), f32, (heads * block, 128), lambda f: (f, 0)),
-        ],
-        [
-            pltpu.VMEM((heads * block, width), bf16),
-            pltpu.VMEM((FRAMES, heads * block, block), f32),
-            pltpu.VMEM((heads * block, 128), f32),
-            pltpu.VMEM((heads * block, 128), f32),
-            pltpu.VMEM((heads * block, width), f32),
-        ],
-        span,
-        after,
-        flops=2 * 2 * 36 * block * block * 256 * heads,
-        moved=10 * 2**20,
-        exps=36 * block * block * heads,
-    )
 
 
 def attend_back_kernel(
@@ -545,7 +625,7 @@
                 weight = jnp.exp(score[:, lanes] - lse)
                 p_scr[rows, lanes] = to_low(weight)
                 s_scr[rows, lanes] = to_low(weight * (grad_w[:, lanes] - inner))
-            dq_scr[rows, :] = dq_scr[rows, :] + mm(s_scr[rows, :], keys, 1, 0)
+        dq_scr[...] = dq_scr[...] + mm(s_scr[...], keys, 1, 0)
         dk_scr[spot, :] = dk_scr[spot, :] + mm(s_scr[...], q_scr[...], 0, 0)
         dv_scr[spot, :] = dv_scr[spot, :] + mm(p_scr[...], g_scr[...], 0, 0)
         return carry
@@ -612,50 +692,63 @@
     )[0]
 
 
-def run_qkv_back(coords, noisy, embed, scale, attn_in, grad, weight, nx, nz, after=()):
+def run_qkv_dw(attn_in, grad, after=()):
+    columns = grad.shape[1]
+    count = 2
+    block, steps = count * PER_FRAME, FRAMES // count
+
+    def kernel(in_ref, g_ref, out_ref, acc):
+        step = pl.program_id(0)
+        accumulate(acc, step, lambda: mm(in_ref[...], g_ref[...], 0, 0))
+
+        @pl.when(step == steps - 1)
+        def finish():
+            out_ref[...] = to_low(acc[...])
+
+    return run_kernel(
+        kernel,
+        (steps,),
+        [
+            (attn_in, (block, D), lambda i: (i, 0)),
+            (grad, (block, columns), lambda i: (i, 0)),
+        ],
+        [((D, columns), bf16)],
+        [pltpu.VMEM((D, columns), f32)],
+        after=after,
+        flops=2 * TOK * D * columns,
+        moved=10 * 2**20,
+    )[0]
+
+
+def run_qkv_back(noisy, embed, scale, grad, weight, after=()):
     columns = weight.shape[1]
-    rows = D // (nx * nz)
-
-    def kernel(coords_ref, noisy_ref, embed_ref, scale_ref, in_ref, g_ref, w_ref, sum_ref, ge_ref, *refs):
-        outs, acc = refs[:nx], refs[nx]
+
+    def kernel(noisy_ref, embed_ref, scale_ref, g_ref, w_ref, sum_ref, ge_ref):
         frame = pl.program_id(0)
-        noisy, grad = noisy_ref[...], g_ref[...]
-        accumulate(acc, frame, mm(in_ref[...], grad, 0, 0))
+        noisy = noisy_ref[...]
         normed, inverse = norm_parts(mm(noisy, embed_ref[...], 1, 0))
-        grad_in = mm(grad, w_ref[...], 1, 1)
+        grad_in = mm(g_ref[...], w_ref[...], 1, 1)
         spot = pl.ds(frame, 1)
         sum_ref[spot, :D] = jnp.sum(grad_in, axis=0, keepdims=True)
         sum_ref[spot, D:] = jnp.sum(grad_in * normed, axis=0, keepdims=True)
         grad_h = norm_back(normed, inverse, grad_in * (1.0 + scale_ref[spot, :]))
-        accumulate(ge_ref, frame, mm(noisy, to_low(grad_h), 0, 0))
-
-        @pl.when(frame == FRAMES - 1)
-        def finish():
-            for mx in range(nx):
-                for mz in range(nz):
-                    place = (coords_ref[2] ^ mz) * coords_ref[5] + (coords_ref[1] ^ mx)
-                    where = pl.ds(pl.multiple_of(place * rows, rows), rows)
-                    outs[mx][mz] = to_low(acc[where, :])
-
-    outs = run_kernel(
+        accumulate(ge_ref, frame, lambda: mm(noisy, to_low(grad_h), 0, 0))
+
+    return run_kernel(
         kernel,
         (FRAMES,),
         [
             (noisy, *frame_rows(PD)),
             (embed,),
             (scale,),
-            (attn_in, *frame_rows(D)),
             (grad, *frame_rows(columns)),
             (weight,),
         ],
-        [((FRAMES, 2 * D), f32), ((PD, D), f32)] + [((nz, rows, columns), bf16)] * nx,
-        [pltpu.VMEM((D, columns), f32)],
-        coords,
-        after,
-        flops=4 * TOK * D * columns,
-        moved=12 * 2**20,
-    )
-    return outs[0], outs[1], {(0, mx): out for mx, out in enumerate(outs[2:])}
+        [((FRAMES, 2 * D), f32), ((PD, D), f32)],
+        after=after,
+        flops=2 * TOK * D * columns,
+        moved=8 * 2**20,
+    )
 
 
 REST = {
@@ -764,21 +857,35 @@
     )
 
 
-def run_up_down(mlp_in, up, down, after=()):
+def parts_of(tokens):
+    size = tokens // 2
+    return [slice(k * size, (k + 1) * size) for k in range(2)]
+
+
+def run_up_down(mlp_in, up, down, dtype, after=()):
     tokens, hidden = mlp_in.shape[0], up.shape[1]
     steps = hidden // CHUNK
 
     def kernel(in_ref, up_ref, down_ref, out_ref, act_ref, part_ref, acc):
         j = pl.program_id(0)
-        out = mm(in_ref[...], up_ref[...], 1, 0)
-        out_ref[...] = out
-        act = to_low(gelu_value(out))
-        act_ref[...] = act
-        accumulate(acc, j, mm(act, down_ref[...], 1, 0))
+
+        @pl.when(j == 0)
+        def clear():
+            acc[...] = jnp.zeros_like(acc)
+
+        spans = parts_of(tokens)
+        ready = mm(in_ref[spans[0], :], up_ref[...], 1, 0)
+        for k, span in enumerate(spans):
+            out = ready
+            if k + 1 < len(spans):
+                ready = mm(in_ref[spans[k + 1], :], up_ref[...], 1, 0)
+            out_ref[span, :] = out
+            act_ref[span, :] = to_low(gelu_value(out))
+        acc[...] = acc[...] + mm(act_ref[...], down_ref[...], 1, 0)
 
         @pl.when(j == steps - 1)
         def finish():
-            part_ref[...] = to_low(acc[...])
+            part_ref[...] = acc[...].astype(part_ref.dtype)
 
     part = (tokens, CHUNK), lambda j: (0, j)
     return run_kernel(
@@ -788,7 +895,7 @@
         [
             ((tokens, hidden), f32, *part),
             ((tokens, hidden), bf16, *part),
-            ((tokens, D), bf16),
+            ((tokens, D), dtype),
         ],
         [pltpu.VMEM((tokens, D), f32)],
         after=after,
@@ -800,18 +907,16 @@
 def accumulate(acc, step, term):
     @pl.when(step == 0)
     def first():
-        acc[...] = term
-
-    @pl.when(step > 0)
-    def more():
-        acc[...] = acc[...] + term
+        acc[...] = jnp.zeros_like(acc)
+
+    acc[...] = acc[...] + term()
 
 
 def run_down(act, down, after=()):
     tokens, hidden = act.shape
 
     def kernel(act_ref, down_ref, out_ref):
-        accumulate(out_ref, pl.program_id(0), mm(act_ref[...], down_ref[...], 1, 0))
+        accumulate(out_ref, pl.program_id(0), lambda: mm(act_ref[...], down_ref[...], 1, 0))
 
     return run_kernel(
         kernel,
@@ -826,43 +931,46 @@
 
 def run_head(flags, hidden1, part, got, rest, head, target, after=()):
     tokens = hidden1.shape[0]
-    per_frame = tokens // FRAMES
+    per_frame, count = tokens // FRAMES, 2
+    block = count * per_frame
 
     def kernel(
         flag_ref, h_ref, p_ref, got_ref, rest_ref, head_ref, t_ref,
         gd_ref, gh_ref, sum_ref, ghead_ref, loss_ref,
     ):
-        frame = pl.program_id(0)
-
-        @pl.when(frame == 0)
+        first = pl.program_id(0) * count
+
+        @pl.when(first == 0)
         def clear():
             ghead_ref[...] = jnp.zeros_like(ghead_ref)
 
-        mod = lambda name: rest_ref[pl.ds(frame, 1), REST[name]]
+        mod = lambda name: by_frame(rest_ref, name, first, count, per_frame)
+        frame_of = lax.broadcasted_iota(jnp.int32, (block, 1), 0) // per_frame
+        true = jnp.where(frame_of == 0, flag_ref[first], flag_ref[first + 1])
         down_out = p_ref[...] + got_ref[...].astype(f32)
         hidden = h_ref[...] + mod("gate_m") * down_out
         normed, inverse = norm_parts(hidden)
         scale = 1.0 + mod("scale_f")
         final_in = to_low(normed * scale + mod("shift_f"))
         pred = mm(final_in, head_ref[...], 1, 0)
-        error = (pred - t_ref[...]) * flag_ref[frame]
-        loss_ref[pl.ds(frame, 1), :] = jnp.broadcast_to(
+        error = (pred - t_ref[...]) * true
+        loss_ref[pl.ds(pl.program_id(0), 1), :] = jnp.broadcast_to(
             jnp.sum(jnp.sum(error * error, axis=1, keepdims=True), axis=0, keepdims=True), (1, 128)
         )
         grad_pred = to_low(2.0 * error / flag_ref[FRAMES])
         ghead_ref[...] = ghead_ref[...] + mm(final_in, grad_pred, 0, 0)
         grad_fin = mm(grad_pred, head_ref[...], 1, 1)
-        store_sums(sum_ref, frame, 1, grad_fin, per_frame)
-        store_sums(sum_ref, frame, 2, grad_fin * normed, per_frame)
+        store_sums(sum_ref, first, 1, grad_fin, per_frame)
+        store_sums(sum_ref, first, 2, grad_fin * normed, per_frame)
         grad = norm_back(normed, inverse, grad_fin * scale)
         gh_ref[...] = grad
-        store_sums(sum_ref, frame, 0, grad * down_out, per_frame)
+        store_sums(sum_ref, first, 0, grad * down_out, per_frame)
         gd_ref[...] = to_low(grad * mod("gate_m"))
 
-    part_spec = (per_frame, D), lambda f: (f, 0)
+    part_spec = (block, D), lambda f: (f, 0)
     return run_kernel(
         kernel,
-        (FRAMES,),
+        (FRAMES // count,),
         [
             (flags, pltpu.SMEM),
             (hidden1, *part_spec),
@@ -870,14 +978,14 @@
             (got, *part_spec),
             (rest,),
             (head,),
-            (target, (per_frame, PD), lambda f: (f, 0)),
+            (target, (block, PD), lambda f: (f, 0)),
         ],
         [
             ((tokens, D), bf16, *part_spec),
             ((tokens, D), f32, *part_spec),
             ((FRAMES, 3 * D), f32),
             ((D, PD), f32),
-            ((FRAMES, 128), f32),
+            ((FRAMES // count, 128), f32),
         ],
         after=after,
         flops=8 * tokens * D * PD,
@@ -904,27 +1012,36 @@
     )[0]
 
 
-def run_act_up_back(grad, down, up_out, up, after=()):
+def run_act_up_back(grad, down, up_out, up, dtype, after=()):
     tokens, hidden = up_out.shape
     steps = hidden // CHUNK
 
     def kernel(g_ref, down_ref, o_ref, up_ref, out_ref, part_ref, acc):
         j = pl.program_id(0)
-        grad_act = mm(g_ref[...], down_ref[...], 1, 1)
-        grad_out = to_low(grad_act * gelu_slope(o_ref[...]))
-        out_ref[...] = grad_out
-        accumulate(acc, j, mm(grad_out, up_ref[...], 1, 1))
+
+        @pl.when(j == 0)
+        def clear():
+            acc[...] = jnp.zeros_like(acc)
+
+        spans = parts_of(tokens)
+        ready = mm(g_ref[spans[0], :], down_ref[...], 1, 1)
+        for k, span in enumerate(spans):
+            grad_act = ready
+            if k + 1 < len(spans):
+                ready = mm(g_ref[spans[k + 1], :], down_ref[...], 1, 1)
+            out_ref[span, :] = to_low(grad_act * gelu_slope(o_ref[span, :]))
+        acc[...] = acc[...] + mm(out_ref[...], up_ref[...], 1, 1)
 
         @pl.when(j == steps - 1)
         def finish():
-            part_ref[...] = to_low(acc[...])
+            part_ref[...] = acc[...].astype(part_ref.dtype)
 
     part = (tokens, CHUNK), lambda j: (0, j)
     return run_kernel(
         kernel,
         (steps,),
         [(grad,), down_rows(down), (up_out, *part), up_columns(up)],
-        [((tokens, hidden), bf16, *part), ((tokens, D), bf16)],
+        [((tokens, hidden), bf16, *part), ((tokens, D), dtype)],
         [pltpu.VMEM((tokens, D), f32)],
         after=after,
         flops=4 * tokens * D * hidden,
@@ -936,7 +1053,7 @@
     tokens, hidden = grad.shape
 
     def kernel(g_ref, up_ref, out_ref):
-        accumulate(out_ref, pl.program_id(0), mm(g_ref[...], up_ref[...], 1, 1))
+        accumulate(out_ref, pl.program_id(0), lambda: mm(g_ref[...], up_ref[...], 1, 1))
 
     return run_kernel(
         kernel,
@@ -988,40 +1105,87 @@
     return dict(zip(groups, outs))
 
 
-def run_up_dw(coords, sizes, ins, grads, proj, after=()):
+def run_act_up_dw(coords, sizes, ins, grad_up, grad, down, up_out, up, after=()):
     groups, nz = group_list(sizes), sizes[2]
-    hidden = grads[0].shape[1]
     rows = D // (len(groups) * nz)
+    tokens, hidden = up_out.shape
     steps = hidden // CHUNK
 
-    def kernel(coords_ref, a_ref, b_ref, ga_ref, gb_ref, proj_ref, *refs):
-        outs, acc = refs[: len(groups)], refs[len(groups)]
+    def kernel(coords_ref, a_ref, b_ref, ga_ref, g_ref, down_ref, o_ref, up_ref, part_ref, *refs):
+        outs, (acc, part_acc, gb_scr) = refs[: len(groups)], refs[len(groups) :]
         j = pl.program_id(0)
 
-        @pl.when(j < steps)
-        def up_part():
-            acc[...] = mm(a_ref[...], ga_ref[...], 0, 0) + mm(b_ref[...], gb_ref[...], 0, 0)
-
-        @pl.when(j == steps)
-        def proj_part():
-            acc[...] = proj_ref[...].astype(f32)
-
+        @pl.when(j == 0)
+        def clear():
+            part_acc[...] = jnp.zeros_like(part_acc)
+
+        spans = parts_of(tokens)
+        ready = mm(g_ref[spans[0], :], down_ref[...], 1, 1)
+        for k, span in enumerate(spans):
+            grad_act = ready
+            if k + 1 < len(spans):
+                ready = mm(g_ref[spans[k + 1], :], down_ref[...], 1, 1)
+            gb_scr[span, :] = to_low(grad_act * gelu_slope(o_ref[span, :]))
+        acc[...] = mm(a_ref[...], ga_ref[...], 0, 0) + mm(b_ref[...], gb_scr[...], 0, 0)
+        part_acc[...] = part_acc[...] + mm(gb_scr[...], up_ref[...], 1, 1)
         for out, (my, mx) in zip(outs, groups):
             for mz in range(nz):
                 first = chip_number(coords_ref, my, mx, mz) * rows
                 out[mz] = to_low(acc[pl.ds(pl.multiple_of(first, rows), rows), :])
 
-    part = (grads[0].shape[0], CHUNK), lambda j: (0, jnp.minimum(j, steps - 1))
+        @pl.when(j == steps - 1)
+        def finish():
+            part_ref[...] = to_low(part_acc[...])
+
+    part = (tokens, CHUNK), lambda j: (0, j)
     outs = run_kernel(
         kernel,
-        (steps + 1,),
-        [(ins[0],), (ins[1],), (grads[0], *part), (grads[1], *part), (proj,)],
-        [((nz, rows, hidden + CHUNK), bf16, (nz, rows, CHUNK), lambda j: (0, 0, j))] * len(groups),
-        [pltpu.VMEM((D, CHUNK), f32)],
+        (steps,),
+        [
+            (ins[0],),
+            (ins[1],),
+            (grad_up, *part),
+            (grad,),
+            down_rows(down),
+            (up_out, *part),
+            up_columns(up),
+        ],
+        [((tokens, D), bf16)]
+        + [((nz, rows, hidden), bf16, (nz, rows, CHUNK), lambda j: (0, 0, j))] * len(groups),
+        [
+            pltpu.VMEM((D, CHUNK), f32),
+            pltpu.VMEM((tokens, D), f32),
+            pltpu.VMEM((tokens, CHUNK), bf16),
+        ],
         coords,
         after,
-        flops=4 * ins[0].shape[0] * D * hidden,
-        moved=14 * 2**20,
+        flops=8 * tokens * D * hidden,
+        moved=26 * 2**20,
+    )
+    return outs[0], dict(zip(groups, outs[1:]))
+
+
+def run_add_pieces(coords, sizes, terms, after=()):
+    groups, nz = group_list(sizes), sizes[2]
+    rows, columns = terms[0].shape[0] // (len(groups) * nz), terms[0].shape[1]
+
+    def kernel(coords_ref, a_ref, b_ref, *refs):
+        outs, acc = refs[: len(groups)], refs[len(groups)]
+        acc[...] = a_ref[...].astype(f32) + b_ref[...].astype(f32)
+        for out, (my, mx) in zip(outs, groups):
+            for mz in range(nz):
+                first = chip_number(coords_ref, my, mx, mz) * rows
+                out[mz] = to_low(acc[pl.ds(pl.multiple_of(first, rows), rows), :])
+
+    outs = run_kernel(
+        kernel,
+        (1,),
+        [(terms[0],), (terms[1],)],
+        [((nz, rows, columns), bf16)] * len(groups),
+        [pltpu.VMEM(terms[0].shape, f32)],
+        coords,
+        after,
+        moved=6 * terms[0].size,
     )
     return dict(zip(groups, outs))
 
@@ -1053,8 +1217,8 @@
         attn_b = jnp.concatenate([a_ref[r] for r in range(rows)], axis=1)
         for r in range(rows):
             ga_ref[r] = grad_attn[:, r * width : (r + 1) * width]
-        accumulate(acc, step, mm(attn_b, low, 0, 0))
-        accumulate(ge_ref, step, mm(n_ref[...], to_low(grad), 0, 0))
+        accumulate(acc, step, lambda: mm(attn_b, low, 0, 0))
+        accumulate(ge_ref, step, lambda: mm(n_ref[...], to_low(grad), 0, 0))
 
         @pl.when(step == steps - 1)
         def finish():
@@ -1234,14 +1398,9 @@
     mine = mine.reshape(rows, part, 3 * width)
     token_cols = count_tok * PD // part
     tokens = jnp.broadcast_to(noisy_own.reshape(1, part, token_cols), (rows, part, token_cols))
-    mine = tie(jnp.concatenate([mine, tokens], axis=2), everyone)
-    mine = lax.all_to_all(mine, "row", 0, 0, tiled=True)
+    mine = row_swap(jnp.concatenate([mine, tokens], axis=2))
     noisy_all = mine[:, :, 3 * width :].reshape(rows, FRAMES, per_frame, PD)
     noisy_all = noisy_all.transpose(1, 0, 2, 3).reshape(TOK, PD)
-    qkv_pieces = chip_gather(
-        mine[:, :, : 3 * width].reshape(rows * part, 3 * width), False, hold=first_terms
-    )
-
     def halves(weight, blocks):
         parts = weight.reshape(weight.shape[0], -1, 2, weight.shape[1] // (2 * blocks))
         mine = lax.dynamic_index_in_dim(parts, core, 2, keepdims=False)
@@ -1256,34 +1415,46 @@
     tall = jnp.concatenate(
         [jnp.where(is_zero, tall_mine, tall_got), jnp.where(is_zero, tall_got, tall_mine)]
     )
-    tall_pieces = chip_gather(tall, hold=qkv_pieces[0][0], hold_x=qkv_pieces[1][0])
-    down_pieces = chip_gather(tie(to_low(down_w), tall_pieces[0][0]))
+    gather_down = Gather(to_low(down_w))
+    gather_down.go_z()
+    gather_down.go_xy()
+    gather_down.go_slant()
+    mine = tie(mine[:, :, : 3 * width], gather_down.own)
+    gather_qkv = Gather(mine.reshape(rows * part, 3 * width), False)
+    gather_qkv.go_z(first_terms)
+    gather_qkv.go_xy()
+    gather_qkv.go_slant()
+    gather_tall = Gather(tie(tall, gather_qkv.own, *gather_down.came_xy()))
+    gather_tall.go_z()
+    gather_tall.go_direct()
+    rest_sent = mod_terms(2, 8)
 
     cosine, sine = group_angles(frame_pos, width // 2)
-    query, keys, values, attn_in, qkv_b = run_qkv(
-        coords, noisy_all, embed_b, shift_a, scale_a, cosine, sine, qkv_pieces,
-        after=(tall_pieces[0][0],),
-    )
-    attn_heads, lse = run_attend(span, query, keys, values, rows)
-    rest_terms = lax.all_to_all(tie(mod_terms(2, 8), query), BOTH, 0, 0, tiled=True)
+    rest_terms = lax.all_to_all(rest_sent, BOTH, 0, 0, tiled=True)
+    query, keys, values, attn_in, qkv_b, attn_heads, lse = run_qkv_attend(
+        coords, span, noisy_all, embed_b, shift_a, scale_a, cosine, sine, gather_qkv.pieces(),
+        rows, after=(gather_tall.own, rest_sent) + tuple(piece[0] for piece in gather_down.slant),
+    )
+    rest_terms = tie(rest_terms, query)
     rest = modulation(rest_terms)
 
     def swap_row(wide):
         return lax.all_to_all(wide, "row", 0, 0, tiled=True)
 
-    attn = tie(attn_heads, rest_terms, down_pieces[0][0]).reshape(rows, count_tok, width)
+    attn = tie(attn_heads, rest_terms).reshape(rows, count_tok, width)
     attn = swap_row(attn)
-    up_b, proj_own = run_place(coords, tall_pieces, (hidden, D // 2), after=(attn_heads,))
+    down_b = run_place(coords, gather_down.pieces(), (D,), after=(attn_heads,))[0]
+    up_b, proj_own = run_place(
+        coords, gather_tall.pieces(), (hidden, D // 2), after=(down_b,)
+    )
     proj_other = exchange(proj_own, 1)
     hidden1, proj_out, mlp_in = run_proj(
         coords, attn, noisy_own, embed_b, rest, proj_own, proj_other
     )
     mlp_in_other = exchange(mlp_in, 1)
-    up_out, act = run_up(mlp_in, up_b)
-    down_b = run_place(coords, down_pieces, (D,), after=(act,))[0]
-    up_out_other, act_other, part_other = run_up_down(mlp_in_other, up_b, down_b)
+    up_out_other, act_other, part_other = run_up_down(mlp_in_other, up_b, down_b, bf16)
     part_got = exchange(part_other, 1)
-    part_own = run_down(act, down_b, after=(part_other,))
+    up_out, act, part_own = run_up_down(mlp_in, up_b, down_b, f32, after=(part_other,))
     flags = jnp.concatenate([is_true.astype(f32), (PD * count).reshape(1)])
     grad_down_out, grad_h2, sums_f, grad_head, losses = run_head(
         flags, hidden1, part_own, part_got, rest, head_b, target
@@ -1291,36 +1462,56 @@
     loss_local = jnp.sum(losses[:, 0])
 
     grad_down_other = exchange(grad_down_out, 1)
-    grad_up = run_act_back(grad_down_out, down_b, up_out)
     down_groups = run_down_dw(
-        coords, sizes, (act, act_other), (grad_down_out, grad_down_other), after=(grad_up,)
-    )
-    scatter_down = lambda hold: chip_scatter(down_groups, hold=hold)
-    grad_up_other, mlp_other = run_act_up_back(
-        grad_down_other, down_b, up_out_other, up_b, after=(down_groups[0, 0],)
+        coords, sizes, (act, act_other), (grad_down_out, grad_down_other)
+    )
+    scatter_down = Scatter(down_groups)
+    grad_up, mlp_own = run_act_up_back(
+        grad_down_out, down_b, up_out, up_b, f32, after=(down_groups[0, 0],)
+    )
+    mlp_other, up_groups = run_act_up_dw(
+        coords, sizes, (mlp_in, mlp_in_other), grad_up, grad_down_other, down_b,
+        up_out_other, up_b, after=tuple(scatter_down.sent.values()),
     )
     mlp_got = exchange(mlp_other, 1)
-    mlp_own = run_up_back(grad_up, up_b, after=(mlp_other,))
+    scatter_down.go_xy()
+    scatter_down.go_z(up_groups[0, 0])
     grad_attn, proj_mine, proj_theirs, sums_m, embed_h1 = run_proj_back(
         coords, grad_h2, mlp_own, mlp_got, hidden1, proj_out, rest,
-        proj_own, proj_other, attn, noisy_own,
+        proj_own, proj_other, attn, noisy_own, after=(scatter_down.own,),
     )
     grad_attn = swap_row(grad_attn).reshape(rows, FRAMES, per_frame, width)
-    proj_term = to_low(proj_mine.astype(f32) + exchange(proj_theirs, 1).astype(f32))
-    tall_groups = run_up_dw(
-        coords, sizes, (mlp_in, mlp_in_other), (grad_up, grad_up_other), proj_term
-    )
-    down_sum, down_xy, down_z = scatter_down(tall_groups[0, 0])
-    tall_sum, tall_xy, tall_z = chip_scatter(tall_groups, direct=True)
+    scatter_up = Scatter(up_groups, grad_attn)
+    proj_groups = run_add_pieces(coords, sizes, (proj_mine, exchange(proj_theirs, 1)))
+    scatter_up.go_xy(proj_groups, grad_attn)
+
+    def mod_row(values_mod, *hold):
+        wide = values_mod.shape[1] // rows
+        total = to_low(row_sum(values_mod, *hold))
+        return lax.dynamic_slice_in_dim(total, row_index * wide, wide, axis=1)
+
+    def mod_all(total):
+        wide = total.shape[-1]
+        total = total.reshape(clips, rows, FRAMES, wide)
+        return total.transpose(0, 2, 1, 3).reshape(clips * FRAMES, rows * wide)
+
+    mod_rest = spread(mod_row(jnp.concatenate([sums_m, sums_f], axis=1)), BOTH)
     grad_qkv = run_attend_back(
         span, query, keys, values, attn_heads, grad_attn, lse, cosine, sine,
-        after=(tall_groups[0, 0], down_z),
-    )
-    sums_a, grad_embed, qkv_groups = run_qkv_back(
-        coords, noisy_all, embed_b, scale_a, attn_in, grad_qkv, qkv_b, nx, nz,
-        after=(tall_z, down_sum),
-    )
-    qkv_sum, unused_xy, qkv_z = chip_scatter(qkv_groups, False)
+        after=(proj_groups[0, 0],) + tuple(scatter_up.sent.values()),
+    )
+    scatter_up.go_z(grad_qkv)
+    grad_qkv_w = run_qkv_dw(
+        attn_in, grad_qkv, after=(scatter_up.own, mod_rest, *scatter_down.came_z)
+    )
+    qkv_terms = grad_qkv_w.reshape(count_dev, part, 3 * width)
+    qkv_terms = lax.all_to_all(qkv_terms, BOTH, 0, 0, tiled=True)
+    sums_a, grad_embed = run_qkv_back(
+        noisy_all, embed_b, scale_a, grad_qkv, qkv_b,
+        after=(grad_qkv_w, *scatter_up.came_z),
+    )
+    tall_sum = scatter_up.result()
+    down_sum = scatter_down.result(sums_a)
     grad_embed = grad_embed + embed_h1
 
     keep = lax.dynamic_slice_in_dim(tall_sum, core * part, part)
@@ -1330,25 +1521,6 @@
     up_sum = pair_sum[:, :, :hidden].reshape(part, 2, count_dev // 2, unit)
     up_sum = up_sum.transpose(0, 2, 1, 3).reshape(part, FF)
     proj_sum = pair_sum[:, :, hidden:].reshape(part, D)
-    qkv_sum = tie(to_low(qkv_sum), tall_sum).reshape(rows, part, 3 * width)
-    qkv_sum = swap_row(qkv_sum).reshape(rows, part, 3, width)
-    turned = dot_low("rdgv,wv->dgrw", qkv_sum[:, :, :2], perm)
-    straight = qkv_sum[:, :, 2:].transpose(1, 2, 0, 3).astype(f32)
-    qkv_sum = jnp.concatenate([turned, straight], axis=1).reshape(part, 3 * D)
-
-    def mod_row(values_mod):
-        wide = values_mod.shape[1] // rows
-        total = to_low(row_sum(values_mod))
-        return lax.dynamic_slice_in_dim(total, row_index * wide, wide, axis=1)
-
-    def mod_all(total):
-        wide = total.shape[-1]
-        total = total.reshape(clips, rows, FRAMES, wide)
-        return total.transpose(0, 2, 1, 3).reshape(clips * FRAMES, rows * wide)
-
-    mod_rest = mod_row(jnp.concatenate([sums_m, sums_f], axis=1))
-    mod_rest = mod_all(spread(tie(mod_rest, grad_qkv), BOTH))
-
     small = jnp.concatenate(
         [
             grad_embed.reshape(PD, count_dev, part).transpose(1, 0, 2).reshape(count_dev, -1),
@@ -1359,7 +1531,8 @@
     small = to_low(small).reshape(count_dev, 1, -1)
     mod_first = mod_row(sums_a)
     wide = mod_first.shape[-1]
-    lines = small.shape[-1] // wide
+    lines = max(small.shape[-1] // wide, 1)
+    small = jnp.pad(small, ((0, 0), (0, 0), (0, lines * wide - small.shape[-1])))
     last = jnp.concatenate(
         [
             jnp.broadcast_to(mod_first[None], (count_dev, FRAMES, wide)),
@@ -1367,12 +1540,17 @@
         ],
         axis=1,
     )
-    last = lax.all_to_all(tie(last, qkv_z), BOTH, 0, 0, tiled=True)
-    mod_first = mod_all(last[:, :FRAMES])
+    last = lax.all_to_all(tie(last, qkv_terms), BOTH, 0, 0, tiled=True)
     small = jnp.sum(last[:, FRAMES:].astype(f32), axis=0).reshape(-1)
     embed_sum = small[: PD * part].reshape(PD, part)
-    head_sum = small[PD * part :].reshape(part, PD)
-    grad_mod_b = jnp.concatenate([mod_first, mod_rest], axis=1)
+    head_sum = small[PD * part : 2 * PD * part].reshape(part, PD)
+    qkv_sum = qkv_terms.reshape(clips, rows, part, 3, width).astype(f32)
+    qkv_sum = to_low(jnp.sum(qkv_sum, axis=0))
+    turned = dot_low("rdgv,wv->dgrw", qkv_sum[:, :, :2], perm)
+    straight = qkv_sum[:, :, 2:].transpose(1, 2, 0, 3).astype(f32)
+    qkv_sum = jnp.concatenate([turned, straight], axis=1).reshape(part, 3 * D)
+
+    grad_mod_b = jnp.concatenate([mod_all(last[:, :FRAMES]), mod_all(mod_rest)], axis=1)
     grad_adaln = dot_low("fd,fm->dm", cond_act, grad_mod_b)
     grad_cond_act = dot_low("fm,dm->fd", grad_mod_b, adaln_low)
     unused_silu, silu_pull = jax.vjp(jax.nn.silu, cond)

time: 622 us -> 537 us (0.86)
  Pallas kernels: 256 us -> 190 us
  waiting for transfers between devices: 164 us -> 130 us
  other arithmetic: 30.6 us -> 43.2 us
    pallas_call x22 -> x20, Pallas kernels: 256 us -> 190 us  [run_kernel(): return call(*([] if scalars is None else [scalars]), *arrays)]
    ppermute x51 -> x50, waiting for transfers between devices: 142 us -> 120 us  [exchange(): return lax.ppermute(values, BOTH, [(i, i ^ mask) for i in range(count)])]
    all_to_all x2, waiting for transfers between devices: 13.7 us -> 0.95 us  [spread(): return lax.all_to_all(copies, axes, 0, 0, tiled=True)]
    all_to_all x3 -> x2, starting transfers between devices: 20 us -> 8 us  [swap_row(): return lax.all_to_all(wide, 'row', 0, 0, tiled=True)]
    all_to_all x3, starting transfers between devices: 15.5 us -> 24.5 us  [the longest x1 11.7 us: body(): last = lax.all_to_all(tie(last, qkv_terms), BOTH, 0, 0, tiled=True)]
    convert_element_type x15 -> x19, other arithmetic: 10.3 us -> 14 us  [to_low(): return values.astype(bf16)]
    ppermute x51 -> x50, starting transfers between devices: 57.7 us -> 55.3 us  [exchange(): return lax.ppermute(values, BOTH, [(i, i ^ mask) for i in range(count)])]
  transfers between devices with their start and end apart: 60 -> 58, of which waited for: 21 -> 17; matrix products, arithmetic and copies ran while one was open for 9% -> 13% of each run, Pallas kernels for 33% -> 25%
where the time goes in v2:
time: 537 us; the launch traced here: 530 us
  Pallas kernels  190 us (35%)
  waiting for transfers between devices  130 us (24%)
  starting transfers between devices  104 us (19%)
  other arithmetic  43.2 us (8%)
  local copies, waits for them, and re-layouts  39.7 us (7%)
  blocking collectives  12.9 us (2%)
  matrix products  5.57 us (1%)
    pallas_call x20, Pallas kernels, run_kernel(): return call(*([] if scalars is None else [scalars]), *arrays)  190 us
    ppermute x50, waiting for transfers between devices, exchange(): return lax.ppermute(values, BOTH, [(i, i ^ mask) for i in range(count)])  120 us
    ppermute x50, starting transfers between devices, exchange(): return lax.ppermute(values, BOTH, [(i, i ^ mask) for i in range(count)])  55.3 us
    convert_element_type x19, other arithmetic, to_low(): return values.astype(bf16)  14 us
    all_to_all x1, blocking collectives, spread(): return lax.all_to_all(copies, axes, 0, 0, tiled=True)  12.9 us
    all_to_all x2, starting transfers between devices, spread(): return lax.all_to_all(copies, axes, 0, 0, tiled=True)  11.7 us
    all_to_all x1, starting transfers between devices, body(): last = lax.all_to_all(tie(last, qkv_terms), BOTH, 0, 0, tiled=True)  11.7 us
    unnamed x135, local copies, waits for them, and re-layouts  11 us
  transfers between devices with their start and end apart: 58, of which 17 were waited for; matrix products, arithmetic and copies ran while one was open for 13% of the time, Pallas kernels for 25%

profile of v2, /device:TPU:0, one launch (start us, length us, event | category | flops | bytes accessed | tf_op | source)
XLA Modules:
  0.0 529.8 jit_solution(4658768175163755881)
XLA Ops:
  14.6 6.1 %all-to-all-start = ((f32[32,1,1040]{2,1,0:T(1,128)}), f32[32,1,1040]{2,1,0:T(1,128)S(1)}, u32[]{:S(2)}, u32[]{:S(2)}) async-start(f32[32,1,1040]{2,1,0:T(1,128)} %broadcast_in_dim.182), calls=%async_computation | async-start | bytes 294912 | tf_op jit(solution)/shard_map/all_to_all | solution.py:317
  60.4 15.4 %collective-permute-done.9 = bf16[128,768]{1,0:T(8,128)(2,1)} collective-permute-done((bf16[128,768]{1,0:T(8,128)(2,1)}, bf16[128,768]{1,0:T(8,128)(2,1)}, u32[]{:S(2)}, u32[]{:S(2)}) %collective-permute-start.9) | collective-permute-done | bytes 196640 | tf_op jit(solution)/shard_map/ppermute | solution.py:147
  77.4 13.9 %collective-permute-done.8 = bf16[128,768]{1,0:T(8,128)(2,1)} collective-permute-done((bf16[128,768]{1,0:T(8,128)(2,1)}, bf16[128,768]{1,0:T(8,128)(2,1)}, u32[]{:S(2)}, u32[]{:S(2)}) %collective-permute-start.8) | collective-permute-done | bytes 196640 | tf_op jit(solution)/shard_map/ppermute | solution.py:147
  107.9 14.7 %collective-permute-done.15 = bf16[64,2560]{1,0:T(8,128)(2,1)S(1)} collective-permute-done((bf16[64,2560]{1,0:T(8,128)(2,1)S(1)}, bf16[64,2560]{1,0:T(8,128)(2,1)S(1)}, u32[]{:S(2)}, u32[]{:S(2)}) %collective-permute-start.15) | collective-permute-done | bytes 327712 | tf_op jit(solution)/shard_map/ppermute | solution.py:147
  127.3 29.3 %shard_map.421 = (bf16[2048,256]{1,0:T(8,128)(2,1)}, bf16[2048,256]{1,0:T(8,128)(2,1)}, bf16[2048,256]{1,0:T(8,128)(2,1)}, bf16[2048,1024]{1,0:T(8,128)(2,1)}, b...) custom-call(s32[22]{0:T(128)} %concatenate.81.refs_0_, bf16[2048,16]{1,0:T(8,128)(2,1)} %bitcast.217, ...), custom_call_target="tpu_custom_call" | custom-call | flops 12884901888 | bytes 20971520 | tf_op jit(solution)/shard_map/pallas_call | solution.py:369
  166.8 14.8 %collective-permute-done.22.refs_3_ = bf16[4,64,2560]{2,1,0:T(8,128)(2,1)} collective-permute-done((bf16[4,64,2560]{2,1,0:T(8,128)(2,1)S(1)}, bf16[4,64,2560]{2,1,0:T(8,128)(2,1)}, u32[]{:S(2)}, u32[]{:S(2)}) %collective-permute-start.22) | collective-permute-done | bytes 1310752 | tf_op jit(solution)/shard_map/ppermute | solution.py:147
  196.7 6.2 %shard_map.424 = (f32[512,1024]{1,0:T(8,128)}, f32[512,1024]{1,0:T(8,128)}, bf16[512,1024]{1,0:T(8,128)(2,1)}) custom-call(s32[6]{0:T(128)} %stack.95.refs_0_, bf16[4,512,256]{2,1,0:T(8,128)(2,1)} %copy-done.6, bf16[512,16]{1,0:T(8,128)(2,1)} %get-tuple-element.365.refs_2_.refs_10_, bf16[16,1024]{1,0:T(8,128)(2,1)} %reshape.520.refs_2_.refs_3_.refs_1_, ...), custom_call_target="tpu_custom_call" | custom-call | flops 1073741824 | bytes 10485760 | tf_op jit(solution)/shard_map/pallas_call | solution.py:369
  206.7 10.6 %shard_map.425 = (f32[512,2048]{1,0:T(8,128)}, bf16[512,2048]{1,0:T(8,128)(2,1)}, bf16[512,1024]{1,0:T(8,128)(2,1)}) custom-call(bf16[512,1024]{1,0:T(8,128)(2,1)} %copy-done.59, bf16[1024,2048]{1,0:T(8,128)(2,1)} %get-tuple-element.117.refs_1_.refs_3_.refs_7_, bf16[2048,1024]{1,0:T(8,128)(2,1)} %shard_map.422.refs_5_.refs_2_.refs_1_), custom_call_target="tpu_custom_call" | custom-call | flops 4294967296 | bytes 16777216 | tf_op jit(solution)/shard_map/pallas_call | solution.py:369
  221.1 11.0 %shard_map.426 = (f32[512,2048]{1,0:T(8,128)}, bf16[512,2048]{1,0:T(8,128)(2,1)}, f32[512,1024]{1,0:T(8,128)}) custom-call(bf16[512,1024]{1,0:T(8,128)(2,1)} %get-tuple-element.116.refs_0_.refs_1_, bf16[1024,2048]{1,0:T(8,128)(2,1)} %get-tuple-element.117.refs_1_.refs_3_.refs_7_, bf16[2048,1024]{1,0:T(8,128)(2,1)} %shard_map.422.refs_5_.refs_2_.refs_1_, ...), custom_call_target="tpu_custom_call" | custom-call | flops 4294967296 | bytes 16777216 | tf_op jit(solution)/shard_map/pallas_call | solution.py:369
  233.1 7.2 %shard_map.427 = (bf16[512,1024]{1,0:T(8,128)(2,1)}, f32[512,1024]{1,0:T(8,128)}, f32[8,3072]{1,0:T(8,128)}, f32[1024,16]{1,0:T(8,128)}, f32[4,128]{1,0:T(4,128)}) custom-call(f32[9]{0:T(128)} %pad_maximum_fusion.25.refs_0_, f32[512,1024]{1,0:T(8,128)} %get-tuple-element.121.refs_1_.refs_4_, f32[512,1024]{1,0:T(8,128)} %get-tuple-element.122.refs_2_, ...), custom_call_target="tpu_custom_call" | custom-call | flops 67108864 | bytes 10485760 | tf_op jit(solution)/shard_map/pallas_call | solution.py:369
  244.2 10.1 %shard_map.428 = (bf16[4,128,1024]{2,1,0:T(8,128)(2,1)}, bf16[4,128,1024]{2,1,0:T(8,128)(2,1)}, bf16[4,128,1024]{2,1,0:T(8,128)(2,1)}, bf16[4,128,1024]{2,1,0:T(8,128)(2,1)}) custom-call(s32[6]{0:T(128)} %stack.95.refs_0_, bf16[512,2048]{1,0:T(8,128)(2,1)} %get-tuple-element.119.refs_1_, bf16[512,2048]{1,0:T(8,128)(2,1)} %get-tuple-element.120.refs_2_, ...), custom_call_target="tpu_custom_call" | custom-call | flops 4294967296 | bytes 10485760 | tf_op jit(solution)/shard_map/pallas_call | solution.py:369
  257.3 11.5 %shard_map.429 = (bf16[512,2048]{1,0:T(8,128)(2,1)}, f32[512,1024]{1,0:T(8,128)}) custom-call(bf16[512,1024]{1,0:T(8,128)(2,1)} %get-tuple-element.123.refs_3_.refs_0_, bf16[2048,1024]{1,0:T(8,128)(2,1)} %shard_map.422.refs_5_.refs_2_.refs_1_, f32[512,2048]{1,0:T(8,128)} %get-tuple-element.127.refs_2_, ...), custom_call_target="tpu_custom_call" | custom-call | flops 4294967296 | bytes 16777216 | tf_op jit(solution)/shard_map/pallas_call | solution.py:369
  273.0 17.8 %shard_map.430 = (bf16[512,1024]{1,0:T(8,128)(2,1)}, bf16[4,64,2048]{2,1,0:T(8,128)(2,1)}, bf16[4,64,2048]{2,1,0:T(8,128)(2,1)}, bf16[4,64,2048]{2,1,0:T(8,128)(2,1)}, bf16[4,64,2048]{2,1,0:T(8,128)(2,1)}) custom-call(s32[6]{0:T(128)} %stack.95.refs_0_, bf16[512,1024]{1,0:T(8,128)(2,1)} %get-tuple-element.116.refs_0_.refs_1_, bf16[512,1024]{1,0:T(8,128)(2,1)} %copy-done.59, ...), custom_call_target="tpu_custom_call" | custom-call | flops 8589934592 | bytes 27262976 | tf_op jit(solution)/shard_map/pallas_call | solution.py:369
  299.7 11.3 %shard_map.431 = (bf16[4,512,256]{2,1,0:T(8,128)(2,1)}, bf16[1024,512]{1,0:T(8,128)(2,1)}, bf16[1024,512]{1,0:T(8,128)(2,1)}, f32[8,3072]{1,0:T(8,128)}, f32[16,1024]{1,0:T(8,128)}) custom-call(s32[6]{0:T(128)} %stack.95.refs_0_, f32[512,1024]{1,0:T(8,128)} %get-tuple-element.136.refs_1_, f32[512,1024]{1,0:T(8,128)} %get-tuple-element.137.refs_2_, ...), custom_call_target="tpu_custom_call" | custom-call | flops 2147483648 | bytes 18874368 | tf_op jit(solution)/shard_map/pallas_call | solution.py:369
  328.2 13.8 %collective-permute-done.41 = bf16[8,6144]{1,0:T(8,128)(2,1)S(1)} collective-permute-done((bf16[8,6144]{1,0:T(8,128)(2,1)S(1)}, bf16[8,6144]{1,0:T(8,128)(2,1)S(1)}, u32[]{:S(2)}, u32[]{:S(2)}) %collective-permute-start.41) | collective-permute-done | bytes 98336 | tf_op jit(solution)/shard_map/ppermute | solution.py:147
  360.7 21.7 %shard_map.433.refs_1_.refs_3_ = bf16[2048,768]{1,0:T(8,128)(2,1)} custom-call(s32[2,8]{1,0:T(2,128)} %copy-done.54, bf16[2048,256]{1,0:T(8,128)(2,1)} %get-tuple-element.112.refs_1_, bf16[2048,256]{1,0:T(8,128)(2,1)} %get-tuple-element.134.refs_2_, bf16[2048,256]{1,0:T(8,128)(2,1)} %get-tuple-element.135.refs_3_, ...), custom_call_target="tpu_custom_call" | custom-call | flops 24159191040 | bytes 12582912 | tf_op jit(solution)/shard_map/pallas_call | solution.py:369
  382.3 15.4 %collective-permute-done.38 = bf16[4,64,2560]{2,1,0:T(8,128)(2,1)S(1)} collective-permute-done((bf16[4,64,2560]{2,1,0:T(8,128)(2,1)S(1)}, bf16[4,64,2560]{2,1,0:T(8,128)(2,1)S(1)}, u32[]{:S(2)}, u32[]{:S(2)}) %collective-permute-start.38) | collective-permute-done | bytes 1310752 | tf_op jit(solution)/shard_map/ppermute | solution.py:147
  409.8 7.7 %shard_map.434.refs_5_ = bf16[1024,768]{1,0:T(8,128)(2,1)} custom-call(bf16[2048,1024]{1,0:T(8,128)(2,1)} %get-tuple-element.151.refs_0_, bf16[2048,768]{1,0:T(8,128)(2,1)} %shard_map.433.refs_1_.refs_3_, bf16[4,64,2560]{2,1,0:T(8,128)(2,1)} %pad_maximum_fusion.refs_2_, bf16[32,8,1536]{2,1,0:T(8,128)(2,1)} %copy-done.7, ...), custom_call_target="tpu_custom_call" | custom-call | flops 3221225472 | bytes 10485760 | tf_op jit(solution)/shard_map/pallas_call | solution.py:369
  417.5 10.0 %all-to-all-start.6 = ((bf16[32,32,768]{2,1,0:T(8,128)(2,1)}), bf16[32,32,768]{2,1,0:T(8,128)(2,1)}, u32[]{:S(2)}, u32[]{:S(2)}) async-start(bf16[32,32,768]{2,1,0:T(8,128)(2,1)} %bitcast.207), calls=%async_computation.6 | async-start | bytes 3145728 | tf_op jit(solution)/shard_map/all_to_all | solution.py:1508
  427.6 11.4 %collective-permute-done.45.refs_7_ = bf16[64,2560]{1,0:T(8,128)(2,1)} collective-permute-done((bf16[64,2560]{1,0:T(8,128)(2,1)S(1)}, bf16[64,2560]{1,0:T(8,128)(2,1)}, u32[]{:S(2)}, u32[]{:S(2)}) %collective-permute-start.45) | collective-permute-done | bytes 327712 | tf_op jit(solution)/shard_map/ppermute | solution.py:147
  439.0 11.9 %shard_map.435 = (f32[8,2048]{1,0:T(8,128)}, f32[16,1024]{1,0:T(8,128)}) custom-call(bf16[2048,16]{1,0:T(8,128)(2,1)} %bitcast.218, bf16[16,1024]{1,0:T(8,128)(2,1)} %reshape.520.refs_2_.refs_3_.refs_1_, f32[8,1024]{1,0:T(8,128)} %get-tuple-element.380.refs_4_.refs_2_, bf16[2048,768]{1,0:T(8,128)(2,1)} %shard_map.433.refs_1_.refs_3_, ...), custom_call_target="tpu_custom_call" | custom-call | flops 3221225472 | bytes 8388608 | tf_op jit(solution)/shard_map/pallas_call | solution.py:369
  463.7 6.8 %all-to-all-done.6 = bf16[32,32,768]{2,1,0:T(8,128)(2,1)} async-done(((bf16[32,32,768]{2,1,0:T(8,128)(2,1)}), bf16[32,32,768]{2,1,0:T(8,128)(2,1)}, u32[]{:S(2)}, u32[]{:S(2)}) %all-to-all-start.6) | async-done | bytes 1572896 | tf_op jit(solution)/shard_map/all_to_all | solution.py:1508
  470.5 11.7 %all-to-all-start.7 = ((bf16[32,10,512]{2,1,0:T(8,128)(2,1)}), bf16[32,10,512]{2,1,0:T(8,128)(2,1)S(1)}, u32[]{:S(2)}, u32[]{:S(2)}) async-start(bf16[32,10,512]{2,1,0:T(8,128)(2,1)} %pad_maximum_fusion.14), calls=%async_computation.7 | async-start | bytes 1048576 | tf_op jit(solution)/shard_map/all_to_all | solution.py:1543
  509.3 12.9 %all_to_all.45 = f32[32,1,128]{2,1,0:T(1,128)S(1)} all-to-all(f32[32,1,128]{2,1,0:T(1,128)S(1)} %broadcast_in_dim.205), channel_id=1, replica_groups=mesh['clip'=8,'row'=4] {'clip','row'}, dimensions={0} | all-to-all | bytes 32768 | tf_op jit(solution)/shard_map/all_to_all | solution.py:317
  (420 shorter events, 221.8 us)
Async XLA Ops:
  2.5 39.0 %collective-permute-start.5 = (bf16[128,1024]{1,0:T(8,128)(2,1)}, bf16[128,1024]{1,0:T(8,128)(2,1)}, u32[]{:S(2)}, u32[]{:S(2)}) collective-permute-start(bf16[128,1024]{1,0:T(8,128)(2,1)} %convert_element_type.299), channel_id=1, source_target_pairs={{0,16},{1,17},{2,18},{3,19},{4,20},{5,21},{6,22},{7,23},{8,24},{9,... | collective-permute-start | bytes 786440 | tf_op jit(solution)/shard_map/ppermute | solution.py:147
  6.5 35.0 %collective-permute-start.4 = (bf16[128,1024]{1,0:T(8,128)(2,1)}, bf16[128,1024]{1,0:T(8,128)(2,1)}, u32[]{:S(2)}, u32[]{:S(2)}) collective-permute-start(bf16[128,1024]{1,0:T(8,128)(2,1)} %convert_element_type.299), channel_id=1, source_target_pairs={{0,8},{1,9},{2,10},{3,11},{4,12},{5,13},{6,14},{7,15},{8,0},{9,1},... | collective-permute-start | bytes 786440 | tf_op jit(solution)/shard_map/ppermute | solution.py:147
  8.1 33.4 %collective-permute-start.6 = (bf16[128,1024]{1,0:T(8,128)(2,1)}, bf16[128,1024]{1,0:T(8,128)(2,1)}, u32[]{:S(2)}, u32[]{:S(2)}) collective-permute-start(bf16[128,1024]{1,0:T(8,128)(2,1)} %convert_element_type.299), channel_id=1, source_target_pairs={{0,24},{1,25},{2,26},{3,27},{4,28},{5,29},{6,30},{7,31},{8,16},{9,... | collective-permute-start | bytes 786440 | tf_op jit(solution)/shard_map/ppermute | solution.py:147
  42.8 51.3 %collective-permute-start.13 = (bf16[4,128,1024]{2,1,0:T(8,128)(2,1)S(1)}, bf16[4,128,1024]{2,1,0:T(8,128)(2,1)S(1)}, u32[]{:S(2)}, u32[]{:S(2)}) collective-permute-start(bf16[4,128,1024]{2,1,0:T(8,128)(2,1)S(1)} %pad_maximum_fusion.4.refs_1_), channel_id=1, source_target_pairs={{0,4},{1,5},{2,6},{3,7},{4,0},{5,1},{6,2},{7,3},{8,12},{9,13},{10,... | collective-permute-start | bytes 3145736 | tf_op jit(solution)/shard_map/ppermute | solution.py:147
  44.6 49.5 %collective-permute-start.12 = (bf16[4,128,1024]{2,1,0:T(8,128)(2,1)S(1)}, bf16[4,128,1024]{2,1,0:T(8,128)(2,1)}, u32[]{:S(2)}, u32[]{:S(2)}) collective-permute-start(bf16[4,128,1024]{2,1,0:T(8,128)(2,1)S(1)} %pad_maximum_fusion.4.refs_1_), channel_id=1, source_target_pairs={{0,2},{1,3},{2,0},{3,1},{4,6},{5,7},{6,4},{7,5},{8,10},{9,11},{10,... | collective-permute-start | bytes 3145736 | tf_op jit(solution)/shard_map/ppermute | solution.py:147
  50.9 105.7 %all-to-all-start.2 = ((bf16[32,8,1536]{2,1,0:T(8,128)(2,1)}), bf16[32,8,1536]{2,1,0:T(8,128)(2,1)S(1)}, u32[]{:S(2)}, u32[]{:S(2)}) async-start(bf16[32,8,1536]{2,1,0:T(8,128)(2,1)} %bitcast.53.refs_10_), calls=%async_computation.2 | async-start | bytes 1572864 | tf_op jit(solution)/shard_map/all_to_all | solution.py:1433
  58.5 32.8 %collective-permute-start.8 = (bf16[128,768]{1,0:T(8,128)(2,1)}, bf16[128,768]{1,0:T(8,128)(2,1)}, u32[]{:S(2)}, u32[]{:S(2)}) collective-permute-start(bf16[128,768]{1,0:T(8,128)(2,1)} %bitcast.41), channel_id=1, source_target_pairs={{0,16},{1,17},{2,18},{3,19},{4,20},{5,21},{6,22},{7,23},{8,24},{9,... | collective-permute-start | bytes 589832 | tf_op jit(solution)/shard_map/ppermute | solution.py:147
  59.7 31.6 %collective-permute-start.7 = (bf16[128,768]{1,0:T(8,128)(2,1)}, bf16[128,768]{1,0:T(8,128)(2,1)S(1)}, u32[]{:S(2)}, u32[]{:S(2)}) collective-permute-start(bf16[128,768]{1,0:T(8,128)(2,1)} %bitcast.41), channel_id=1, source_target_pairs={{0,8},{1,9},{2,10},{3,11},{4,12},{5,13},{6,14},{7,15},{8,0},{9,1},... | collective-permute-start | bytes 589832 | tf_op jit(solution)/shard_map/ppermute | solution.py:147
  92.5 33.3 %collective-permute-start.10 = (bf16[4,128,768]{2,1,0:T(8,128)(2,1)S(1)}, bf16[4,128,768]{2,1,0:T(8,128)(2,1)S(1)}, u32[]{:S(2)}, u32[]{:S(2)}) collective-permute-start(bf16[4,128,768]{2,1,0:T(8,128)(2,1)S(1)} %pad_maximum_fusion.10.refs_7_), channel_id=1, source_target_pairs={{0,4},{1,5},{2,6},{3,7},{4,0},{5,1},{6,2},{7,3},{8,12},{9,13},{10,... | collective-permute-start | bytes 2359304 | tf_op jit(solution)/shard_map/ppermute | solution.py:147
  98.7 27.6 %collective-permute-start.18 = (bf16[2,128,1024]{2,1,0:T(8,128)(2,1)S(1)}, bf16[2,128,1024]{2,1,0:T(8,128)(2,1)S(1)}, u32[]{:S(2)}, u32[]{:S(2)}) collective-permute-start(bf16[2,128,1024]{2,1,0:T(8,128)(2,1)S(1)} %slice.218), channel_id=1, source_target_pairs={{0,2},{1,3},{2,0},{3,1},{4,6},{5,7},{6,4},{7,5},{8,10},{9,11},{10,... | collective-permute-start | bytes 1572872 | tf_op jit(solution)/shard_map/ppermute | solution.py:147
  122.7 44.1 %collective-permute-start.23 = (bf16[4,64,2560]{2,1,0:T(8,128)(2,1)S(1)}, bf16[4,64,2560]{2,1,0:T(8,128)(2,1)}, u32[]{:S(2)}, u32[]{:S(2)}) collective-permute-start(bf16[4,64,2560]{2,1,0:T(8,128)(2,1)S(1)} %pad_maximum_fusion.1.refs_9_.refs_1_), channel_id=1, source_target_pairs={{0,6},{1,7},{2,4},{3,5},{4,2},{5,3},{6,0},{7,1},{8,14},{9,15},{10,... | collective-permute-start | bytes 3932168 | tf_op jit(solution)/shard_map/ppermute | solution.py:147
  124.1 57.5 %collective-permute-start.22 = (bf16[4,64,2560]{2,1,0:T(8,128)(2,1)S(1)}, bf16[4,64,2560]{2,1,0:T(8,128)(2,1)}, u32[]{:S(2)}, u32[]{:S(2)}) collective-permute-start(bf16[4,64,2560]{2,1,0:T(8,128)(2,1)S(1)} %pad_maximum_fusion.1.refs_9_.refs_1_), channel_id=1, source_target_pairs={{0,4},{1,5},{2,6},{3,7},{4,0},{5,1},{6,2},{7,3},{8,12},{9,13},{10,... | collective-permute-start | bytes 3932168 | tf_op jit(solution)/shard_map/ppermute | solution.py:147
  125.8 55.8 %collective-permute-start.21 = (bf16[4,64,2560]{2,1,0:T(8,128)(2,1)S(1)}, bf16[4,64,2560]{2,1,0:T(8,128)(2,1)}, u32[]{:S(2)}, u32[]{:S(2)}) collective-permute-start(bf16[4,64,2560]{2,1,0:T(8,128)(2,1)S(1)} %pad_maximum_fusion.1.refs_9_.refs_1_), channel_id=1, source_target_pairs={{0,2},{1,3},{2,0},{3,1},{4,6},{5,7},{6,4},{7,5},{8,10},{9,11},{10,... | collective-permute-start | bytes 3932168 | tf_op jit(solution)/shard_map/ppermute | solution.py:147
  158.0 37.4 %all-to-all-start.3 = ((bf16[4,512,256]{2,1,0:T(8,128)(2,1)}), bf16[4,512,256]{2,1,0:T(8,128)(2,1)S(1)}, u32[]{:S(2)}, u32[]{:S(2)}) async-start(bf16[4,512,256]{2,1,0:T(8,128)(2,1)} %bitcast.197), calls=%async_computation.3 | async-start | bytes 2097152 | tf_op jit(solution)/shard_map/all_to_all | solution.py:1442
  314.0 36.0 %collective-permute-start.36 = (bf16[2,64,2048]{2,1,0:T(8,128)(2,1)}, bf16[2,64,2048]{2,1,0:T(8,128)(2,1)S(1)}, u32[]{:S(2)}, u32[]{:S(2)}) collective-permute-start(bf16[2,64,2048]{2,1,0:T(8,128)(2,1)} %get-tuple-element.358), channel_id=1, source_target_pairs={{0,2},{1,3},{2,0},{3,1},{4,6},{5,7},{6,4},{7,5},{8,10},{9,11},{10,... | collective-permute-start | bytes 1572872 | tf_op jit(solution)/shard_map/ppermute | solution.py:147
  314.6 34.1 %collective-permute-start.35 = (bf16[2,64,2048]{2,1,0:T(8,128)(2,1)}, bf16[2,64,2048]{2,1,0:T(8,128)(2,1)}, u32[]{:S(2)}, u32[]{:S(2)}) collective-permute-start(bf16[2,64,2048]{2,1,0:T(8,128)(2,1)} %get-tuple-element.359), channel_id=1, source_target_pairs={{0,4},{1,5},{2,6},{3,7},{4,0},{5,1},{6,2},{7,3},{8,12},{9,13},{10,... | collective-permute-start | bytes 1572872 | tf_op jit(solution)/shard_map/ppermute | solution.py:147
  324.0 81.9 %collective-permute-start.43 = (bf16[128,1024]{1,0:T(8,128)(2,1)}, bf16[128,1024]{1,0:T(8,128)(2,1)}, u32[]{:S(2)}, u32[]{:S(2)}) collective-permute-start(bf16[128,1024]{1,0:T(8,128)(2,1)} %get-tuple-element.355), channel_id=1, source_target_pairs={{0,24},{1,25},{2,26},{3,27},{4,28},{5,29},{6,30},{7,31},{8,16},{9,... | collective-permute-start | bytes 786440 | tf_op jit(solution)/shard_map/ppermute | solution.py:147
  325.6 83.4 %collective-permute-start.42 = (bf16[128,1024]{1,0:T(8,128)(2,1)}, bf16[128,1024]{1,0:T(8,128)(2,1)}, u32[]{:S(2)}, u32[]{:S(2)}) collective-permute-start(bf16[128,1024]{1,0:T(8,128)(2,1)} %get-tuple-element.356), channel_id=1, source_target_pairs={{0,16},{1,17},{2,18},{3,19},{4,20},{5,21},{6,22},{7,23},{8,24},{9,... | collective-permute-start | bytes 786440 | tf_op jit(solution)/shard_map/ppermute | solution.py:147
  342.9 66.0 %all-to-all-start.5 = ((bf16[32,8,1536]{2,1,0:T(8,128)(2,1)}), bf16[32,8,1536]{2,1,0:T(8,128)(2,1)S(1)}, u32[]{:S(2)}, u32[]{:S(2)}) async-start(bf16[32,8,1536]{2,1,0:T(8,128)(2,1)} %broadcast_in_dim.200), calls=%async_computation.5 | async-start | bytes 1572864 | tf_op jit(solution)/shard_map/all_to_all | solution.py:317
  357.1 42.2 %collective-permute-start.39 = (bf16[4,64,512]{2,1,0:T(8,128)(2,1)}, bf16[4,64,512]{2,1,0:T(8,128)(2,1)S(1)}, u32[]{:S(2)}, u32[]{:S(2)}) collective-permute-start(bf16[4,64,512]{2,1,0:T(8,128)(2,1)} %get-tuple-element.158), channel_id=1, source_target_pairs={{0,6},{1,7},{2,4},{3,5},{4,2},{5,3},{6,0},{7,1},{8,14},{9,15},{10,... | collective-permute-start | bytes 786440 | tf_op jit(solution)/shard_map/ppermute | solution.py:147
  359.9 37.8 %collective-permute-start.38 = (bf16[4,64,2560]{2,1,0:T(8,128)(2,1)S(1)}, bf16[4,64,2560]{2,1,0:T(8,128)(2,1)S(1)}, u32[]{:S(2)}, u32[]{:S(2)}) collective-permute-start(bf16[4,64,2560]{2,1,0:T(8,128)(2,1)S(1)} %pad_maximum_fusion.3), channel_id=1, source_target_pairs={{0,4},{1,5},{2,6},{3,7},{4,0},{5,1},{6,2},{7,3},{8,12},{9,13},{10,... | collective-permute-start | bytes 3932168 | tf_op jit(solution)/shard_map/ppermute | solution.py:147
  360.5 38.8 %collective-permute-start.37 = (bf16[4,64,2560]{2,1,0:T(8,128)(2,1)S(1)}, bf16[4,64,2560]{2,1,0:T(8,128)(2,1)S(1)}, u32[]{:S(2)}, u32[]{:S(2)}) collective-permute-start(bf16[4,64,2560]{2,1,0:T(8,128)(2,1)S(1)} %pad_maximum_fusion.2), channel_id=1, source_target_pairs={{0,2},{1,3},{2,0},{3,1},{4,6},{5,7},{6,4},{7,5},{8,10},{9,11},{10,... | collective-permute-start | bytes 3932168 | tf_op jit(solution)/shard_map/ppermute | solution.py:147
  405.9 33.1 %collective-permute-start.45 = (bf16[64,2560]{1,0:T(8,128)(2,1)S(1)}, bf16[64,2560]{1,0:T(8,128)(2,1)}, u32[]{:S(2)}, u32[]{:S(2)}) collective-permute-start(bf16[64,2560]{1,0:T(8,128)(2,1)S(1)} %get-tuple-element.354), channel_id=1, source_target_pairs={{0,16},{1,17},{2,18},{3,19},{4,20},{5,21},{6,22},{7,23},{8,24},{9,... | collective-permute-start | bytes 983048 | tf_op jit(solution)/shard_map/ppermute | solution.py:147
  417.5 53.0 %all-to-all-start.6 = ((bf16[32,32,768]{2,1,0:T(8,128)(2,1)}), bf16[32,32,768]{2,1,0:T(8,128)(2,1)}, u32[]{:S(2)}, u32[]{:S(2)}) async-start(bf16[32,32,768]{2,1,0:T(8,128)(2,1)} %bitcast.207), calls=%async_computation.6 | async-start | bytes 3145728 | tf_op jit(solution)/shard_map/all_to_all | solution.py:1508
  (96 other events, 1135.5 us)

commit v3 on v2

--- a/solution.py
+++ b/solution.py
@@ -238,7 +238,7 @@
         self.came = [exchange(piece, masks[g]) for g, piece in sent.items()]
         self.came_slant = [exchange(piece, mask) for piece, mask in slant]
 
-    def go_z(self, *hold):
+    def take_xy(self, *hold):
         came = list(self.came)
         if hold:
             came = [tie(array, *hold) for array in came]
@@ -247,7 +247,10 @@
         if self.extra is not None:
             terms = [array[:, :, width:] for array in came] + self.came_slant
             self.own = jnp.concatenate([self.own, total(self.extra[0, 0], terms)], axis=2)
-        self.came_z = [exchange(self.own[m], mask) for m, mask in self.z_masks.items()]
+
+    def go_z(self, *hold):
+        own = tie(self.own, *hold) if hold else self.own
+        self.came_z = [exchange(own[m], mask) for m, mask in self.z_masks.items()]
 
     def result(self, *hold):
         came = list(self.came_z)
@@ -1430,10 +1433,11 @@
     rest_sent = mod_terms(2, 8)
 
     cosine, sine = group_angles(frame_pos, width // 2)
+    flags = jnp.concatenate([is_true.astype(f32), (PD * count).reshape(1)])
     rest_terms = lax.all_to_all(rest_sent, BOTH, 0, 0, tiled=True)
     query, keys, values, attn_in, qkv_b, attn_heads, lse = run_qkv_attend(
         coords, span, noisy_all, embed_b, shift_a, scale_a, cosine, sine, gather_qkv.pieces(),
-        rows, after=(gather_tall.own, rest_sent) + tuple(piece[0] for piece in gather_down.slant),
+        rows, after=(gather_tall.own, rest_sent, flags, head_b) + tuple(piece[0] for piece in gather_down.slant),
     )
     rest_terms = tie(rest_terms, query)
     rest = modulation(rest_terms)
@@ -1455,7 +1459,6 @@
     up_out_other, act_other, part_other = run_up_down(mlp_in_other, up_b, down_b, bf16)
     part_got = exchange(part_other, 1)
     up_out, act, part_own = run_up_down(mlp_in, up_b, down_b, f32, after=(part_other,))
-    flags = jnp.concatenate([is_true.astype(f32), (PD * count).reshape(1)])
     grad_down_out, grad_h2, sums_f, grad_head, losses = run_head(
         flags, hidden1, part_own, part_got, rest, head_b, target
     )
@@ -1475,13 +1478,14 @@
     )
     mlp_got = exchange(mlp_other, 1)
     scatter_down.go_xy()
-    scatter_down.go_z(up_groups[0, 0])
+    scatter_down.take_xy(up_groups[0, 0])
+    scatter_down.go_z()
     grad_attn, proj_mine, proj_theirs, sums_m, embed_h1 = run_proj_back(
         coords, grad_h2, mlp_own, mlp_got, hidden1, proj_out, rest,
         proj_own, proj_other, attn, noisy_own, after=(scatter_down.own,),
     )
     grad_attn = swap_row(grad_attn).reshape(rows, FRAMES, per_frame, width)
-    scatter_up = Scatter(up_groups, grad_attn)
+    scatter_up = Scatter(up_groups, proj_mine)
     proj_groups = run_add_pieces(coords, sizes, (proj_mine, exchange(proj_theirs, 1)))
     scatter_up.go_xy(proj_groups, grad_attn)
 
@@ -1500,27 +1504,20 @@
         span, query, keys, values, attn_heads, grad_attn, lse, cosine, sine,
         after=(proj_groups[0, 0],) + tuple(scatter_up.sent.values()),
     )
-    scatter_up.go_z(grad_qkv)
+    scatter_up.take_xy(grad_qkv)
     grad_qkv_w = run_qkv_dw(
         attn_in, grad_qkv, after=(scatter_up.own, mod_rest, *scatter_down.came_z)
     )
     qkv_terms = grad_qkv_w.reshape(count_dev, part, 3 * width)
     qkv_terms = lax.all_to_all(qkv_terms, BOTH, 0, 0, tiled=True)
+    scatter_up.go_z(qkv_terms)
     sums_a, grad_embed = run_qkv_back(
         noisy_all, embed_b, scale_a, grad_qkv, qkv_b,
-        after=(grad_qkv_w, *scatter_up.came_z),
-    )
-    tall_sum = scatter_up.result()
+        after=(grad_qkv_w,),
+    )
     down_sum = scatter_down.result(sums_a)
     grad_embed = grad_embed + embed_h1
 
-    keep = lax.dynamic_slice_in_dim(tall_sum, core * part, part)
-    got = exchange(to_low(lax.dynamic_slice_in_dim(tall_sum, (1 - core) * part, part)), 1)
-    got = got.astype(f32)
-    pair_sum = jnp.stack([jnp.where(is_zero, keep, got), jnp.where(is_zero, got, keep)], axis=1)
-    up_sum = pair_sum[:, :, :hidden].reshape(part, 2, count_dev // 2, unit)
-    up_sum = up_sum.transpose(0, 2, 1, 3).reshape(part, FF)
-    proj_sum = pair_sum[:, :, hidden:].reshape(part, D)
     small = jnp.concatenate(
         [
             grad_embed.reshape(PD, count_dev, part).transpose(1, 0, 2).reshape(count_dev, -1),
@@ -1544,8 +1541,8 @@
     small = jnp.sum(last[:, FRAMES:].astype(f32), axis=0).reshape(-1)
     embed_sum = small[: PD * part].reshape(PD, part)
     head_sum = small[PD * part : 2 * PD * part].reshape(part, PD)
-    qkv_sum = qkv_terms.reshape(clips, rows, part, 3, width).astype(f32)
-    qkv_sum = to_low(jnp.sum(qkv_sum, axis=0))
+    qkv_sum = tie(qkv_terms, last).reshape(clips, rows, part, 3 * width).astype(f32)
+    qkv_sum = to_low(jnp.sum(qkv_sum, axis=0)).reshape(rows, part, 3, width)
     turned = dot_low("rdgv,wv->dgrw", qkv_sum[:, :, :2], perm)
     straight = qkv_sum[:, :, 2:].transpose(1, 2, 0, 3).astype(f32)
     qkv_sum = jnp.concatenate([turned, straight], axis=1).reshape(part, 3 * D)
@@ -1560,18 +1557,29 @@
     )
 
     fixes = (1.0 - beta_one**STEP, 1.0 - beta_two**STEP)
-    reduced = (
-        embed_sum, grad_table, grad_adaln, qkv_sum, proj_sum, up_sum, down_sum, head_sum.T,
-    )
+    reduced = [
+        embed_sum, grad_table, grad_adaln, qkv_sum, None, None, down_sum, head_sum.T,
+    ]
     turned = (1, 7)
     flip = lambda k, array: jnp.swapaxes(array, -1, -2) if k in turned else array
     weights = [flip(k, array) for k, array in enumerate(masters)]
-    entries = [
-        (weights[k], reduced[k], flip(k, firsts[k]), flip(k, seconds[k])) for k in range(8)
-    ]
     moms, updates, rows_of_sums = [None] * 8, [None] * 8, []
-    for group in ((6,), (4, 5), (3,), (0, 1, 2, 7)):
-        got_moms, got_updates, sums = run_lamb([entries[k] for k in group], group, fixes)
+    for group in ((6,), (3,), (0, 1, 2, 7), (4, 5)):
+        if group == (4, 5):
+            tall_sum = scatter_up.result(rows_of_sums[-1])
+
+            keep = lax.dynamic_slice_in_dim(tall_sum, core * part, part)
+            got = exchange(to_low(lax.dynamic_slice_in_dim(tall_sum, (1 - core) * part, part)), 1)
+            got = got.astype(f32)
+            pair_sum = jnp.stack([jnp.where(is_zero, keep, got), jnp.where(is_zero, got, keep)], axis=1)
+            up_sum = pair_sum[:, :, :hidden].reshape(part, 2, count_dev // 2, unit)
+            up_sum = up_sum.transpose(0, 2, 1, 3).reshape(part, FF)
+            proj_sum = pair_sum[:, :, hidden:].reshape(part, D)
+            reduced[4], reduced[5] = proj_sum, up_sum
+        entries = [
+            (weights[k], reduced[k], flip(k, firsts[k]), flip(k, seconds[k])) for k in group
+        ]
+        got_moms, got_updates, sums = run_lamb(entries, group, fixes)
         rows_of_sums.append(sums)
         for k, mom, update in zip(group, got_moms, got_updates):
             moms[k], updates[k] = flip(k, mom), update

time: 537 us -> 534 us (level)
  Pallas kernels: 190 us -> 225 us
  waiting for transfers between devices: 130 us -> 108 us
  starting transfers between devices: 104 us -> 89.9 us
    ppermute x50, waiting for transfers between devices: 120 us -> 83 us  [exchange(): return lax.ppermute(values, BOTH, [(i, i ^ mask) for i in range(count)])]
    pallas_call x20, Pallas kernels: 190 us -> 225 us  [run_kernel(): return call(*([] if scalars is None else [scalars]), *arrays)]
    all_to_all x1, waiting for transfers between devices: 0.01 us -> 9.09 us  [body(): last = lax.all_to_all(tie(last, qkv_terms), BOTH, 0, 0, tiled=True)]
    all_to_all x1, starting transfers between devices: 11.7 us -> 4 us  [body(): last = lax.all_to_all(tie(last, qkv_terms), BOTH, 0, 0, tiled=True)]
    all_to_all x1, waiting for transfers between devices: 6.79 us -> 13.6 us  [body(): qkv_terms = lax.all_to_all(qkv_terms, BOTH, 0, 0, tiled=True)]
    unnamed x135 -> x145, local copies, waits for them, and re-layouts: 11 us -> 11.6 us
  transfers between devices with their start and end apart: 58 -> 58, of which waited for: 17 -> 17; matrix products, arithmetic and copies ran while one was open for 13% -> 13% of each run, Pallas kernels for 25% -> 33%
where the time goes in v3:
time: 534 us; the launch traced here: 526 us
  Pallas kernels  225 us (42%)
  waiting for transfers between devices  108 us (20%)
  starting transfers between devices  89.9 us (17%)
  local copies, waits for them, and re-layouts  41.9 us (8%)
  other arithmetic  39.7 us (7%)
  blocking collectives  10.7 us (2%)
  matrix products  6.61 us (1%)
    pallas_call x20, Pallas kernels, run_kernel(): return call(*([] if scalars is None else [scalars]), *arrays)  225 us
    ppermute x50, waiting for transfers between devices, exchange(): return lax.ppermute(values, BOTH, [(i, i ^ mask) for i in range(count)])  83 us
    ppermute x50, starting transfers between devices, exchange(): return lax.ppermute(values, BOTH, [(i, i ^ mask) for i in range(count)])  55 us
    all_to_all x1, waiting for transfers between devices, body(): qkv_terms = lax.all_to_all(qkv_terms, BOTH, 0, 0, tiled=True)  13.6 us
    all_to_all x2, starting transfers between devices, spread(): return lax.all_to_all(copies, axes, 0, 0, tiled=True)  11.6 us
    unnamed x145, local copies, waits for them, and re-layouts  11.6 us
    all_to_all x1, blocking collectives, spread(): return lax.all_to_all(copies, axes, 0, 0, tiled=True)  10.7 us
  transfers between devices with their start and end apart: 58, of which 17 were waited for; matrix products, arithmetic and copies ran while one was open for 13% of the time, Pallas kernels for 33%

profile of v3, /device:TPU:0, one launch (start us, length us, event | category | flops | bytes accessed | tf_op | source)
XLA Modules:
  0.0 526.2 jit_solution(341240844245489103)
XLA Ops:
  14.6 6.1 %all-to-all-start = ((f32[32,1,1040]{2,1,0:T(1,128)}), f32[32,1,1040]{2,1,0:T(1,128)S(1)}, u32[]{:S(2)}, u32[]{:S(2)}) async-start(f32[32,1,1040]{2,1,0:T(1,128)} %broadcast_in_dim.182), calls=%async_computation | async-start | bytes 294912 | tf_op jit(solution)/shard_map/all_to_all | solution.py:320
  64.0 13.2 %collective-permute-done.9 = bf16[128,768]{1,0:T(8,128)(2,1)} collective-permute-done((bf16[128,768]{1,0:T(8,128)(2,1)}, bf16[128,768]{1,0:T(8,128)(2,1)}, u32[]{:S(2)}, u32[]{:S(2)}) %collective-permute-start.9) | collective-permute-done | bytes 196640 | tf_op jit(solution)/shard_map/ppermute | solution.py:147
  78.7 13.9 %collective-permute-done.8 = bf16[128,768]{1,0:T(8,128)(2,1)} collective-permute-done((bf16[128,768]{1,0:T(8,128)(2,1)}, bf16[128,768]{1,0:T(8,128)(2,1)}, u32[]{:S(2)}, u32[]{:S(2)}) %collective-permute-start.8) | collective-permute-done | bytes 196640 | tf_op jit(solution)/shard_map/ppermute | solution.py:147
  109.2 14.7 %collective-permute-done.15 = bf16[64,2560]{1,0:T(8,128)(2,1)S(1)} collective-permute-done((bf16[64,2560]{1,0:T(8,128)(2,1)S(1)}, bf16[64,2560]{1,0:T(8,128)(2,1)S(1)}, u32[]{:S(2)}, u32[]{:S(2)}) %collective-permute-start.15) | collective-permute-done | bytes 327712 | tf_op jit(solution)/shard_map/ppermute | solution.py:147
  128.6 43.9 %shard_map.421 = (bf16[2048,256]{1,0:T(8,128)(2,1)}, bf16[2048,256]{1,0:T(8,128)(2,1)}, bf16[2048,256]{1,0:T(8,128)(2,1)}, bf16[2048,1024]{1,0:T(8,128)(2,1)}, b...) custom-call(s32[22]{0:T(128)} %concatenate.81.refs_0_, bf16[2048,16]{1,0:T(8,128)(2,1)} %bitcast.220, ...), custom_call_target="tpu_custom_call" | custom-call | flops 12884901888 | bytes 20971520 | tf_op jit(solution)/shard_map/pallas_call | solution.py:372
  182.9 5.7 %shard_map.423 = (bf16[1024,2048]{1,0:T(8,128)(2,1)}, bf16[1024,512]{1,0:T(8,128)(2,1)}) custom-call(s32[6]{0:T(128)} %stack.95.refs_0_, bf16[4,64,2560]{2,1,0:T(8,128)(2,1)} %copy-done.3, bf16[4,64,2560]{2,1,0:T(8,128)(2,1)} %collective-permute-done.21.refs_2_, bf16[4,64,2560]{2,1,0:T(8,128)(2,1)} %collective-permute-done.22.refs_3_, ...), custom_call_target="tpu_custom_call" | custom-call | bytes 10485760 | tf_op jit(solution)/shard_map/pallas_call | solution.py:372
  198.0 6.2 %shard_map.424 = (f32[512,1024]{1,0:T(8,128)}, f32[512,1024]{1,0:T(8,128)}, bf16[512,1024]{1,0:T(8,128)(2,1)}) custom-call(s32[6]{0:T(128)} %stack.95.refs_0_, bf16[4,512,256]{2,1,0:T(8,128)(2,1)} %copy-done.6, bf16[512,16]{1,0:T(8,128)(2,1)} %get-tuple-element.375.refs_2_.refs_10_, bf16[16,1024]{1,0:T(8,128)(2,1)} %reshape.523.refs_2_.refs_3_.refs_1_, ...), custom_call_target="tpu_custom_call" | custom-call | flops 1073741824 | bytes 10485760 | tf_op jit(solution)/shard_map/pallas_call | solution.py:372
  208.1 10.6 %shard_map.425 = (f32[512,2048]{1,0:T(8,128)}, bf16[512,2048]{1,0:T(8,128)(2,1)}, bf16[512,1024]{1,0:T(8,128)(2,1)}) custom-call(bf16[512,1024]{1,0:T(8,128)(2,1)} %copy-done.62, bf16[1024,2048]{1,0:T(8,128)(2,1)} %get-tuple-element.122.refs_1_.refs_3_.refs_7_, bf16[2048,1024]{1,0:T(8,128)(2,1)} %shard_map.422.refs_5_.refs_2_.refs_1_), custom_call_target="tpu_custom_call" | custom-call | flops 4294967296 | bytes 16777216 | tf_op jit(solution)/shard_map/pallas_call | solution.py:372
  218.8 10.9 %shard_map.426 = (f32[512,2048]{1,0:T(8,128)}, bf16[512,2048]{1,0:T(8,128)(2,1)}, f32[512,1024]{1,0:T(8,128)}) custom-call(bf16[512,1024]{1,0:T(8,128)(2,1)} %get-tuple-element.121.refs_0_.refs_1_, bf16[1024,2048]{1,0:T(8,128)(2,1)} %get-tuple-element.122.refs_1_.refs_3_.refs_7_, bf16[2048,1024]{1,0:T(8,128)(2,1)} %shard_map.422.refs_5_.refs_2_.refs_1_, ...), custom_call_target="tpu_custom_call" | custom-call | flops 4294967296 | bytes 16777216 | tf_op jit(solution)/shard_map/pallas_call | solution.py:372
  230.8 7.2 %shard_map.427 = (bf16[512,1024]{1,0:T(8,128)(2,1)}, f32[512,1024]{1,0:T(8,128)}, f32[8,3072]{1,0:T(8,128)}, f32[1024,16]{1,0:T(8,128)}, f32[4,128]{1,0:T(4,128)}) custom-call(f32[9]{0:T(128)} %pad_maximum_fusion.25.refs_11_.refs_0_, f32[512,1024]{1,0:T(8,128)} %get-tuple-element.126.refs_1_.refs_4_, f32[512,1024]{1,0:T(8,128)} %get-tuple-element.127.refs_2_, ...), custom_call_target="tpu_custom_call" | custom-call | flops 67108864 | bytes 10485760 | tf_op jit(solution)/shard_map/pallas_call | solution.py:372
  241.9 10.2 %shard_map.428 = (bf16[4,128,1024]{2,1,0:T(8,128)(2,1)}, bf16[4,128,1024]{2,1,0:T(8,128)(2,1)}, bf16[4,128,1024]{2,1,0:T(8,128)(2,1)}, bf16[4,128,1024]{2,1,0:T(8,128)(2,1)}) custom-call(s32[6]{0:T(128)} %stack.95.refs_0_, bf16[512,2048]{1,0:T(8,128)(2,1)} %get-tuple-element.124.refs_1_, bf16[512,2048]{1,0:T(8,128)(2,1)} %get-tuple-element.125.refs_2_, ...), custom_call_target="tpu_custom_call" | custom-call | flops 4294967296 | bytes 10485760 | tf_op jit(solution)/shard_map/pallas_call | solution.py:372
  255.0 11.5 %shard_map.429 = (bf16[512,2048]{1,0:T(8,128)(2,1)}, f32[512,1024]{1,0:T(8,128)}) custom-call(bf16[512,1024]{1,0:T(8,128)(2,1)} %get-tuple-element.128.refs_3_.refs_0_, bf16[2048,1024]{1,0:T(8,128)(2,1)} %shard_map.422.refs_5_.refs_2_.refs_1_, f32[512,2048]{1,0:T(8,128)} %get-tuple-element.132.refs_2_, ...), custom_call_target="tpu_custom_call" | custom-call | flops 4294967296 | bytes 16777216 | tf_op jit(solution)/shard_map/pallas_call | solution.py:372
  270.7 17.7 %shard_map.430 = (bf16[512,1024]{1,0:T(8,128)(2,1)}, bf16[4,64,2048]{2,1,0:T(8,128)(2,1)}, bf16[4,64,2048]{2,1,0:T(8,128)(2,1)}, bf16[4,64,2048]{2,1,0:T(8,128)(2,1)}, bf16[4,64,2048]{2,1,0:T(8,128)(2,1)}) custom-call(s32[6]{0:T(128)} %stack.95.refs_0_, bf16[512,1024]{1,0:T(8,128)(2,1)} %get-tuple-element.121.refs_0_.refs_1_, bf16[512,1024]{1,0:T(8,128)(2,1)} %copy-done.62, ...), custom_call_target="tpu_custom_call" | custom-call | flops 8589934592 | bytes 27262976 | tf_op jit(solution)/shard_map/pallas_call | solution.py:372
  296.9 11.3 %shard_map.431 = (bf16[4,512,256]{2,1,0:T(8,128)(2,1)}, bf16[1024,512]{1,0:T(8,128)(2,1)}, bf16[1024,512]{1,0:T(8,128)(2,1)}, f32[8,3072]{1,0:T(8,128)}, f32[16,1024]{1,0:T(8,128)}) custom-call(s32[6]{0:T(128)} %stack.95.refs_0_, f32[512,1024]{1,0:T(8,128)} %get-tuple-element.141.refs_1_, f32[512,1024]{1,0:T(8,128)} %get-tuple-element.142.refs_2_, ...), custom_call_target="tpu_custom_call" | custom-call | flops 2147483648 | bytes 18874368 | tf_op jit(solution)/shard_map/pallas_call | solution.py:372
  321.9 7.7 %collective-permute-done.41 = bf16[8,6144]{1,0:T(8,128)(2,1)S(1)} collective-permute-done((bf16[8,6144]{1,0:T(8,128)(2,1)S(1)}, bf16[8,6144]{1,0:T(8,128)(2,1)S(1)}, u32[]{:S(2)}, u32[]{:S(2)}) %collective-permute-start.41) | collective-permute-done | bytes 98336 | tf_op jit(solution)/shard_map/ppermute | solution.py:147
  337.2 5.6 %all-to-all-start.5 = ((bf16[32,8,1536]{2,1,0:T(8,128)(2,1)}), bf16[32,8,1536]{2,1,0:T(8,128)(2,1)S(1)}, u32[]{:S(2)}, u32[]{:S(2)}) async-start(bf16[32,8,1536]{2,1,0:T(8,128)(2,1)} %broadcast_in_dim.200), calls=%async_computation.5 | async-start | bytes 1572864 | tf_op jit(solution)/shard_map/all_to_all | solution.py:320
  346.5 42.0 %shard_map.433.refs_1_.refs_3_ = bf16[2048,768]{1,0:T(8,128)(2,1)} custom-call(s32[2,8]{1,0:T(2,128)} %copy-done.57, bf16[2048,256]{1,0:T(8,128)(2,1)} %get-tuple-element.117.refs_1_, bf16[2048,256]{1,0:T(8,128)(2,1)} %get-tuple-element.139.refs_2_, bf16[2048,256]{1,0:T(8,128)(2,1)} %get-tuple-element.140.refs_3_, ...), custom_call_target="tpu_custom_call" | custom-call | flops 24159191040 | bytes 12582912 | tf_op jit(solution)/shard_map/pallas_call | solution.py:372
  397.5 7.7 %shard_map.434.refs_5_ = bf16[1024,768]{1,0:T(8,128)(2,1)} custom-call(bf16[2048,1024]{1,0:T(8,128)(2,1)} %get-tuple-element.156.refs_0_, bf16[2048,768]{1,0:T(8,128)(2,1)} %shard_map.433.refs_1_.refs_3_, bf16[4,64,2560]{2,1,0:T(8,128)(2,1)} %pad_maximum_fusion.refs_2_, bf16[32,8,1536]{2,1,0:T(8,128)(2,1)} %copy-done.7, ...), custom_call_target="tpu_custom_call" | custom-call | flops 3221225472 | bytes 10485760 | tf_op jit(solution)/shard_map/pallas_call | solution.py:372
  411.2 11.9 %shard_map.435 = (f32[8,2048]{1,0:T(8,128)}, f32[16,1024]{1,0:T(8,128)}) custom-call(bf16[2048,16]{1,0:T(8,128)(2,1)} %bitcast.221, bf16[16,1024]{1,0:T(8,128)(2,1)} %reshape.523.refs_2_.refs_3_.refs_1_, f32[8,1024]{1,0:T(8,128)} %get-tuple-element.390.refs_4_.refs_2_, bf16[2048,768]{1,0:T(8,128)(2,1)} %shard_map.433.refs_1_.refs_3_, ...), custom_call_target="tpu_custom_call" | custom-call | flops 3221225472 | bytes 8388608 | tf_op jit(solution)/shard_map/pallas_call | solution.py:372
  434.2 13.6 %all-to-all-done.6 = bf16[32,32,768]{2,1,0:T(8,128)(2,1)S(1)} async-done(((bf16[32,32,768]{2,1,0:T(8,128)(2,1)}), bf16[32,32,768]{2,1,0:T(8,128)(2,1)S(1)}, u32[]{:S(2)}, u32[]{:S(2)}) %all-to-all-start.6) | async-done | bytes 1572896 | tf_op jit(solution)/shard_map/all_to_all | solution.py:1512
  458.3 9.1 %all-to-all-done.7 = bf16[32,10,512]{2,1,0:T(8,128)(2,1)} async-done(((bf16[32,10,512]{2,1,0:T(8,128)(2,1)}), bf16[32,10,512]{2,1,0:T(8,128)(2,1)}, u32[]{:S(2)}, u32[]{:S(2)}) %all-to-all-start.7) | async-done | bytes 327712 | tf_op jit(solution)/shard_map/all_to_all | solution.py:1540
  475.1 5.8 %shard_map.438 = (f32[2,16,32]{2,1,0:T(8,128)}, f32[16,32]{1,0:T(8,128)}, f32[2,32,1000]{2,1,0:T(8,128)}, f32[32,1000]{1,0:T(8,128)}, f32[2,32,8192]{2,1,0:T(8,1...) custom-call(f32[16,32]{1,0:T(8,128)} %refs_1_.1, ...), custom_call_target="tpu_custom_call" | custom-call | bytes 8264704 | tf_op jit(solution)/shard_map/pallas_call | solution.py:372
  480.9 13.9 %collective-permute-done.47 = bf16[64,2560]{1,0:T(8,128)(2,1)} collective-permute-done((bf16[64,2560]{1,0:T(8,128)(2,1)}, bf16[64,2560]{1,0:T(8,128)(2,1)}, u32[]{:S(2)}, u32[]{:S(2)}) %collective-permute-start.47) | collective-permute-done | bytes 327712 | tf_op jit(solution)/shard_map/ppermute | solution.py:147
  507.9 10.7 %all_to_all.45 = f32[32,1,128]{2,1,0:T(1,128)S(1)} all-to-all(f32[32,1,128]{2,1,0:T(1,128)S(1)} %broadcast_in_dim.205), channel_id=1, replica_groups=mesh['clip'=8,'row'=4] {'clip','row'}, dimensions={0} | all-to-all | bytes 32768 | tf_op jit(solution)/shard_map/all_to_all | solution.py:320
  (430 shorter events, 210.1 us)
Async XLA Ops:
  2.5 42.4 %collective-permute-start.5 = (bf16[128,1024]{1,0:T(8,128)(2,1)}, bf16[128,1024]{1,0:T(8,128)(2,1)}, u32[]{:S(2)}, u32[]{:S(2)}) collective-permute-start(bf16[128,1024]{1,0:T(8,128)(2,1)} %convert_element_type.299), channel_id=1, source_target_pairs={{0,16},{1,17},{2,18},{3,19},{4,20},{5,21},{6,22},{7,23},{8,24},{9,... | collective-permute-start | bytes 786440 | tf_op jit(solution)/shard_map/ppermute | solution.py:147
  6.5 38.3 %collective-permute-start.4 = (bf16[128,1024]{1,0:T(8,128)(2,1)}, bf16[128,1024]{1,0:T(8,128)(2,1)}, u32[]{:S(2)}, u32[]{:S(2)}) collective-permute-start(bf16[128,1024]{1,0:T(8,128)(2,1)} %convert_element_type.299), channel_id=1, source_target_pairs={{0,8},{1,9},{2,10},{3,11},{4,12},{5,13},{6,14},{7,15},{8,0},{9,1},... | collective-permute-start | bytes 786440 | tf_op jit(solution)/shard_map/ppermute | solution.py:147
  8.1 36.8 %collective-permute-start.6 = (bf16[128,1024]{1,0:T(8,128)(2,1)}, bf16[128,1024]{1,0:T(8,128)(2,1)}, u32[]{:S(2)}, u32[]{:S(2)}) collective-permute-start(bf16[128,1024]{1,0:T(8,128)(2,1)} %convert_element_type.299), channel_id=1, source_target_pairs={{0,24},{1,25},{2,26},{3,27},{4,28},{5,29},{6,30},{7,31},{8,16},{9,... | collective-permute-start | bytes 786440 | tf_op jit(solution)/shard_map/ppermute | solution.py:147
  46.1 49.3 %collective-permute-start.13 = (bf16[4,128,1024]{2,1,0:T(8,128)(2,1)S(1)}, bf16[4,128,1024]{2,1,0:T(8,128)(2,1)S(1)}, u32[]{:S(2)}, u32[]{:S(2)}) collective-permute-start(bf16[4,128,1024]{2,1,0:T(8,128)(2,1)S(1)} %pad_maximum_fusion.4.refs_1_), channel_id=1, source_target_pairs={{0,4},{1,5},{2,6},{3,7},{4,0},{5,1},{6,2},{7,3},{8,12},{9,13},{10,... | collective-permute-start | bytes 3145736 | tf_op jit(solution)/shard_map/ppermute | solution.py:147
  48.0 47.5 %collective-permute-start.12 = (bf16[4,128,1024]{2,1,0:T(8,128)(2,1)S(1)}, bf16[4,128,1024]{2,1,0:T(8,128)(2,1)}, u32[]{:S(2)}, u32[]{:S(2)}) collective-permute-start(bf16[4,128,1024]{2,1,0:T(8,128)(2,1)S(1)} %pad_maximum_fusion.4.refs_1_), channel_id=1, source_target_pairs={{0,2},{1,3},{2,0},{3,1},{4,6},{5,7},{6,4},{7,5},{8,10},{9,11},{10,... | collective-permute-start | bytes 3145736 | tf_op jit(solution)/shard_map/ppermute | solution.py:147
  52.2 120.3 %all-to-all-start.2 = ((bf16[32,8,1536]{2,1,0:T(8,128)(2,1)}), bf16[32,8,1536]{2,1,0:T(8,128)(2,1)S(1)}, u32[]{:S(2)}, u32[]{:S(2)}) async-start(bf16[32,8,1536]{2,1,0:T(8,128)(2,1)} %bitcast.53.refs_10_), calls=%async_computation.2 | async-start | bytes 1572864 | tf_op jit(solution)/shard_map/all_to_all | solution.py:1437
  61.3 31.3 %collective-permute-start.8 = (bf16[128,768]{1,0:T(8,128)(2,1)}, bf16[128,768]{1,0:T(8,128)(2,1)}, u32[]{:S(2)}, u32[]{:S(2)}) collective-permute-start(bf16[128,768]{1,0:T(8,128)(2,1)} %bitcast.41), channel_id=1, source_target_pairs={{0,16},{1,17},{2,18},{3,19},{4,20},{5,21},{6,22},{7,23},{8,24},{9,... | collective-permute-start | bytes 589832 | tf_op jit(solution)/shard_map/ppermute | solution.py:147
  62.5 30.1 %collective-permute-start.7 = (bf16[128,768]{1,0:T(8,128)(2,1)}, bf16[128,768]{1,0:T(8,128)(2,1)S(1)}, u32[]{:S(2)}, u32[]{:S(2)}) collective-permute-start(bf16[128,768]{1,0:T(8,128)(2,1)} %bitcast.41), channel_id=1, source_target_pairs={{0,8},{1,9},{2,10},{3,11},{4,12},{5,13},{6,14},{7,15},{8,0},{9,1},... | collective-permute-start | bytes 589832 | tf_op jit(solution)/shard_map/ppermute | solution.py:147
  93.8 33.3 %collective-permute-start.10 = (bf16[4,128,768]{2,1,0:T(8,128)(2,1)S(1)}, bf16[4,128,768]{2,1,0:T(8,128)(2,1)S(1)}, u32[]{:S(2)}, u32[]{:S(2)}) collective-permute-start(bf16[4,128,768]{2,1,0:T(8,128)(2,1)S(1)} %pad_maximum_fusion.10.refs_7_), channel_id=1, source_target_pairs={{0,4},{1,5},{2,6},{3,7},{4,0},{5,1},{6,2},{7,3},{8,12},{9,13},{10,... | collective-permute-start | bytes 2359304 | tf_op jit(solution)/shard_map/ppermute | solution.py:147
  96.8 27.0 %collective-permute-start.15 = (bf16[64,2560]{1,0:T(8,128)(2,1)S(1)}, bf16[64,2560]{1,0:T(8,128)(2,1)S(1)}, u32[]{:S(2)}, u32[]{:S(2)}) collective-permute-start(bf16[64,2560]{1,0:T(8,128)(2,1)S(1)} %copy-done.13), channel_id=1, source_target_pairs={{0,16},{1,17},{2,18},{3,19},{4,20},{5,21},{6,22},{7,23},{8,24},{9,... | collective-permute-start | bytes 983048 | tf_op jit(solution)/shard_map/ppermute | solution.py:147
  96.9 27.0 %collective-permute-start.14 = (bf16[64,2560]{1,0:T(8,128)(2,1)S(1)}, bf16[64,2560]{1,0:T(8,128)(2,1)S(1)}, u32[]{:S(2)}, u32[]{:S(2)}) collective-permute-start(bf16[64,2560]{1,0:T(8,128)(2,1)S(1)} %copy-done.13), channel_id=1, source_target_pairs={{0,8},{1,9},{2,10},{3,11},{4,12},{5,13},{6,14},{7,15},{8,0},{9,1},... | collective-permute-start | bytes 983048 | tf_op jit(solution)/shard_map/ppermute | solution.py:147
  100.0 27.6 %collective-permute-start.18 = (bf16[2,128,1024]{2,1,0:T(8,128)(2,1)S(1)}, bf16[2,128,1024]{2,1,0:T(8,128)(2,1)S(1)}, u32[]{:S(2)}, u32[]{:S(2)}) collective-permute-start(bf16[2,128,1024]{2,1,0:T(8,128)(2,1)S(1)} %slice.219), channel_id=1, source_target_pairs={{0,2},{1,3},{2,0},{3,1},{4,6},{5,7},{6,4},{7,5},{8,10},{9,11},{10,... | collective-permute-start | bytes 1572872 | tf_op jit(solution)/shard_map/ppermute | solution.py:147
  124.1 58.7 %collective-permute-start.23 = (bf16[4,64,2560]{2,1,0:T(8,128)(2,1)S(1)}, bf16[4,64,2560]{2,1,0:T(8,128)(2,1)}, u32[]{:S(2)}, u32[]{:S(2)}) collective-permute-start(bf16[4,64,2560]{2,1,0:T(8,128)(2,1)S(1)} %pad_maximum_fusion.1.refs_9_.refs_1_), channel_id=1, source_target_pairs={{0,6},{1,7},{2,4},{3,5},{4,2},{5,3},{6,0},{7,1},{8,14},{9,15},{10,... | collective-permute-start | bytes 3932168 | tf_op jit(solution)/shard_map/ppermute | solution.py:147
  125.5 57.5 %collective-permute-start.22 = (bf16[4,64,2560]{2,1,0:T(8,128)(2,1)S(1)}, bf16[4,64,2560]{2,1,0:T(8,128)(2,1)}, u32[]{:S(2)}, u32[]{:S(2)}) collective-permute-start(bf16[4,64,2560]{2,1,0:T(8,128)(2,1)S(1)} %pad_maximum_fusion.1.refs_9_.refs_1_), channel_id=1, source_target_pairs={{0,4},{1,5},{2,6},{3,7},{4,0},{5,1},{6,2},{7,3},{8,12},{9,13},{10,... | collective-permute-start | bytes 3932168 | tf_op jit(solution)/shard_map/ppermute | solution.py:147
  127.1 55.8 %collective-permute-start.21 = (bf16[4,64,2560]{2,1,0:T(8,128)(2,1)S(1)}, bf16[4,64,2560]{2,1,0:T(8,128)(2,1)}, u32[]{:S(2)}, u32[]{:S(2)}) collective-permute-start(bf16[4,64,2560]{2,1,0:T(8,128)(2,1)S(1)} %pad_maximum_fusion.1.refs_9_.refs_1_), channel_id=1, source_target_pairs={{0,2},{1,3},{2,0},{3,1},{4,6},{5,7},{6,4},{7,5},{8,10},{9,11},{10,... | collective-permute-start | bytes 3932168 | tf_op jit(solution)/shard_map/ppermute | solution.py:147
  313.7 80.2 %collective-permute-start.43 = (bf16[128,1024]{1,0:T(8,128)(2,1)}, bf16[128,1024]{1,0:T(8,128)(2,1)}, u32[]{:S(2)}, u32[]{:S(2)}) collective-permute-start(bf16[128,1024]{1,0:T(8,128)(2,1)} %get-tuple-element.365), channel_id=1, source_target_pairs={{0,24},{1,25},{2,26},{3,27},{4,28},{5,29},{6,30},{7,31},{8,16},{9,... | collective-permute-start | bytes 786440 | tf_op jit(solution)/shard_map/ppermute | solution.py:147
  315.3 78.6 %collective-permute-start.42 = (bf16[128,1024]{1,0:T(8,128)(2,1)}, bf16[128,1024]{1,0:T(8,128)(2,1)}, u32[]{:S(2)}, u32[]{:S(2)}) collective-permute-start(bf16[128,1024]{1,0:T(8,128)(2,1)} %get-tuple-element.366), channel_id=1, source_target_pairs={{0,16},{1,17},{2,18},{3,19},{4,20},{5,21},{6,22},{7,23},{8,24},{9,... | collective-permute-start | bytes 786440 | tf_op jit(solution)/shard_map/ppermute | solution.py:147
  337.2 59.4 %all-to-all-start.5 = ((bf16[32,8,1536]{2,1,0:T(8,128)(2,1)}), bf16[32,8,1536]{2,1,0:T(8,128)(2,1)S(1)}, u32[]{:S(2)}, u32[]{:S(2)}) async-start(bf16[32,8,1536]{2,1,0:T(8,128)(2,1)} %broadcast_in_dim.200), calls=%async_computation.5 | async-start | bytes 1572864 | tf_op jit(solution)/shard_map/all_to_all | solution.py:320
  342.9 46.7 %collective-permute-start.39 = (bf16[4,64,512]{2,1,0:T(8,128)(2,1)S(1)}, bf16[4,64,512]{2,1,0:T(8,128)(2,1)S(1)}, u32[]{:S(2)}, u32[]{:S(2)}) collective-permute-start(bf16[4,64,512]{2,1,0:T(8,128)(2,1)S(1)} %copy-done.66), channel_id=1, source_target_pairs={{0,6},{1,7},{2,4},{3,5},{4,2},{5,3},{6,0},{7,1},{8,14},{9,15},{10,... | collective-permute-start | bytes 786440 | tf_op jit(solution)/shard_map/ppermute | solution.py:147
  345.8 42.7 %collective-permute-start.38 = (bf16[4,64,2560]{2,1,0:T(8,128)(2,1)S(1)}, bf16[4,64,2560]{2,1,0:T(8,128)(2,1)S(1)}, u32[]{:S(2)}, u32[]{:S(2)}) collective-permute-start(bf16[4,64,2560]{2,1,0:T(8,128)(2,1)S(1)} %pad_maximum_fusion.3), channel_id=1, source_target_pairs={{0,4},{1,5},{2,6},{3,7},{4,0},{5,1},{6,2},{7,3},{8,12},{9,13},{10,... | collective-permute-start | bytes 3932168 | tf_op jit(solution)/shard_map/ppermute | solution.py:147
  346.3 43.3 %collective-permute-start.37 = (bf16[4,64,2560]{2,1,0:T(8,128)(2,1)S(1)}, bf16[4,64,2560]{2,1,0:T(8,128)(2,1)S(1)}, u32[]{:S(2)}, u32[]{:S(2)}) collective-permute-start(bf16[4,64,2560]{2,1,0:T(8,128)(2,1)S(1)} %copy-done.14), channel_id=1, source_target_pairs={{0,2},{1,3},{2,0},{3,1},{4,6},{5,7},{6,4},{7,5},{8,10},{9,11},{10,... | collective-permute-start | bytes 3932168 | tf_op jit(solution)/shard_map/ppermute | solution.py:147
  405.2 42.6 %all-to-all-start.6 = ((bf16[32,32,768]{2,1,0:T(8,128)(2,1)}), bf16[32,32,768]{2,1,0:T(8,128)(2,1)S(1)}, u32[]{:S(2)}, u32[]{:S(2)}) async-start(bf16[32,32,768]{2,1,0:T(8,128)(2,1)} %bitcast.209), calls=%async_computation.6 | async-start | bytes 3145728 | tf_op jit(solution)/shard_map/all_to_all | solution.py:1512
  454.0 41.2 %collective-permute-start.46 = (bf16[64,2560]{1,0:T(8,128)(2,1)}, bf16[64,2560]{1,0:T(8,128)(2,1)}, u32[]{:S(2)}, u32[]{:S(2)}) collective-permute-start(bf16[64,2560]{1,0:T(8,128)(2,1)} %get-tuple-element.362), channel_id=1, source_target_pairs={{0,8},{1,9},{2,10},{3,11},{4,12},{5,13},{6,14},{7,15},{8,0},{9,1},... | collective-permute-start | bytes 983048 | tf_op jit(solution)/shard_map/ppermute | solution.py:147
  458.2 36.7 %collective-permute-start.47 = (bf16[64,2560]{1,0:T(8,128)(2,1)}, bf16[64,2560]{1,0:T(8,128)(2,1)}, u32[]{:S(2)}, u32[]{:S(2)}) collective-permute-start(bf16[64,2560]{1,0:T(8,128)(2,1)} %get-tuple-element.364), channel_id=1, source_target_pairs={{0,16},{1,17},{2,18},{3,19},{4,20},{5,21},{6,22},{7,23},{8,24},{9,... | collective-permute-start | bytes 983048 | tf_op jit(solution)/shard_map/ppermute | solution.py:147
  (101 other events, 1214.4 us)

commit v4 on v3

--- a/solution.py
+++ b/solution.py
@@ -249,8 +249,10 @@
             self.own = jnp.concatenate([self.own, total(self.extra[0, 0], terms)], axis=2)
 
     def go_z(self, *hold):
-        own = tie(self.own, *hold) if hold else self.own
-        self.came_z = [exchange(own[m], mask) for m, mask in self.z_masks.items()]
+        parts = {m: self.own[m] for m in self.z_masks}
+        if hold:
+            parts = {m: tie(part, *hold) for m, part in parts.items()}
+        self.came_z = [exchange(parts[m], mask) for m, mask in self.z_masks.items()]
 
     def result(self, *hold):
         came = list(self.came_z)
@@ -1537,7 +1539,9 @@
         ],
         axis=1,
     )
-    last = lax.all_to_all(tie(last, qkv_terms), BOTH, 0, 0, tiled=True)
+    fixes = (1.0 - beta_one**STEP, 1.0 - beta_two**STEP)
+    early = run_lamb([(down_w, down_sum, down_avg, down_sq)], (6,), fixes)
+    last = lax.all_to_all(tie(last, qkv_terms, early[2]), BOTH, 0, 0, tiled=True)
     small = jnp.sum(last[:, FRAMES:].astype(f32), axis=0).reshape(-1)
     embed_sum = small[: PD * part].reshape(PD, part)
     head_sum = small[PD * part : 2 * PD * part].reshape(part, PD)
@@ -1556,7 +1560,6 @@
         "fl,fd->dl", one_hot, grad_cond, precision=precise, preferred_element_type=f32
     )
 
-    fixes = (1.0 - beta_one**STEP, 1.0 - beta_two**STEP)
     reduced = [
         embed_sum, grad_table, grad_adaln, qkv_sum, None, None, down_sum, head_sum.T,
     ]
@@ -1566,7 +1569,7 @@
     moms, updates, rows_of_sums = [None] * 8, [None] * 8, []
     for group in ((6,), (3,), (0, 1, 2, 7), (4, 5)):
         if group == (4, 5):
-            tall_sum = scatter_up.result(rows_of_sums[-1])
+            tall_sum = scatter_up.result(*rows_of_sums)
 
             keep = lax.dynamic_slice_in_dim(tall_sum, core * part, part)
             got = exchange(to_low(lax.dynamic_slice_in_dim(tall_sum, (1 - core) * part, part)), 1)
@@ -1579,7 +1582,7 @@
         entries = [
             (weights[k], reduced[k], flip(k, firsts[k]), flip(k, seconds[k])) for k in group
         ]
-        got_moms, got_updates, sums = run_lamb(entries, group, fixes)
+        got_moms, got_updates, sums = early if group == (6,) else run_lamb(entries, group, fixes)
         rows_of_sums.append(sums)
         for k, mom, update in zip(group, got_moms, got_updates):
             moms[k], updates[k] = flip(k, mom), update

time: 534 us -> 530 us (level)
  Pallas kernels: 225 us -> 198 us
  waiting for transfers between devices: 108 us -> 122 us
  blocking collectives: 10.7 us -> 16.3 us
    pallas_call x20, Pallas kernels: 225 us -> 198 us  [run_kernel(): return call(*([] if scalars is None else [scalars]), *arrays)]
    ppermute x50, waiting for transfers between devices: 83 us -> 96.6 us  [exchange(): return lax.ppermute(values, BOTH, [(i, i ^ mask) for i in range(count)])]
    all_to_all x1, blocking collectives: 10.7 us -> 16.3 us  [spread(): return lax.all_to_all(copies, axes, 0, 0, tiled=True)]
    unnamed x145 -> x141, local copies, waits for them, and re-layouts: 11.6 us -> 11.6 us
  transfers between devices with their start and end apart: 58 -> 58, of which waited for: 17 -> 19; matrix products, arithmetic and copies ran while one was open for 13% -> 14% of each run, Pallas kernels for 33% -> 28%
where the time goes in v4:
time: 530 us; the launch traced here: 522 us
  Pallas kernels  198 us (37%)
  waiting for transfers between devices  122 us (23%)
  starting transfers between devices  91 us (17%)
  other arithmetic  43 us (8%)
  local copies, waits for them, and re-layouts  40.6 us (8%)
  blocking collectives  16.3 us (3%)
  matrix products  6.69 us (1%)
    pallas_call x20, Pallas kernels, run_kernel(): return call(*([] if scalars is None else [scalars]), *arrays)  198 us
    ppermute x50, waiting for transfers between devices, exchange(): return lax.ppermute(values, BOTH, [(i, i ^ mask) for i in range(count)])  96.6 us
    ppermute x50, starting transfers between devices, exchange(): return lax.ppermute(values, BOTH, [(i, i ^ mask) for i in range(count)])  56.7 us
    all_to_all x1, blocking collectives, spread(): return lax.all_to_all(copies, axes, 0, 0, tiled=True)  16.3 us
    all_to_all x1, waiting for transfers between devices, body(): qkv_terms = lax.all_to_all(qkv_terms, BOTH, 0, 0, tiled=True)  13.2 us
    unnamed x141, local copies, waits for them, and re-layouts  11.6 us
  transfers between devices with their start and end apart: 58, of which 19 were waited for; matrix products, arithmetic and copies ran while one was open for 14% of the time, Pallas kernels for 28%

profile of v4, /device:TPU:0, one launch (start us, length us, event | category | flops | bytes accessed | tf_op | source)
XLA Modules:
  0.0 521.7 jit_solution(11231916029903421063)
XLA Ops:
  14.6 6.1 %all-to-all-start = ((f32[32,1,1040]{2,1,0:T(1,128)}), f32[32,1,1040]{2,1,0:T(1,128)S(1)}, u32[]{:S(2)}, u32[]{:S(2)}) async-start(f32[32,1,1040]{2,1,0:T(1,128)} %broadcast_in_dim.182), calls=%async_computation | async-start | bytes 294912 | tf_op jit(solution)/shard_map/all_to_all | solution.py:322
  64.4 13.2 %collective-permute-done.9 = bf16[128,768]{1,0:T(8,128)(2,1)} collective-permute-done((bf16[128,768]{1,0:T(8,128)(2,1)}, bf16[128,768]{1,0:T(8,128)(2,1)}, u32[]{:S(2)}, u32[]{:S(2)}) %collective-permute-start.9) | collective-permute-done | bytes 196640 | tf_op jit(solution)/shard_map/ppermute | solution.py:147
  79.2 13.9 %collective-permute-done.8 = bf16[128,768]{1,0:T(8,128)(2,1)} collective-permute-done((bf16[128,768]{1,0:T(8,128)(2,1)}, bf16[128,768]{1,0:T(8,128)(2,1)}, u32[]{:S(2)}, u32[]{:S(2)}) %collective-permute-start.8) | collective-permute-done | bytes 196640 | tf_op jit(solution)/shard_map/ppermute | solution.py:147
  109.7 14.7 %collective-permute-done.15 = bf16[64,2560]{1,0:T(8,128)(2,1)S(1)} collective-permute-done((bf16[64,2560]{1,0:T(8,128)(2,1)S(1)}, bf16[64,2560]{1,0:T(8,128)(2,1)S(1)}, u32[]{:S(2)}, u32[]{:S(2)}) %collective-permute-start.15) | collective-permute-done | bytes 327712 | tf_op jit(solution)/shard_map/ppermute | solution.py:147
  129.1 32.6 %shard_map.421 = (bf16[2048,256]{1,0:T(8,128)(2,1)}, bf16[2048,256]{1,0:T(8,128)(2,1)}, bf16[2048,256]{1,0:T(8,128)(2,1)}, bf16[2048,1024]{1,0:T(8,128)(2,1)}, b...) custom-call(s32[22]{0:T(128)} %concatenate.81.refs_0_, bf16[2048,16]{1,0:T(8,128)(2,1)} %bitcast.220, ...), custom_call_target="tpu_custom_call" | custom-call | flops 12884901888 | bytes 20971520 | tf_op jit(solution)/shard_map/pallas_call | solution.py:374
  172.0 11.5 %collective-permute-done.22.refs_3_ = bf16[4,64,2560]{2,1,0:T(8,128)(2,1)} collective-permute-done((bf16[4,64,2560]{2,1,0:T(8,128)(2,1)S(1)}, bf16[4,64,2560]{2,1,0:T(8,128)(2,1)}, u32[]{:S(2)}, u32[]{:S(2)}) %collective-permute-start.22) | collective-permute-done | bytes 1310752 | tf_op jit(solution)/shard_map/ppermute | solution.py:147
  183.4 5.7 %shard_map.423 = (bf16[1024,2048]{1,0:T(8,128)(2,1)}, bf16[1024,512]{1,0:T(8,128)(2,1)}) custom-call(s32[6]{0:T(128)} %stack.95.refs_0_, bf16[4,64,2560]{2,1,0:T(8,128)(2,1)} %copy-done.3, bf16[4,64,2560]{2,1,0:T(8,128)(2,1)} %collective-permute-done.21.refs_2_, bf16[4,64,2560]{2,1,0:T(8,128)(2,1)} %collective-permute-done.22.refs_3_, ...), custom_call_target="tpu_custom_call" | custom-call | bytes 10485760 | tf_op jit(solution)/shard_map/pallas_call | solution.py:374
  198.5 6.2 %shard_map.424 = (f32[512,1024]{1,0:T(8,128)}, f32[512,1024]{1,0:T(8,128)}, bf16[512,1024]{1,0:T(8,128)(2,1)}) custom-call(s32[6]{0:T(128)} %stack.95.refs_0_, bf16[4,512,256]{2,1,0:T(8,128)(2,1)} %copy-done.6, bf16[512,16]{1,0:T(8,128)(2,1)} %get-tuple-element.379.refs_2_.refs_10_, bf16[16,1024]{1,0:T(8,128)(2,1)} %reshape.523.refs_2_.refs_3_.refs_1_, ...), custom_call_target="tpu_custom_call" | custom-call | flops 1073741824 | bytes 10485760 | tf_op jit(solution)/shard_map/pallas_call | solution.py:374
  208.6 10.6 %shard_map.425 = (f32[512,2048]{1,0:T(8,128)}, bf16[512,2048]{1,0:T(8,128)(2,1)}, bf16[512,1024]{1,0:T(8,128)(2,1)}) custom-call(bf16[512,1024]{1,0:T(8,128)(2,1)} %copy-done.61, bf16[1024,2048]{1,0:T(8,128)(2,1)} %get-tuple-element.124.refs_1_.refs_3_.refs_7_, bf16[2048,1024]{1,0:T(8,128)(2,1)} %shard_map.422.refs_5_.refs_2_.refs_1_), custom_call_target="tpu_custom_call" | custom-call | flops 4294967296 | bytes 16777216 | tf_op jit(solution)/shard_map/pallas_call | solution.py:374
  219.4 10.9 %shard_map.426 = (f32[512,2048]{1,0:T(8,128)}, bf16[512,2048]{1,0:T(8,128)(2,1)}, f32[512,1024]{1,0:T(8,128)}) custom-call(bf16[512,1024]{1,0:T(8,128)(2,1)} %get-tuple-element.123.refs_0_.refs_1_, bf16[1024,2048]{1,0:T(8,128)(2,1)} %get-tuple-element.124.refs_1_.refs_3_.refs_7_, bf16[2048,1024]{1,0:T(8,128)(2,1)} %shard_map.422.refs_5_.refs_2_.refs_1_, ...), custom_call_target="tpu_custom_call" | custom-call | flops 4294967296 | bytes 16777216 | tf_op jit(solution)/shard_map/pallas_call | solution.py:374
  231.3 7.2 %shard_map.427 = (bf16[512,1024]{1,0:T(8,128)(2,1)}, f32[512,1024]{1,0:T(8,128)}, f32[8,3072]{1,0:T(8,128)}, f32[1024,16]{1,0:T(8,128)}, f32[4,128]{1,0:T(4,128)}) custom-call(f32[9]{0:T(128)} %pad_maximum_fusion.25.refs_11_.refs_0_, f32[512,1024]{1,0:T(8,128)} %get-tuple-element.128.refs_1_.refs_4_, f32[512,1024]{1,0:T(8,128)} %get-tuple-element.129.refs_2_, ...), custom_call_target="tpu_custom_call" | custom-call | flops 67108864 | bytes 10485760 | tf_op jit(solution)/shard_map/pallas_call | solution.py:374
  242.4 10.1 %shard_map.428 = (bf16[4,128,1024]{2,1,0:T(8,128)(2,1)}, bf16[4,128,1024]{2,1,0:T(8,128)(2,1)}, bf16[4,128,1024]{2,1,0:T(8,128)(2,1)}, bf16[4,128,1024]{2,1,0:T(8,128)(2,1)}) custom-call(s32[6]{0:T(128)} %stack.95.refs_0_, bf16[512,2048]{1,0:T(8,128)(2,1)} %get-tuple-element.126.refs_1_, bf16[512,2048]{1,0:T(8,128)(2,1)} %get-tuple-element.127.refs_2_, ...), custom_call_target="tpu_custom_call" | custom-call | flops 4294967296 | bytes 10485760 | tf_op jit(solution)/shard_map/pallas_call | solution.py:374
  255.6 11.5 %shard_map.429 = (bf16[512,2048]{1,0:T(8,128)(2,1)}, f32[512,1024]{1,0:T(8,128)}) custom-call(bf16[512,1024]{1,0:T(8,128)(2,1)} %get-tuple-element.130.refs_3_.refs_0_, bf16[2048,1024]{1,0:T(8,128)(2,1)} %shard_map.422.refs_5_.refs_2_.refs_1_, f32[512,2048]{1,0:T(8,128)} %get-tuple-element.134.refs_2_, ...), custom_call_target="tpu_custom_call" | custom-call | flops 4294967296 | bytes 16777216 | tf_op jit(solution)/shard_map/pallas_call | solution.py:374
  271.3 17.7 %shard_map.430 = (bf16[512,1024]{1,0:T(8,128)(2,1)}, bf16[4,64,2048]{2,1,0:T(8,128)(2,1)}, bf16[4,64,2048]{2,1,0:T(8,128)(2,1)}, bf16[4,64,2048]{2,1,0:T(8,128)(2,1)}, bf16[4,64,2048]{2,1,0:T(8,128)(2,1)}) custom-call(s32[6]{0:T(128)} %stack.95.refs_0_, bf16[512,1024]{1,0:T(8,128)(2,1)} %get-tuple-element.123.refs_0_.refs_1_, bf16[512,1024]{1,0:T(8,128)(2,1)} %copy-done.61, ...), custom_call_target="tpu_custom_call" | custom-call | flops 8589934592 | bytes 27262976 | tf_op jit(solution)/shard_map/pallas_call | solution.py:374
  297.4 11.3 %shard_map.431 = (bf16[4,512,256]{2,1,0:T(8,128)(2,1)}, bf16[1024,512]{1,0:T(8,128)(2,1)}, bf16[1024,512]{1,0:T(8,128)(2,1)}, f32[8,3072]{1,0:T(8,128)}, f32[16,1024]{1,0:T(8,128)}) custom-call(s32[6]{0:T(128)} %stack.95.refs_0_, f32[512,1024]{1,0:T(8,128)} %get-tuple-element.143.refs_1_, f32[512,1024]{1,0:T(8,128)} %get-tuple-element.144.refs_2_, ...), custom_call_target="tpu_custom_call" | custom-call | flops 2147483648 | bytes 18874368 | tf_op jit(solution)/shard_map/pallas_call | solution.py:374
  323.6 6.5 %collective-permute-done.41 = bf16[8,6144]{1,0:T(8,128)(2,1)S(1)} collective-permute-done((bf16[8,6144]{1,0:T(8,128)(2,1)S(1)}, bf16[8,6144]{1,0:T(8,128)(2,1)S(1)}, u32[]{:S(2)}, u32[]{:S(2)}) %collective-permute-start.41) | collective-permute-done | bytes 98336 | tf_op jit(solution)/shard_map/ppermute | solution.py:147
  346.0 26.3 %shard_map.433.refs_1_.refs_3_ = bf16[2048,768]{1,0:T(8,128)(2,1)} custom-call(s32[2,8]{1,0:T(2,128)} %copy-done.56, bf16[2048,256]{1,0:T(8,128)(2,1)} %get-tuple-element.119.refs_1_, bf16[2048,256]{1,0:T(8,128)(2,1)} %get-tuple-element.141.refs_2_, bf16[2048,256]{1,0:T(8,128)(2,1)} %get-tuple-element.142.refs_3_, ...), custom_call_target="tpu_custom_call" | custom-call | flops 24159191040 | bytes 12582912 | tf_op jit(solution)/shard_map/pallas_call | solution.py:374
  372.2 15.7 %collective-permute-done.38 = bf16[4,64,2560]{2,1,0:T(8,128)(2,1)S(1)} collective-permute-done((bf16[4,64,2560]{2,1,0:T(8,128)(2,1)S(1)}, bf16[4,64,2560]{2,1,0:T(8,128)(2,1)S(1)}, u32[]{:S(2)}, u32[]{:S(2)}) %collective-permute-start.38) | collective-permute-done | bytes 1310752 | tf_op jit(solution)/shard_map/ppermute | solution.py:147
  396.8 7.7 %shard_map.434.refs_5_ = bf16[1024,768]{1,0:T(8,128)(2,1)} custom-call(bf16[2048,1024]{1,0:T(8,128)(2,1)} %get-tuple-element.158.refs_0_, bf16[2048,768]{1,0:T(8,128)(2,1)} %shard_map.433.refs_1_.refs_3_, bf16[4,64,2560]{2,1,0:T(8,128)(2,1)} %pad_maximum_fusion.refs_2_, bf16[32,8,1536]{2,1,0:T(8,128)(2,1)} %copy-done.7, ...), custom_call_target="tpu_custom_call" | custom-call | flops 3221225472 | bytes 10485760 | tf_op jit(solution)/shard_map/pallas_call | solution.py:374
  410.8 11.9 %shard_map.435 = (f32[8,2048]{1,0:T(8,128)}, f32[16,1024]{1,0:T(8,128)}) custom-call(bf16[2048,16]{1,0:T(8,128)(2,1)} %bitcast.221, bf16[16,1024]{1,0:T(8,128)(2,1)} %reshape.523.refs_2_.refs_3_.refs_1_, f32[8,1024]{1,0:T(8,128)} %get-tuple-element.394.refs_4_.refs_2_, bf16[2048,768]{1,0:T(8,128)(2,1)} %shard_map.433.refs_1_.refs_3_, ...), custom_call_target="tpu_custom_call" | custom-call | flops 3221225472 | bytes 8388608 | tf_op jit(solution)/shard_map/pallas_call | solution.py:374
  433.9 13.2 %all-to-all-done.6 = bf16[32,32,768]{2,1,0:T(8,128)(2,1)S(1)} async-done(((bf16[32,32,768]{2,1,0:T(8,128)(2,1)}), bf16[32,32,768]{2,1,0:T(8,128)(2,1)S(1)}, u32[]{:S(2)}, u32[]{:S(2)}) %all-to-all-start.6) | async-done | bytes 1572896 | tf_op jit(solution)/shard_map/all_to_all | solution.py:1514
  456.5 10.1 %all-to-all-done.7 = bf16[32,10,512]{2,1,0:T(8,128)(2,1)} async-done(((bf16[32,10,512]{2,1,0:T(8,128)(2,1)}), bf16[32,10,512]{2,1,0:T(8,128)(2,1)}, u32[]{:S(2)}, u32[]{:S(2)}) %all-to-all-start.7) | async-done | bytes 327712 | tf_op jit(solution)/shard_map/all_to_all | solution.py:1544
  480.3 5.8 %shard_map.438 = (f32[2,16,32]{2,1,0:T(8,128)}, f32[16,32]{1,0:T(8,128)}, f32[2,32,1000]{2,1,0:T(8,128)}, f32[32,1000]{1,0:T(8,128)}, f32[2,32,8192]{2,1,0:T(8,1...) custom-call(f32[16,32]{1,0:T(8,128)} %refs_1_.1, ...), custom_call_target="tpu_custom_call" | custom-call | bytes 8264704 | tf_op jit(solution)/shard_map/pallas_call | solution.py:374
  497.8 16.3 %all_to_all.45 = f32[32,1,128]{2,1,0:T(1,128)S(1)} all-to-all(f32[32,1,128]{2,1,0:T(1,128)S(1)} %broadcast_in_dim.205), channel_id=1, replica_groups=mesh['clip'=8,'row'=4] {'clip','row'}, dimensions={0} | all-to-all | bytes 32768 | tf_op jit(solution)/shard_map/all_to_all | solution.py:322
  (426 shorter events, 220.0 us)
Async XLA Ops:
  2.5 42.9 %collective-permute-start.5 = (bf16[128,1024]{1,0:T(8,128)(2,1)}, bf16[128,1024]{1,0:T(8,128)(2,1)}, u32[]{:S(2)}, u32[]{:S(2)}) collective-permute-start(bf16[128,1024]{1,0:T(8,128)(2,1)} %convert_element_type.299), channel_id=1, source_target_pairs={{0,16},{1,17},{2,18},{3,19},{4,20},{5,21},{6,22},{7,23},{8,24},{9,... | collective-permute-start | bytes 786440 | tf_op jit(solution)/shard_map/ppermute | solution.py:147
  6.5 38.8 %collective-permute-start.4 = (bf16[128,1024]{1,0:T(8,128)(2,1)}, bf16[128,1024]{1,0:T(8,128)(2,1)}, u32[]{:S(2)}, u32[]{:S(2)}) collective-permute-start(bf16[128,1024]{1,0:T(8,128)(2,1)} %convert_element_type.299), channel_id=1, source_target_pairs={{0,8},{1,9},{2,10},{3,11},{4,12},{5,13},{6,14},{7,15},{8,0},{9,1},... | collective-permute-start | bytes 786440 | tf_op jit(solution)/shard_map/ppermute | solution.py:147
  8.1 37.3 %collective-permute-start.6 = (bf16[128,1024]{1,0:T(8,128)(2,1)}, bf16[128,1024]{1,0:T(8,128)(2,1)}, u32[]{:S(2)}, u32[]{:S(2)}) collective-permute-start(bf16[128,1024]{1,0:T(8,128)(2,1)} %convert_element_type.299), channel_id=1, source_target_pairs={{0,24},{1,25},{2,26},{3,27},{4,28},{5,29},{6,30},{7,31},{8,16},{9,... | collective-permute-start | bytes 786440 | tf_op jit(solution)/shard_map/ppermute | solution.py:147
  46.6 49.3 %collective-permute-start.13 = (bf16[4,128,1024]{2,1,0:T(8,128)(2,1)S(1)}, bf16[4,128,1024]{2,1,0:T(8,128)(2,1)S(1)}, u32[]{:S(2)}, u32[]{:S(2)}) collective-permute-start(bf16[4,128,1024]{2,1,0:T(8,128)(2,1)S(1)} %pad_maximum_fusion.4.refs_1_), channel_id=1, source_target_pairs={{0,4},{1,5},{2,6},{3,7},{4,0},{5,1},{6,2},{7,3},{8,12},{9,13},{10,... | collective-permute-start | bytes 3145736 | tf_op jit(solution)/shard_map/ppermute | solution.py:147
  48.5 47.5 %collective-permute-start.12 = (bf16[4,128,1024]{2,1,0:T(8,128)(2,1)S(1)}, bf16[4,128,1024]{2,1,0:T(8,128)(2,1)}, u32[]{:S(2)}, u32[]{:S(2)}) collective-permute-start(bf16[4,128,1024]{2,1,0:T(8,128)(2,1)S(1)} %pad_maximum_fusion.4.refs_1_), channel_id=1, source_target_pairs={{0,2},{1,3},{2,0},{3,1},{4,6},{5,7},{6,4},{7,5},{8,10},{9,11},{10,... | collective-permute-start | bytes 3145736 | tf_op jit(solution)/shard_map/ppermute | solution.py:147
  52.7 109.0 %all-to-all-start.2 = ((bf16[32,8,1536]{2,1,0:T(8,128)(2,1)}), bf16[32,8,1536]{2,1,0:T(8,128)(2,1)S(1)}, u32[]{:S(2)}, u32[]{:S(2)}) async-start(bf16[32,8,1536]{2,1,0:T(8,128)(2,1)} %bitcast.53.refs_10_), calls=%async_computation.2 | async-start | bytes 1572864 | tf_op jit(solution)/shard_map/all_to_all | solution.py:1439
  61.7 31.3 %collective-permute-start.8 = (bf16[128,768]{1,0:T(8,128)(2,1)}, bf16[128,768]{1,0:T(8,128)(2,1)}, u32[]{:S(2)}, u32[]{:S(2)}) collective-permute-start(bf16[128,768]{1,0:T(8,128)(2,1)} %bitcast.41), channel_id=1, source_target_pairs={{0,16},{1,17},{2,18},{3,19},{4,20},{5,21},{6,22},{7,23},{8,24},{9,... | collective-permute-start | bytes 589832 | tf_op jit(solution)/shard_map/ppermute | solution.py:147
  63.0 30.1 %collective-permute-start.7 = (bf16[128,768]{1,0:T(8,128)(2,1)}, bf16[128,768]{1,0:T(8,128)(2,1)S(1)}, u32[]{:S(2)}, u32[]{:S(2)}) collective-permute-start(bf16[128,768]{1,0:T(8,128)(2,1)} %bitcast.41), channel_id=1, source_target_pairs={{0,8},{1,9},{2,10},{3,11},{4,12},{5,13},{6,14},{7,15},{8,0},{9,1},... | collective-permute-start | bytes 589832 | tf_op jit(solution)/shard_map/ppermute | solution.py:147
  94.3 33.3 %collective-permute-start.10 = (bf16[4,128,768]{2,1,0:T(8,128)(2,1)S(1)}, bf16[4,128,768]{2,1,0:T(8,128)(2,1)S(1)}, u32[]{:S(2)}, u32[]{:S(2)}) collective-permute-start(bf16[4,128,768]{2,1,0:T(8,128)(2,1)S(1)} %pad_maximum_fusion.10.refs_7_), channel_id=1, source_target_pairs={{0,4},{1,5},{2,6},{3,7},{4,0},{5,1},{6,2},{7,3},{8,12},{9,13},{10,... | collective-permute-start | bytes 2359304 | tf_op jit(solution)/shard_map/ppermute | solution.py:147
  100.5 27.6 %collective-permute-start.18 = (bf16[2,128,1024]{2,1,0:T(8,128)(2,1)S(1)}, bf16[2,128,1024]{2,1,0:T(8,128)(2,1)S(1)}, u32[]{:S(2)}, u32[]{:S(2)}) collective-permute-start(bf16[2,128,1024]{2,1,0:T(8,128)(2,1)S(1)} %slice.219), channel_id=1, source_target_pairs={{0,2},{1,3},{2,0},{3,1},{4,6},{5,7},{6,4},{7,5},{8,10},{9,11},{10,... | collective-permute-start | bytes 1572872 | tf_op jit(solution)/shard_map/ppermute | solution.py:147
  124.6 47.4 %collective-permute-start.23 = (bf16[4,64,2560]{2,1,0:T(8,128)(2,1)S(1)}, bf16[4,64,2560]{2,1,0:T(8,128)(2,1)}, u32[]{:S(2)}, u32[]{:S(2)}) collective-permute-start(bf16[4,64,2560]{2,1,0:T(8,128)(2,1)S(1)} %pad_maximum_fusion.1.refs_9_.refs_1_), channel_id=1, source_target_pairs={{0,6},{1,7},{2,4},{3,5},{4,2},{5,3},{6,0},{7,1},{8,14},{9,15},{10,... | collective-permute-start | bytes 3932168 | tf_op jit(solution)/shard_map/ppermute | solution.py:147
  126.0 57.5 %collective-permute-start.22 = (bf16[4,64,2560]{2,1,0:T(8,128)(2,1)S(1)}, bf16[4,64,2560]{2,1,0:T(8,128)(2,1)}, u32[]{:S(2)}, u32[]{:S(2)}) collective-permute-start(bf16[4,64,2560]{2,1,0:T(8,128)(2,1)S(1)} %pad_maximum_fusion.1.refs_9_.refs_1_), channel_id=1, source_target_pairs={{0,4},{1,5},{2,6},{3,7},{4,0},{5,1},{6,2},{7,3},{8,12},{9,13},{10,... | collective-permute-start | bytes 3932168 | tf_op jit(solution)/shard_map/ppermute | solution.py:147
  127.6 55.8 %collective-permute-start.21 = (bf16[4,64,2560]{2,1,0:T(8,128)(2,1)S(1)}, bf16[4,64,2560]{2,1,0:T(8,128)(2,1)}, u32[]{:S(2)}, u32[]{:S(2)}) collective-permute-start(bf16[4,64,2560]{2,1,0:T(8,128)(2,1)S(1)} %pad_maximum_fusion.1.refs_9_.refs_1_), channel_id=1, source_target_pairs={{0,2},{1,3},{2,0},{3,1},{4,6},{5,7},{6,4},{7,5},{8,10},{9,11},{10,... | collective-permute-start | bytes 3932168 | tf_op jit(solution)/shard_map/ppermute | solution.py:147
  163.1 34.1 %all-to-all-start.3 = ((bf16[4,512,256]{2,1,0:T(8,128)(2,1)}), bf16[4,512,256]{2,1,0:T(8,128)(2,1)S(1)}, u32[]{:S(2)}, u32[]{:S(2)}) async-start(bf16[4,512,256]{2,1,0:T(8,128)(2,1)} %bitcast.199), calls=%async_computation.3 | async-start | bytes 2097152 | tf_op jit(solution)/shard_map/all_to_all | solution.py:1448
  314.2 79.9 %collective-permute-start.43 = (bf16[128,1024]{1,0:T(8,128)(2,1)}, bf16[128,1024]{1,0:T(8,128)(2,1)}, u32[]{:S(2)}, u32[]{:S(2)}) collective-permute-start(bf16[128,1024]{1,0:T(8,128)(2,1)} %get-tuple-element.369), channel_id=1, source_target_pairs={{0,24},{1,25},{2,26},{3,27},{4,28},{5,29},{6,30},{7,31},{8,16},{9,... | collective-permute-start | bytes 786440 | tf_op jit(solution)/shard_map/ppermute | solution.py:147
  315.8 78.3 %collective-permute-start.42 = (bf16[128,1024]{1,0:T(8,128)(2,1)}, bf16[128,1024]{1,0:T(8,128)(2,1)}, u32[]{:S(2)}, u32[]{:S(2)}) collective-permute-start(bf16[128,1024]{1,0:T(8,128)(2,1)} %get-tuple-element.370), channel_id=1, source_target_pairs={{0,16},{1,17},{2,18},{3,19},{4,20},{5,21},{6,22},{7,23},{8,24},{9,... | collective-permute-start | bytes 786440 | tf_op jit(solution)/shard_map/ppermute | solution.py:147
  337.7 58.1 %all-to-all-start.5 = ((bf16[32,8,1536]{2,1,0:T(8,128)(2,1)}), bf16[32,8,1536]{2,1,0:T(8,128)(2,1)S(1)}, u32[]{:S(2)}, u32[]{:S(2)}) async-start(bf16[32,8,1536]{2,1,0:T(8,128)(2,1)} %broadcast_in_dim.200), calls=%async_computation.5 | async-start | bytes 1572864 | tf_op jit(solution)/shard_map/all_to_all | solution.py:322
  342.4 47.6 %collective-permute-start.39 = (bf16[4,64,512]{2,1,0:T(8,128)(2,1)}, bf16[4,64,512]{2,1,0:T(8,128)(2,1)S(1)}, u32[]{:S(2)}, u32[]{:S(2)}) collective-permute-start(bf16[4,64,512]{2,1,0:T(8,128)(2,1)} %get-tuple-element.165), channel_id=1, source_target_pairs={{0,6},{1,7},{2,4},{3,5},{4,2},{5,3},{6,0},{7,1},{8,14},{9,15},{10,... | collective-permute-start | bytes 786440 | tf_op jit(solution)/shard_map/ppermute | solution.py:147
  345.2 42.7 %collective-permute-start.38 = (bf16[4,64,2560]{2,1,0:T(8,128)(2,1)S(1)}, bf16[4,64,2560]{2,1,0:T(8,128)(2,1)S(1)}, u32[]{:S(2)}, u32[]{:S(2)}) collective-permute-start(bf16[4,64,2560]{2,1,0:T(8,128)(2,1)S(1)} %pad_maximum_fusion.3), channel_id=1, source_target_pairs={{0,4},{1,5},{2,6},{3,7},{4,0},{5,1},{6,2},{7,3},{8,12},{9,13},{10,... | collective-permute-start | bytes 3932168 | tf_op jit(solution)/shard_map/ppermute | solution.py:147
  345.8 44.2 %collective-permute-start.37 = (bf16[4,64,2560]{2,1,0:T(8,128)(2,1)S(1)}, bf16[4,64,2560]{2,1,0:T(8,128)(2,1)S(1)}, u32[]{:S(2)}, u32[]{:S(2)}) collective-permute-start(bf16[4,64,2560]{2,1,0:T(8,128)(2,1)S(1)} %copy-done.13), channel_id=1, source_target_pairs={{0,2},{1,3},{2,0},{3,1},{4,6},{5,7},{6,4},{7,5},{8,10},{9,11},{10,... | collective-permute-start | bytes 3932168 | tf_op jit(solution)/shard_map/ppermute | solution.py:147
  404.5 42.6 %all-to-all-start.6 = ((bf16[32,32,768]{2,1,0:T(8,128)(2,1)}), bf16[32,32,768]{2,1,0:T(8,128)(2,1)S(1)}, u32[]{:S(2)}, u32[]{:S(2)}) async-start(bf16[32,32,768]{2,1,0:T(8,128)(2,1)} %bitcast.209), calls=%async_computation.6 | async-start | bytes 3145728 | tf_op jit(solution)/shard_map/all_to_all | solution.py:1514
  452.1 35.5 %collective-permute-start.46 = (bf16[64,2560]{1,0:T(8,128)(2,1)}, bf16[64,2560]{1,0:T(8,128)(2,1)}, u32[]{:S(2)}, u32[]{:S(2)}) collective-permute-start(bf16[64,2560]{1,0:T(8,128)(2,1)} %get-tuple-element.180), channel_id=1, source_target_pairs={{0,8},{1,9},{2,10},{3,11},{4,12},{5,13},{6,14},{7,15},{8,0},{9,1},... | collective-permute-start | bytes 983048 | tf_op jit(solution)/shard_map/ppermute | solution.py:147
  454.0 33.6 %collective-permute-start.47 = (bf16[64,2560]{1,0:T(8,128)(2,1)}, bf16[64,2560]{1,0:T(8,128)(2,1)}, u32[]{:S(2)}, u32[]{:S(2)}) collective-permute-start(bf16[64,2560]{1,0:T(8,128)(2,1)} %get-tuple-element.182), channel_id=1, source_target_pairs={{0,16},{1,17},{2,18},{3,19},{4,20},{5,21},{6,22},{7,23},{8,24},{9,... | collective-permute-start | bytes 983048 | tf_op jit(solution)/shard_map/ppermute | solution.py:147
  456.4 29.7 %collective-permute-start.48 = (bf16[64,2560]{1,0:T(8,128)(2,1)}, bf16[64,2560]{1,0:T(8,128)(2,1)}, u32[]{:S(2)}, u32[]{:S(2)}) collective-permute-start(bf16[64,2560]{1,0:T(8,128)(2,1)} %get-tuple-element.184), channel_id=1, source_target_pairs={{0,24},{1,25},{2,26},{3,27},{4,28},{5,29},{6,30},{7,31},{8,16},{9,... | collective-permute-start | bytes 983048 | tf_op jit(solution)/shard_map/ppermute | solution.py:147
  (99 other events, 1152.1 us)
